TPU v7x, 128 devices: a whole 4x4x4 slice. The times are simulated.
128 devices in a mesh: ty: 8 (over z, core), tx: 16 (over y, x).
Axes of the slice: x: 4, y: 4, z: 4, core: 2. Of those that a mesh axis runs over, the one named last changes fastest.
Arguments:
- atmos: float32 [3, 16, 512, 2048], P(None, None, 'ty', 'tx'), may hold values from -3 to 3
- slot_tile: int32 [3072], replicated, may hold values from -1 to 8191, as said below
- fuel_cat: int32 [3072, 3200], P(('ty', 'tx')), may hold values from 0 to 12
- front_burn: int32 [3072, 3200], P(('ty', 'tx')), may hold values 0 or 1
- front_depth: float32 [3072, 3200], P(('ty', 'tx')), may hold values from 0.2 to 2
- fuel_rate: float32 [13], replicated, may hold values from 0.1 to 0.6
- fuel_heat: float32 [13], replicated, may hold values from 0.5 to 5
Outputs:
- atmos_out: float32 [3, 16, 512, 2048], P(None, None, 'ty', 'tx')
- fire_level: float32 [3072, 3200], P(('ty', 'tx'))
Inputs may be any that keep to these rules, and one draw needn't show every extreme that they name: `slot_tile`: entries are -1 for an empty slot or distinct fire tile numbers; each device's live slots come first; the cells of exactly 8 live tiles lie on every device; the live tiles whose cells lie on one device fill at most 2 slots of any one device, and some pair of devices reaches it; some device has all 24 slots live; the last tile of the window is always listed.
All inputs are finite; a program needn't handle non-finite values. No bound on the sum of `front_burn` on one device may be relied on, other than what follows from the above.
Results may differ from a plain program's by a relative error of at most 0.0001.
Values sent between devices are 32-bit elements; how exact they have to be, the bound alone decides.
No kernel may reach another device: no remote copies, remote signals or barrier semaphores. Data moves between devices by JAX's collectives and lax.ppermute only.
A program may use at most 128 MiB of HBM per device.

v0:
```python
import jax
import jax.numpy as jnp
from jax import lax
from jax.sharding import PartitionSpec as P

FTY = 8
FTX = 16
REF = 5
STEPS = 2


TIME_STEP = 0.2
LATERAL_MIXING = 0.25
VERTICAL_MIXING = 0.5
CORIOLIS = 0.3
BUOYANCY = 0.5
HEAT_GAIN = 1.0
FIRE_STEP = 1.0
WIND_GAIN = 1.0
FRONT_WIDTH = 0.5


def with_halo(x, sides, width):
    for axis, dim in sides:
        size, length = (lax.axis_size(axis), x.shape[dim])
        up = [(i, (i + 1) % size) for i in range(size - 1)]
        down = [(j, i) for i, j in up]
        last = lax.slice_in_dim(x, length - width, length, axis=dim)
        first = lax.slice_in_dim(x, 0, width, axis=dim)
        before = lax.ppermute(last, axis, up)
        after = lax.ppermute(first, axis, down)
        x = jnp.concatenate([before, x, after], axis=dim)
    return x


def tendency(padded):
    centre = padded[:, :, 1:-1, 1:-1]
    eastern = padded[:, :, 1:-1, 2:]
    western = padded[:, :, 1:-1, :-2]
    northern = padded[:, :, 2:, 1:-1]
    southern = padded[:, :, :-2, 1:-1]
    zonal_wind = centre[0:1]
    north_wind = centre[1:2]
    advect = (
        jnp.maximum(zonal_wind, 0.0) * (centre - western)
        + jnp.minimum(zonal_wind, 0.0) * (eastern - centre)
        + jnp.maximum(north_wind, 0.0) * (centre - southern)
        + jnp.minimum(north_wind, 0.0) * (northern - centre)
    )
    lateral = eastern + western + northern + southern - 4.0 * centre
    above_level = jnp.concatenate([centre[:, 1:], centre[:, -1:]], axis=1)
    below_level = jnp.concatenate([centre[:, :1], centre[:, :-1]], axis=1)
    vertical = above_level + below_level - 2.0 * centre
    change = -advect + LATERAL_MIXING * lateral + VERTICAL_MIXING * vertical
    slope_east = 0.5 * (eastern[2] - western[2])
    slope_north = 0.5 * (northern[2] - southern[2])
    zonal_change = change[0] + CORIOLIS * centre[1] - BUOYANCY * slope_east
    north_change = change[1] - CORIOLIS * centre[0] - BUOYANCY * slope_north
    return jnp.stack([zonal_change, north_change, change[2]])


def advance(air_state, extend):
    first_rate = tendency(extend(air_state))
    middle = air_state + TIME_STEP * first_rate
    second = tendency(extend(middle))
    return air_state + 0.5 * TIME_STEP * (first_rate + second)


def fire_advance(front_level, tile_wind, rate_cell, heat_cell):
    tile_count = front_level.shape[0]
    fire_rows = FTY * REF
    fire_cols = FTX * REF
    tile_cells = FTY * FTX
    level_grid = front_level.reshape(tile_count, fire_rows, fire_cols)

    def spread_out(coarse):
        coarse = coarse.reshape(tile_count, FTY, 1, FTX, 1)
        return jnp.broadcast_to(coarse, (tile_count, FTY, REF, FTX, REF)).reshape(
            tile_count, fire_rows, fire_cols
        )

    zonal_fire = spread_out(tile_wind[:, :tile_cells])
    north_fire = spread_out(tile_wind[:, tile_cells:])
    edged_grid = jnp.pad(level_grid, ((0, 0), (1, 1), (1, 1)), mode="edge")
    slope_east = 0.5 * (edged_grid[:, 1:-1, 2:] - edged_grid[:, 1:-1, :-2])
    slope_north = 0.5 * (edged_grid[:, 2:, 1:-1] - edged_grid[:, :-2, 1:-1])
    stretch = jnp.sqrt(1.0 + slope_east * slope_east + slope_north * slope_north)
    along_wind = (zonal_fire * slope_east + north_fire * slope_north) / stretch
    rate_full = rate_cell.reshape(tile_count, fire_rows, fire_cols)
    heat_full = heat_cell.reshape(tile_count, fire_rows, fire_cols)
    spread_speed = rate_full * (1.0 + WIND_GAIN * jax.nn.softplus(along_wind))
    advanced = level_grid - FIRE_STEP * spread_speed * stretch
    released = heat_full * (
        jax.nn.sigmoid(-advanced / FRONT_WIDTH) - jax.nn.sigmoid(-level_grid / FRONT_WIDTH)
    )
    per_cell = released.reshape(tile_count, FTY, REF, FTX, REF).mean(axis=(2, 4))
    return (
        advanced.reshape(tile_count, fire_rows * fire_cols),
        per_cell.reshape(tile_count, tile_cells),
    )


def tile_blocks(air_state):
    surface = air_state[0:2, 0]
    tile_rows = surface.shape[1] // FTY
    tile_cols = surface.shape[2] // FTX
    blocks = surface.reshape(2, tile_rows, FTY, tile_cols, FTX).transpose(1, 3, 0, 2, 4)
    return blocks.reshape(tile_rows * tile_cols, 2 * FTY * FTX)


def heat_field(blocks, tile_rows, tile_cols):
    return (
        blocks.reshape(tile_rows, tile_cols, FTY, FTX)
        .transpose(0, 2, 1, 3)
        .reshape(tile_rows * FTY, tile_cols * FTX)
    )


def extend(air_state):
    return with_halo(air_state, (("ty", 2), ("tx", 3)), 1)


def pick_index(selected):
    positions = lax.broadcasted_iota(jnp.int32, selected.shape, selected.ndim - 1)
    return (jnp.sum(jnp.where(selected, positions, 0), axis=-1), jnp.any(selected, axis=-1))


def take_rows(source_table, row_index, present):
    picked = jnp.take(source_table, row_index, axis=0)
    return jnp.where(present[:, None], picked, 0.0)


def on_device(atmos, slot_tile, fuel_cat, front_burn, front_depth, fuel_rate, fuel_heat):
    across_cols = lax.axis_size("tx")
    myself = lax.axis_index("ty") * across_cols + lax.axis_index("tx")
    tiles_down = atmos.shape[2] // FTY
    tiles_across = atmos.shape[3] // FTX
    total_across = across_cols * tiles_across
    slot_count = fuel_cat.shape[0]
    is_live = slot_tile >= 0
    tile_ids = jnp.where(is_live, slot_tile, 0)
    tile_row = tile_ids // total_across
    tile_col = tile_ids % total_across
    owner_rank = tile_row // tiles_down * across_cols + tile_col // tiles_across
    local_tile = tile_row % tiles_down * tiles_across + tile_col % tiles_across
    is_mine = is_live & (owner_rank == myself)
    my_live = lax.dynamic_slice_in_dim(is_live, myself * slot_count, slot_count)
    fuel_kinds = jnp.arange(fuel_rate.shape[0], dtype=jnp.int32)
    matches = fuel_cat[None] == fuel_kinds[:, None, None]
    rate_cell = jnp.sum(jnp.where(matches, fuel_rate[:, None, None], 0.0), axis=0)
    heat_cell = jnp.sum(jnp.where(matches, fuel_heat[:, None, None], 0.0), axis=0)
    start_level = jnp.where(front_burn == 1, -front_depth, front_depth)
    tile_list = jnp.arange(tiles_down * tiles_across, dtype=jnp.int32)
    source_slot, has_source = pick_index(
        is_mine[None, :] & (local_tile[None, :] == tile_list[:, None])
    )
    air_state = atmos
    front_level = start_level
    for section_index in range(STEPS):
        blocks = tile_blocks(air_state)
        send_rows = jnp.where(is_mine[:, None], jnp.take(blocks, local_tile, axis=0), 0.0)
        tile_wind = lax.psum_scatter(send_rows, ("ty", "tx"), scatter_dimension=0, tiled=True)
        advanced, released = fire_advance(front_level, tile_wind, rate_cell, heat_cell)
        front_level = jnp.where(my_live[:, None], advanced, front_level)
        released = jnp.where(my_live[:, None], released, 0.0)
        air_state = advance(air_state, extend)
        gathered = lax.all_gather(released, ("ty", "tx"), axis=0, tiled=True)
        heat_blocks = take_rows(gathered, source_slot, has_source)
        air_state = air_state.at[2, 0].add(
            HEAT_GAIN * heat_field(heat_blocks, tiles_down, tiles_across)
        )
    return (air_state, front_level)


def solution(mesh):
    in_specs = (
        P(None, None, "ty", "tx"),
        P(),
        P(("ty", "tx"), None),
        P(("ty", "tx"), None),
        P(("ty", "tx"), None),
        P(),
        P(),
    )
    out_specs = (P(None, None, "ty", "tx"), P(("ty", "tx"), None))
    return jax.shard_map(
        on_device, mesh=mesh, in_specs=in_specs, out_specs=out_specs, check_vma=False
    )
```

profile of v0, /device:TPU:1, one launch (start us, length us, event | category | flops | bytes accessed | tf_op | source)
XLA Modules:
  0.0 660.2 jit_solution(2662314875149158334)
XLA Ops:
  9.9 9.8 %gather_fusion = f32[3072,256]{1,0:T(8,128)S(1)} fusion(f32[64,256]{1,0:T(8,128)S(1)} %reshape.170, s32[3072]{0:T(1024)S(1)} %fusion.74), kind=kCustom, calls=%fused_computation.clone | custom fusion | bytes 6303744 | tf_op jit(solution)/shard_map/jit(_take)/gather | solution.py:161
  19.8 3.4 select_select_fusion.1
  25.3 3.3 collective-permute-start.1
  28.6 3.5 collective-permute-start
  47.7 3.1 collective-permute-start.2
  50.8 2.7 copy.179
  64.9 2.7 copy.180
  67.7 5.3 fusion.9
  83.3 151.2 %reduce-scatter.3.cloned.1.call-done = f32[24,256]{1,0:T(8,128)} async-done(((f32[3072,256]{1,0:T(8,128)}), f32[24,256]{1,0:T(8,128)}) %reduce-scatter.3.cloned.1.call-update) | async-done | bytes 24592 | tf_op jit(solution)/shard_map/reduce_scatter | solution.py:162
  238.4 2.7 reshape.171
  241.1 2.7 copy.192
  246.4 2.7 reshape.172
  249.2 2.7 copy.194
  251.9 4.5 subtract_multiply_fusion.1
  256.4 2.7 copy.195
  259.1 2.7 reshape.173
  273.7 2.8 collective-permute-start.6
  286.8 5.2 fusion.12
  296.6 33.6 %all-gather.3.cloned.1.call-done = f32[3072,128]{1,0:T(8,128)} async-done(((f32[24,128]{1,0:T(8,128)}), f32[3072,128]{1,0:T(8,128)}) %all-gather.3.cloned.1.call-update) | async-done | bytes 1572880 | tf_op jit(solution)/shard_map/all_gather | solution.py:167
  335.2 12.3 %gather_fusion.2 = f32[3072,256]{1,0:T(8,128)} fusion(f32[64,256]{1,0:T(8,128)S(1)} %reshape.178, s32[3072]{0:T(1024)S(1)} %copy-done.43), kind=kCustom, calls=%fused_computation.2.clone | custom fusion | bytes 6303744 | tf_op jit(solution)/shard_map/jit(_take)/gather | solution.py:161
  347.5 5.2 select_select_fusion
  365.7 2.7 copy.198
  380.0 4.9 fusion.17
  386.9 4.5 collective-permute-start.12
  395.4 162.4 %reduce-scatter.5.cloned.1.call-done = f32[24,256]{1,0:T(8,128)} async-done(((f32[3072,256]{1,0:T(8,128)}), f32[24,256]{1,0:T(8,128)}) %reduce-scatter.5.cloned.1.call-update) | async-done | bytes 24592 | tf_op jit(solution)/shard_map/reduce_scatter | solution.py:162
  560.3 2.7 reshape.179
  567.6 2.7 reshape.180
  573.1 4.2 subtract_multiply_fusion
  577.3 2.7 copy.216
  580.0 2.7 reshape.181
  602.6 5.2 fusion.20
  611.8 37.9 %all-gather.5.cloned.1.call-done = f32[3072,128]{1,0:T(8,128)} async-done(((f32[24,128]{1,0:T(8,128)}), f32[3072,128]{1,0:T(8,128)}) %all-gather.5.cloned.1.call-update) | async-done | bytes 1572880 | tf_op jit(solution)/shard_map/all_gather | solution.py:167
  (260 shorter events, 147.7 us)
Async XLA Ops:
  7.2 227.3 %reduce-scatter.3.cloned.1.call-start = ((), (), s32[]{:S(2)}) async-start(), calls=%async_computation.2 | async-start | bytes 3170304 | tf_op jit(solution)/shard_map/reduce_scatter | solution.py:162
  8.5 11.2 %copy-start.44 = (pred[3072]{0:T(1024)(128)(4,1)}, pred[3072]{0:T(1024)(128)(4,1)S(1)}, u32[]{:S(2)}) copy-start(pred[3072]{0:T(1024)(128)(4,1)S(1)} %get-tuple-element.36) | copy-start | bytes 9220
  8.5 24.1 %copy-start.34 = (s32[3072]{0:T(1024)}, s32[3072]{0:T(1024)S(1)}, u32[]{:S(2)}) copy-start(s32[3072]{0:T(1024)S(1)} %get-tuple-element.37) | copy-start | bytes 36868
  8.6 11.2 %copy-start.42 = (s32[3072]{0:T(1024)}, s32[3072]{0:T(1024)S(1)}, u32[]{:S(2)}) copy-start(s32[3072]{0:T(1024)S(1)} %fusion.74) | copy-start | bytes 36868
  23.2 8.9 %copy-start.25 = (f32[24,3200]{1,0:T(8,128)S(1)}, f32[24,3200]{1,0:T(8,128)}, u32[]{:S(2)}) copy-start(f32[24,3200]{1,0:T(8,128)} %param.19) | copy-start | bytes 921604
  23.2 8.9 %copy-start.26 = (s32[24,3200]{1,0:T(8,128)S(1)}, s32[24,3200]{1,0:T(8,128)}, u32[]{:S(2)}) copy-start(s32[24,3200]{1,0:T(8,128)} %param.18) | copy-start | bytes 921604
  23.3 307.0 %all-gather.3.cloned.1.call-start = ((), (), s32[]{:S(2)}) async-start(), calls=%async_computation.3 | async-start | bytes 1585152 | tf_op jit(solution)/shard_map/all_gather | solution.py:167
  25.3 17.7 %collective-permute-start.1 = (f32[3,16,1,128]{3,2,1,0:T(1,128)}, f32[3,16,1,128]{3,2,1,0:T(1,128)S(1)}, u32[]{:S(2)}, u32[]{:S(2)}) collective-permute-start(f32[3,16,1,128]{3,2,1,0:T(1,128)} %get-tuple-element.93), channel_id=1, source_target_pairs={{16,0},{32,16},{48,32},{64,48},{80,64},{96,80},{112,96},{17,1},{33... | collective-permute-start | bytes 73736 | tf_op jit(solution)/shard_map/ppermute | solution.py:31
  28.6 14.4 %collective-permute-start = (f32[3,16,1,128]{3,2,1,0:T(1,128)}, f32[3,16,1,128]{3,2,1,0:T(1,128)S(1)}, u32[]{:S(2)}, u32[]{:S(2)}) collective-permute-start(f32[3,16,1,128]{3,2,1,0:T(1,128)} %get-tuple-element.92), channel_id=1, source_target_pairs={{0,16},{16,32},{32,48},{48,64},{64,80},{80,96},{96,112},{1,17},{17... | collective-permute-start | bytes 73736 | tf_op jit(solution)/shard_map/ppermute | solution.py:30
  47.7 15.4 %collective-permute-start.2 = (f32[3,16,66,1]{2,1,3,0:T(8,128)S(1)}, f32[3,16,66,1]{2,1,3,0:T(8,128)S(1)}, u32[]{:S(2)}, u32[]{:S(2)}) collective-permute-start(f32[3,16,66,1]{2,1,3,0:T(8,128)S(1)} %copy.177), channel_id=1, source_target_pairs={{0,1},{1,2},{2,3},{3,4},{4,5},{5,6},{6,7},{7,8},{8,9},{9,10},{10,1... | collective-permute-start | bytes 38024 | tf_op jit(solution)/shard_map/ppermute | solution.py:30
  53.5 11.4 %collective-permute-start.3 = (f32[3,16,66,1]{2,1,3,0:T(8,128)}, f32[3,16,66,1]{2,1,3,0:T(8,128)}, u32[]{:S(2)}, u32[]{:S(2)}) collective-permute-start(f32[3,16,66,1]{2,1,3,0:T(8,128)} %copy.179), channel_id=1, source_target_pairs={{1,0},{2,1},{3,2},{4,3},{5,4},{6,5},{7,6},{8,7},{9,8},{10,9},{11,1... | collective-permute-start | bytes 38024 | tf_op jit(solution)/shard_map/ppermute | solution.py:31
  67.7 5.3 copy-start.2
  76.6 191.1 %collective-permute-start.4 = (f32[3,16,1,128]{3,2,1,0:T(1,128)}, f32[3,16,1,128]{3,2,1,0:T(1,128)S(1)}, u32[]{:S(2)}, u32[]{:S(2)}) collective-permute-start(f32[3,16,1,128]{3,2,1,0:T(1,128)} %get-tuple-element.81), channel_id=1, source_target_pairs={{0,16},{16,32},{32,48},{48,64},{64,80},{80,96},{96,112},{1,17},{17... | collective-permute-start | bytes 73736 | tf_op jit(solution)/shard_map/ppermute | solution.py:30
  79.3 188.4 %collective-permute-start.5 = (f32[3,16,1,128]{3,2,1,0:T(1,128)}, f32[3,16,1,128]{3,2,1,0:T(1,128)}, u32[]{:S(2)}, u32[]{:S(2)}) collective-permute-start(f32[3,16,1,128]{3,2,1,0:T(1,128)} %get-tuple-element.82), channel_id=1, source_target_pairs={{16,0},{32,16},{48,32},{64,48},{80,64},{96,80},{112,96},{17,1},{33... | collective-permute-start | bytes 73736 | tf_op jit(solution)/shard_map/ppermute | solution.py:31
  266.2 291.5 %reduce-scatter.5.cloned.1.call-start = ((), (), s32[]{:S(2)}) async-start(), calls=%async_computation.4 | async-start | bytes 3170304 | tf_op jit(solution)/shard_map/reduce_scatter | solution.py:162
  273.7 7.4 %collective-permute-start.6 = (f32[3,16,66,1]{2,1,3,0:T(8,128)}, f32[3,16,66,1]{2,1,3,0:T(8,128)}, u32[]{:S(2)}, u32[]{:S(2)}) collective-permute-start(f32[3,16,66,1]{2,1,3,0:T(8,128)} %copy.181), channel_id=1, source_target_pairs={{0,1},{1,2},{2,3},{3,4},{4,5},{5,6},{6,7},{7,8},{8,9},{9,10},{10,1... | collective-permute-start | bytes 38024 | tf_op jit(solution)/shard_map/ppermute | solution.py:30
  279.2 5.0 collective-permute-start.7
  295.4 36.9 %copy-start.49 = (pred[64]{0:T(512)(128)(4,1)S(1)}, pred[64]{0:T(512)(128)(4,1)}, u32[]{:S(2)}) copy-start(pred[64]{0:T(512)(128)(4,1)} %fusion.24) | copy-start | bytes 196
  295.4 36.9 %copy-start.51 = (pred[64]{0:T(512)(128)(4,1)S(1)}, pred[64]{0:T(512)(128)(4,1)}, u32[]{:S(2)}) copy-start(pred[64]{0:T(512)(128)(4,1)} %compare_and_fusion.1) | copy-start | bytes 196
  296.5 56.3 %copy-start.20 = (f32[24,40,80]{2,1,0:T(8,128)}, f32[24,40,80]{2,1,0:T(8,128)S(1)}, u32[]{:S(2)}) copy-start(f32[24,40,80]{2,1,0:T(8,128)S(1)} %reshape.177) | copy-start | bytes 921604
  335.2 12.3 %copy-start.45 = (pred[3072]{0:T(1024)(128)(4,1)S(1)}, pred[3072]{0:T(1024)(128)(4,1)}, u32[]{:S(2)}) copy-start(pred[3072]{0:T(1024)(128)(4,1)} %copy-done.44) | copy-start | bytes 9220
  352.7 297.0 %all-gather.5.cloned.1.call-start = ((), (), s32[]{:S(2)}) async-start(), calls=%async_computation.5 | async-start | bytes 1585152 | tf_op jit(solution)/shard_map/all_gather | solution.py:167
  354.5 8.0 %collective-permute-start.8 = (f32[3,16,1,128]{3,2,1,0:T(1,128)S(1)}, f32[3,16,1,128]{3,2,1,0:T(1,128)S(1)}, u32[]{:S(2)}, u32[]{:S(2)}) collective-permute-start(f32[3,16,1,128]{3,2,1,0:T(1,128)S(1)} %get-tuple-element.70), channel_id=1, source_target_pairs={{0,16},{16,32},{32,48},{48,64},{64,80},{80,96},{96,112},{1,17},{17... | collective-permute-start | bytes 73736 | tf_op jit(solution)/shard_map/ppermute | solution.py:30
  356.5 6.0 collective-permute-start.9
  368.4 5.0 collective-permute-start.10
  372.1 5.3 collective-permute-start.11
  386.9 200.1 %collective-permute-start.12 = (f32[3,16,1,128]{3,2,1,0:T(1,128)S(1)}, f32[3,16,1,128]{3,2,1,0:T(1,128)S(1)}, u32[]{:S(2)}, u32[]{:S(2)}) collective-permute-start(f32[3,16,1,128]{3,2,1,0:T(1,128)S(1)} %get-tuple-element.59), channel_id=1, source_target_pairs={{0,16},{16,32},{32,48},{48,64},{64,80},{80,96},{96,112},{1,17},{17... | collective-permute-start | bytes 73736 | tf_op jit(solution)/shard_map/ppermute | solution.py:30
  391.5 195.6 %collective-permute-start.13 = (f32[3,16,1,128]{3,2,1,0:T(1,128)S(1)}, f32[3,16,1,128]{3,2,1,0:T(1,128)S(1)}, u32[]{:S(2)}, u32[]{:S(2)}) collective-permute-start(f32[3,16,1,128]{3,2,1,0:T(1,128)S(1)} %get-tuple-element.60), channel_id=1, source_target_pairs={{16,0},{32,16},{48,32},{64,48},{80,64},{96,80},{112,96},{17,1},{33... | collective-permute-start | bytes 73736 | tf_op jit(solution)/shard_map/ppermute | solution.py:31
  591.7 6.0 collective-permute-start.14
  596.1 4.6 collective-permute-start.15
  610.8 41.0 %copy-start.50 = (pred[64]{0:T(512)(128)(4,1)S(1)}, pred[64]{0:T(512)(128)(4,1)}, u32[]{:S(2)}) copy-start(pred[64]{0:T(512)(128)(4,1)} %fusion.24) | copy-start | bytes 196
  610.8 41.0 %copy-start.52 = (pred[64]{0:T(512)(128)(4,1)S(1)}, pred[64]{0:T(512)(128)(4,1)}, u32[]{:S(2)}) copy-start(pred[64]{0:T(512)(128)(4,1)} %compare_and_fusion.1) | copy-start | bytes 196
  (43 other events, 100.9 us)
Sparse Core Ops, SparseCore 0:
  23.4 211.0 reduce-scatter.2
  266.3 63.8 all-gather.2
  352.8 204.8 reduce-scatter.4
  585.8 63.8 all-gather.4
where the time goes:
time: 663 us; the launch traced here: 660 us
  waiting for transfers between devices  389 us (59%)
  local copies, waits for them, and re-layouts  147 us (22%)
  other arithmetic  70.5 us (11%)
  starting transfers between devices  38.8 us (6%)
  between operations  14.7 us (2%)
    reduce_scatter x2, waiting for transfers between devices, on_device(): lax.psum_scatter(send_rows, ('ty', 'tx'), scatter_dimension=0, tiled=True)  314 us
    all_gather x2, waiting for transfers between devices, on_device(): gathered = lax.all_gather(released, ('ty', 'tx'), axis=0, tiled=True)  71.5 us
    ppermute x8, starting transfers between devices, with_halo(): before = lax.ppermute(last, axis, up)  23.3 us
    gather x2, local copies, waits for them, and re-layouts, on_device(): jnp.take(blocks, local_tile, axis=0)  22.1 us
    reshape x8, local copies, waits for them, and re-layouts, spread_out(): jnp.broadcast_to(coarse, (tile_count, FTY, REF, FTX, REF))  21.8 us
    add x4, other arithmetic, tendency(): change = -advect + LATERAL_MIXING * lateral + VERTICAL_MIXING * vertical  20.6 us
    slice x12, local copies, waits for them, and re-layouts, with_halo(): last = lax.slice_in_dim(x, length - width, length, axis=dim)  19.7 us
    ppermute x8, starting transfers between devices, with_halo(): after = lax.ppermute(first, axis, down)  15.3 us
  transfers between devices with their start and end apart: 20, of which 7 were waited for; matrix products, arithmetic and copies ran while one was open for 26% of the time, Pallas kernels for 0%

commit v1 on v0

v1 whole, which is shorter than its diff:
```python
import jax
import jax.numpy as jnp
import numpy as np
from jax import lax
from jax.experimental import pallas as pl
from jax.experimental.pallas import tpu as pltpu
from jax.sharding import PartitionSpec as P

AXES = ("ty", "tx")
NTY, NTX, DEVICES = 8, 16, 128
LEV, AY, AX = 16, 64, 128
SLOTS, FC = 24, 3200
ROWS = 88
TOP = 12
F32, BF16 = jnp.float32, jnp.bfloat16


def roll(x, shift, axis):
    size = x.shape[axis]
    return pltpu.roll(x, shift % size, axis) if shift % size else x


def iota(shape, dim):
    return lax.broadcasted_iota(jnp.int32, shape, dim)


def parts(x):
    high = x.astype(BF16)
    rest = x - high.astype(F32)
    middle = rest.astype(BF16)
    low = (rest - middle.astype(F32)).astype(BF16)
    return high, middle, low


def dot(a, b):
    return jnp.dot(a, b, preferred_element_type=F32)


def pick(onehot, x):
    a = onehot.astype(BF16)
    high, middle, low = parts(x)
    return dot(a, high) + dot(a, middle) + dot(a, low)


def swap_blocks(x):
    x = x.reshape(x.shape[0] // 8, 8, 128)
    sub, group = iota(x.shape, 1), iota(x.shape, 2) // 16
    for step in (1, 2, 4):
        sub_bit, group_bit = (sub & step) != 0, (group & step) != 0
        below = roll(roll(x, -step, 1), 16 * step, 2)
        above = roll(roll(x, step, 1), -16 * step, 2)
        x = jnp.where(sub_bit == group_bit, x, jnp.where(group_bit, below, above))
    return x.reshape(x.shape[0] * 8, 128)


def slot_facts(tile):
    row, col = tile >> 7, tile & 127
    owner = (row >> 3) * NTX + (col >> 3)
    local = (row & 7) * 8 + (col & 7)
    live = tile >= 0
    return jnp.where(live, owner, -1), local + 1, live


def earlier(member):
    lower = (iota((32, 32), 0) > iota((32, 32), 1)).astype(F32).astype(BF16)
    return dot(lower, member.astype(BF16))


def slots_of(owner, local, home):
    member = (owner == home).astype(F32)
    before = earlier(member)
    numbers = member * local.astype(F32)
    return [
        jnp.sum(jnp.where(before == float(j), numbers, 0.0), axis=0, keepdims=True)
        for j in (0, 1)
    ]


def pack_columns(atmos, east, west):
    lane = iota((AY, 128), 1)
    group, spot = lane // 16, lane % 16
    for half in range(2):
        to_east = jnp.zeros((AY, 128), F32)
        to_west = jnp.zeros((AY, 128), F32)
        for c in range(3):
            both = jnp.zeros((AY, 128), F32)
            for k in range(8):
                moved = roll(atmos[c, half * 8 + k], 16 * k + 4, 1)
                both = jnp.where(group == k, moved, both)
            inside = (spot >= 4 * c) & (spot < 4 * c + 4)
            to_east = jnp.where(inside, roll(both, 4 * c, 1), to_east)
            to_west = jnp.where(inside, roll(both, 4 * c - 4, 1), to_west)
        east[half] = to_east
        west[half] = to_west


def pack_rows(low_rows, high_rows, from_west, from_east, east, west, up, down):
    def put(piece, high, low):
        where = pl.ds(4 * (piece % 2), 4)
        up[piece // 2, where, :] = high
        down[piece // 2, where, :] = low

    for c in range(3):
        for level in range(LEV):
            put(c * LEV + level, high_rows[c, level, 4:8, :], low_rows[c, level, 0:4, :])
    for i, source in enumerate((from_west, from_east, east, west)):
        for half in range(2):
            put(48 + 2 * i + half, source[half, 60:64, :], source[half, 0:4, :])


def rim_of(c, from_west, from_east, east, west):
    spot = iota(east.shape, 1) % 16
    out = jnp.where(spot < 3, roll(east, -(4 * c + 1), 1), 0.0)
    out = jnp.where((spot >= 3) & (spot < 7), roll(from_east, 3 - 4 * c, 1), out)
    out = jnp.where((spot >= 8) & (spot < 12), roll(from_west, 8 - 4 * c, 1), out)
    return jnp.where((spot >= 12) & (spot < 15), roll(west, 12 - 4 * c, 1), out)


def inside_window(first, rows, flags):
    y = iota((rows, 128), 0) + (first - TOP)
    return ((y >= 0) | (flags[1] > 0)) & ((y < AY) | (flags[1] < NTY - 1))


def rim_inside(first, rows, flags):
    spot = iota((rows, 128), 1) % 16
    east_out = (spot >= 3) & (spot < 7) & (flags[2] == NTX - 1)
    west_out = (spot >= 8) & (spot < 12) & (flags[2] == 0)
    return inside_window(first, rows, flags) & ~(east_out | west_out)


def fill_rim(rim, halves, flags, messages, low, high):
    from_west, from_east, east, west = messages
    for c in range(3):
        for half in range(halves):
            body = rim_of(c, *(m[half] for m in messages))
            rim[c, half, TOP : TOP + AY, :] = jnp.where(rim_inside(TOP, AY, flags), body, 0.0)
            for source, first in ((low, 8), (high, 76)):
                pieces = []
                for i in range(4):
                    piece = 48 + 2 * i + half
                    pieces.append(source[piece // 2, 4 * (piece % 2) : 4 * (piece % 2) + 4, :])
                rows = rim_of(c, *pieces)
                rim[c, half, first : first + 4, :] = jnp.where(rim_inside(first, 4, flags), rows, 0.0)


def fill_main(main, atmos, levels, flags, low, high):
    for c in range(3):
        for level in range(levels):
            piece = c * LEV + level
            where = slice(4 * (piece % 2), 4 * (piece % 2) + 4)
            main[c, level, TOP : TOP + AY, :] = atmos[c, level]
            main[c, level, 8:12, :] = jnp.where(flags[1] > 0, low[piece // 2, where, :], 0.0)
            main[c, level, 76:80, :] = jnp.where(flags[1] < NTY - 1, high[piece // 2, where, :], 0.0)


def tendency(centre, east, west, north, south, vertical):
    u, v, _ = centre
    up, vp = jnp.maximum(u, 0.0), jnp.maximum(v, 0.0)
    k_west, k_east = up + 0.25, up - u + 0.25
    k_south, k_north = vp + 0.25, vp - v + 0.25
    k_centre = k_west + k_east + k_south + k_north + 1.0
    out = []
    for c in range(3):
        out.append(
            k_west * west[c]
            + k_east * east[c]
            + k_south * south[c]
            + k_north * north[c]
            + 0.5 * vertical[c]
            - k_centre * centre[c]
        )
    out[0] = out[0] + 0.3 * v - 0.25 * (east[2] - west[2])
    out[1] = out[1] - 0.3 * u - 0.25 * (north[2] - south[2])
    return out


def edge_lanes(rim, edge, halves):
    spot = iota((72, 128), 1) % 16
    for c in range(3):
        for half in range(halves):
            x = rim[c, half, 8:80, :]
            edge[c, half, 8:80, :] = jnp.where(spot == 4, roll(x, -7, 1), x)


def main_tendency(source, edge, level, last, first, rows):
    lane = iota((rows, 128), 1)
    above, below = jnp.minimum(level + 1, last), jnp.maximum(level - 1, 0)
    shift = 124 - 16 * (level % 8)
    here = pl.ds(first, rows)
    centre, east, west, north, south, vertical = [], [], [], [], [], []
    for c in range(3):
        x = source[c, level, here, :]
        side = pltpu.roll(edge[c, level // 8, here, :], shift, 1)
        centre.append(x)
        east.append(jnp.where(lane == 127, side, roll(x, -1, 1)))
        west.append(jnp.where(lane == 0, side, roll(x, 1, 1)))
        north.append(source[c, level, pl.ds(first + 1, rows), :])
        south.append(source[c, level, pl.ds(first - 1, rows), :])
        vertical.append(source[c, above, here, :] + source[c, below, here, :])
    return centre, tendency(centre, east, west, north, south, vertical)


def rim_tendency(source, halves, half, first, rows):
    lane = iota((rows, 128), 1)
    here = pl.ds(first, rows)
    centre, east, west, north, south, vertical = [], [], [], [], [], []
    for c in range(3):
        x = source[c, half, here, :]
        next_up = source[c, 1, here, :] if half == 0 and halves == 2 else x
        next_down = source[c, 0, here, :] if half == 1 else x
        above = jnp.where(lane < 112, roll(x, -16, 1), x if next_up is x else roll(next_up, -16, 1))
        below = jnp.where(lane >= 16, roll(x, 16, 1), x if next_down is x else roll(next_down, 16, 1))
        centre.append(x)
        east.append(roll(x, -1, 1))
        west.append(roll(x, 1, 1))
        north.append(source[c, half, pl.ds(first + 1, rows), :])
        south.append(source[c, half, pl.ds(first - 1, rows), :])
        vertical.append(above + below)
    return centre, tendency(centre, east, west, north, south, vertical)


CHUNKS = ((8, 24), (32, 24), (56, 24))


def first_stage(source, target, edge, low, high, last, flags):
    def body(level, carry):
        for first, rows in CHUNKS:
            centre, change = main_tendency(source, edge, level, last, first, rows)
            for c in range(3):
                value = centre[c] + 0.2 * change[c]
                if first != 32:
                    value = jnp.where(inside_window(first, rows, flags), value, 0.0)
                target[c, level, pl.ds(first, rows), :] = value
        return carry

    lax.fori_loop(low, high, body, 0)


def second_stage(source, state, edge, low, high, last, chunks, write):
    def body(level, carry):
        for first, rows in chunks:
            centre, change = main_tendency(source, edge, level, last, first, rows)
            for c in range(3):
                old = state[c, level, pl.ds(first, rows), :]
                write(c, level, first, rows, 0.5 * (old + centre[c]) + 0.1 * change[c])
        return carry

    lax.fori_loop(low, high, body, 0)


def first_rim_stage(source, target, halves, flags):
    for half in range(halves):
        for first, rows in CHUNKS:
            centre, change = rim_tendency(source, halves, half, first, rows)
            for c in range(3):
                value = centre[c] + 0.2 * change[c]
                target[c, half, pl.ds(first, rows), :] = jnp.where(rim_inside(first, rows, flags), value, 0.0)


def second_rim_stage(source, state, halves, flags):
    for half in range(halves):
        for first, rows in CHUNKS:
            centre, change = rim_tendency(source, halves, half, first, rows)
            for c in range(3):
                here = pl.ds(first, rows)
                value = 0.5 * (state[c, half, here, :] + centre[c]) + 0.1 * change[c]
                state[c, half, here, :] = jnp.where(rim_inside(first, rows, flags), value, 0.0)


def clear_ends(*buffers):
    for ref in buffers:
        for a in range(ref.shape[0]):
            for b in range(ref.shape[1]):
                ref[a, b, 0:8, :] = jnp.zeros((8, 128), F32)
                ref[a, b, 80:88, :] = jnp.zeros((8, 128), F32)


def wind_kernel(
    flags, atmos, from_west, from_east, east, west, low, high, tiles, out, main, middle, rim, rim_middle, edge
):
    clear_ends(main, middle, rim, rim_middle)
    fill_rim(rim, 1, flags, (from_west, from_east, east, west), low, high)
    fill_main(main, atmos, 3, flags, low, high)
    edge_lanes(rim, edge, 1)
    first_stage(main, middle, edge, 0, 2, 2, flags)
    first_rim_stage(rim, rim_middle, 1, flags)
    edge_lanes(rim_middle, edge, 1)
    later = [[], []]
    for first, rows in ((12, 32), (44, 32)):
        centre, change = main_tendency(middle, edge, 0, 2, first, rows)
        for c in range(2):
            later[c].append(0.5 * (main[c, 0, pl.ds(first, rows), :] + centre[c]) + 0.1 * change[c])
    fields = [atmos[0, 0], atmos[1, 0]] + [jnp.concatenate(x, axis=0) for x in later]
    blocks = jnp.concatenate([swap_blocks(f) for f in fields], axis=1)
    owner, local, _ = slot_facts(tiles[...])
    numbers = slots_of(owner, local, flags[0])
    wanted = iota((64, 128), 0).astype(F32) + 1.0
    chosen = jnp.concatenate([(n == wanted).astype(F32) for n in numbers], axis=0)
    chosen = chosen.T
    half = iota((128, 128), 1) // 64
    onehot = jnp.concatenate([jnp.where(half == j, chosen, 0.0) for j in (0, 1)], axis=0)
    picked = pick(onehot, jnp.concatenate([blocks, blocks], axis=0))
    for j in range(2):
        for q in range(4):
            out[pl.ds(j * 4 + q, 128, stride=8), :] = picked[j * 128 : (j + 1) * 128, q * 128 : (q + 1) * 128]


def step_kernel(
    flags, atmos, from_west, from_east, east, west, low, high, main, rim, middle, rim_middle, edge
):
    clear_ends(main, middle, rim, rim_middle)
    fill_rim(rim, 2, flags, (from_west, from_east, east, west), low, high)
    fill_main(main, atmos, LEV, flags, low, high)
    edge_lanes(rim, edge, 2)
    first_stage(main, middle, edge, 0, LEV, LEV - 1, flags)
    first_rim_stage(rim, rim_middle, 2, flags)
    edge_lanes(rim_middle, edge, 2)

    def write(c, level, first, rows, value):
        if first != 32:
            value = jnp.where(inside_window(first, rows, flags), value, 0.0)
        main[c, level, pl.ds(first, rows), :] = value

    second_stage(middle, main, edge, 0, LEV, LEV - 1, CHUNKS, write)
    second_rim_stage(rim_middle, rim, 2, flags)


def fuel_kernel(rates, heats, category, burn, depth, rate, heat, level):
    kind = category[...]
    rate_cell = jnp.zeros(kind.shape, F32)
    heat_cell = jnp.zeros(kind.shape, F32)
    for k in range(13):
        match = kind == k
        rate_cell = jnp.where(match, rates[k], rate_cell)
        heat_cell = jnp.where(match, heats[k], heat_cell)
    rate[...] = rate_cell
    heat[...] = heat_cell
    level[...] = jnp.where(burn[...] == 1, -depth[...], depth[...])


def fire_kernel(
    flags, received, tiles, rate, heat, level, column, spread, gather, out, new_level, wind, released
):
    mine = jnp.sum(
        jnp.where(iota((32, 128), 1) == flags[0], tiles[...].astype(F32), 0.0), axis=1, keepdims=True
    ).astype(jnp.int32)
    owner, _, live = slot_facts(mine)
    member = (owner == iota((32, 128), 1)).astype(F32)
    before = earlier(member)
    places = [jnp.where(before == float(j), member, 0.0) for j in (0, 1)]

    rows = [[received[pl.ds(j * 4 + q, 128, stride=8), :] for q in range(4)] for j in range(2)]
    table = jnp.concatenate([jnp.concatenate(r, axis=1) for r in rows], axis=0)
    winds = pick(jnp.concatenate(places, axis=1), table)
    winds = jnp.concatenate([winds[:, q * 128 : (q + 1) * 128] for q in range(4)], axis=0)
    high, middle, low = parts(winds)
    wind[...] = dot(high, spread[...]) + dot(middle, spread[...]) + dot(low, spread[...])

    col = column[...]
    cell = iota((8, FC), 1)
    first_col, last_col = col == 0, col == 79
    first_row, last_row = cell < 80, cell >= FC - 80
    for g in range(3):
        here = slice(8 * g, 8 * g + 8)
        alive = live[here]
        p = level[here, :]
        tanh_p = jnp.tanh(p)
        for t in range(2):
            u = wind[t * 64 + 8 * g : t * 64 + 8 * g + 8, :]
            v = wind[t * 64 + 32 + 8 * g : t * 64 + 40 + 8 * g, :]
            east = jnp.where(last_col, p, roll(p, -1, 1))
            west = jnp.where(first_col, p, roll(p, 1, 1))
            north = jnp.where(last_row, p, roll(p, -80, 1))
            south = jnp.where(first_row, p, roll(p, 80, 1))
            gx, gy = 0.5 * (east - west), 0.5 * (north - south)
            square = 1.0 + gx * gx + gy * gy
            inverse = lax.rsqrt(square)
            along = (u * gx + v * gy) * inverse
            softplus = jnp.maximum(along, 0.0) + jnp.log(1.0 + jnp.exp(-jnp.abs(along)))
            moved = p - rate[here, :] * (1.0 + softplus) * (square * inverse)
            p = jnp.where(alive, moved, p)
            tanh_new = jnp.tanh(p)
            released[t * 32 + 8 * g : t * 32 + 8 * g + 8, :] = heat[here, :] * (tanh_p - tanh_new)
            tanh_p = tanh_new
        new_level[here, :] = p
    for t in range(2):
        released[t * 32 + 24 : t * 32 + 32, :] = jnp.zeros((8, FC), F32)
    high, middle, low = parts(released[...])
    sums = 0.02 * (dot(high, gather[...]) + dot(middle, gather[...]) + dot(low, gather[...]))

    heats = jnp.concatenate([sums[0:32], sums[32:64]], axis=1)
    zeros = jnp.zeros((64, 256), F32)
    stacked = jnp.concatenate([heats, heats, zeros], axis=0)
    chosen = jnp.concatenate(places + [jnp.zeros((64, 128), F32)], axis=0).T
    part = iota((128, 128), 1) // 32
    onehot = jnp.concatenate([jnp.where(part == j, chosen, 0.0) for j in (0, 1)], axis=0)
    blocks = pick(onehot, stacked)
    lane = iota((128, 128), 1)
    group, spot = lane // 16, lane % 16
    for j in range(2):
        first = blocks[j * 128 : (j + 1) * 128, 0:128]
        out[pl.ds(j, 128, stride=8), :] = first
        out[pl.ds(2 + j, 128, stride=8), :] = blocks[j * 128 : (j + 1) * 128, 128:256]
        north, south = roll(first, -16, 0), roll(first, 16, 0)
        west, east = roll(first, 1, 0), roll(first, -1, 0)
        strip = jnp.where(group < 2, north, jnp.where(group >= 6, south, 0.0))
        middle_rows = (group >= 2) & (group < 6)
        west_moved = jnp.where(group < 4, roll(west, 30, 1), roll(west, -34, 1))
        east_moved = jnp.where(group < 4, roll(east, 34, 1), roll(east, -30, 1))
        strip = jnp.where(middle_rows & (spot >= 14), west, strip)
        strip = jnp.where(middle_rows & ((spot == 12) | (spot == 13)), west_moved, strip)
        strip = jnp.where(middle_rows & (spot < 2), east, strip)
        strip = jnp.where(middle_rows & ((spot == 2) | (spot == 3)), east_moved, strip)
        strip = jnp.where(lane == 40, roll(roll(first, 17, 0), 41, 1), strip)
        strip = jnp.where(lane == 41, roll(roll(first, 15, 0), 57, 1), strip)
        strip = jnp.where(lane == 56, roll(roll(first, -15, 0), 41, 1), strip)
        strip = jnp.where(lane == 57, roll(roll(first, -17, 0), 57, 1), strip)
        out[pl.ds(4 + j, 128, stride=8), :] = strip
        out[pl.ds(6 + j, 128, stride=8), :] = jnp.zeros((128, 128), F32)


def heat_fields(flags, received, tiles):
    me, ty, tx = flags[0], flags[1], flags[2]
    owner, local, _ = slot_facts(tiles[...])

    def numbers(dy, dx):
        ok = (ty + dy >= 0) & (ty + dy < NTY) & (tx + dx >= 0) & (tx + dx < NTX)
        return slots_of(owner, local, jnp.where(ok, me + dy * NTX + dx, -7))

    here = numbers(0, 0)
    north, south, west, east = numbers(1, 0), numbers(-1, 0), numbers(0, -1), numbers(0, 1)
    south_west, south_east = numbers(-1, -1), numbers(-1, 1)
    north_west, north_east = numbers(1, -1), numbers(1, 1)
    tile = iota((64, 128), 0).astype(F32) + 1.0
    edge_tile = iota((8, 128), 0).astype(F32) + 1.0
    row = iota((80, 128), 0)
    first_tile = ((row // 8 - 1) * 8 + 1).astype(F32)
    body = (row >= 8) & (row < 72)
    home, strips = [], []
    for j in range(2):
        home.append((here[j] == tile).astype(F32))
        from_south = (south[j] == edge_tile + 56.0).astype(F32)
        from_north = (north[j] == edge_tile).astype(F32)
        from_west = body & (west[j] == first_tile + 7.0)
        from_west = from_west | ((row == 7) & (south_west[j] == 64.0)) | ((row == 72) & (north_west[j] == 8.0))
        from_east = body & (east[j] == first_tile)
        from_east = from_east | ((row == 7) & (south_east[j] == 57.0)) | ((row == 72) & (north_east[j] == 1.0))
        strips.append(
            jnp.concatenate([from_south, from_north, from_west.astype(F32), from_east.astype(F32)], axis=0)
        )
    rows = [received[pl.ds(q, 128, stride=8), :] for q in range(6)]
    table = jnp.concatenate(
        [jnp.concatenate([rows[0], rows[2]], axis=1), jnp.concatenate([rows[1], rows[3]], axis=1)], axis=0
    )
    home = pick(jnp.concatenate(home, axis=1), table)
    strips = pick(jnp.concatenate(strips, axis=1), jnp.concatenate(rows[4:6], axis=0))
    lane8 = iota((8, 128), 1)
    blocks = jnp.concatenate(
        [
            jnp.where(lane8 >= 96, strips[0:8], 0.0),
            home[:, 0:128],
            jnp.where(lane8 < 32, strips[8:16], 0.0),
        ],
        axis=0,
    )
    first, second = swap_blocks(blocks), swap_blocks(home[:, 128:256])

    lane = iota((80, 128), 1)
    group, spot, y = lane // 16, lane % 16, row % 8
    straight = (y >= 2) & (y < 6)
    corner = (row == 7) | (row == 72)
    wanted_group = jnp.where(y < 2, y + 2, jnp.where(y > 5, y - 2, y))
    wanted_group = jnp.where(row == 7, 2, jnp.where(row == 72, 3, wanted_group))
    fits = group == wanted_group
    west_spot = spot - jnp.where(corner, 8, jnp.where(straight, 14, 12))
    east_spot = spot - jnp.where(corner, 9, jnp.where(straight, 0, 2))
    width = jnp.where(corner, 1, 2)
    west_fits = fits & (west_spot >= 0) & (west_spot < width)
    east_fits = fits & (east_spot >= 0) & (east_spot < width)
    value = jnp.where(west_fits, strips[16:96], 0.0) + jnp.where(east_fits, strips[96:176], 0.0)
    for shift in (64, 32, 16):
        value = value + roll(value, shift, 1)
    to_west = jnp.where(corner, roll(value, 3, 1), jnp.where(straight, roll(value, -4, 1), roll(value, -2, 1)))
    to_east = jnp.where(corner, roll(value, -6, 1), jnp.where(straight, roll(value, 3, 1), roll(value, 1, 1)))
    rim = jnp.where((lane == 11) | ((lane == 10) & ~corner), to_west, 0.0)
    rim = jnp.where((lane == 3) | ((lane == 4) & ~corner), to_east, rim)
    rim = jnp.where((lane == 12) | (lane == 13), roll(first, 12, 1), rim)
    rim = jnp.where((lane == 1) | (lane == 2), roll(first, 3, 1), rim)
    return first, second, rim


def last_kernel(flags, received, tiles, main_in, rim_in, out, main, middle, rim, rim_middle, edge, sems):
    copies = [
        pltpu.make_async_copy(main_in, main, sems.at[0]),
        pltpu.make_async_copy(rim_in, rim, sems.at[1]),
    ]
    for copy in copies:
        copy.start()
    clear_ends(middle, rim_middle)
    first, second, rim_heat = heat_fields(flags, received, tiles)
    for copy in copies:
        copy.wait()
    main[2, 0, 4:84, :] = main[2, 0, 4:84, :] + first
    rim[2, 0, 4:84, :] = rim[2, 0, 4:84, :] + rim_heat
    edge_lanes(rim, edge, 2)
    first_stage(main, middle, edge, 0, LEV, LEV - 1, flags)
    first_rim_stage(rim, rim_middle, 2, flags)
    edge_lanes(rim_middle, edge, 2)

    def write(c, level, first_row, rows, value):
        out[c, level, pl.ds(first_row - TOP, rows), :] = value

    second_stage(middle, main, edge, 0, LEV, LEV - 1, ((12, 32), (44, 32)), write)
    out[2, 0] = out[2, 0] + second


SMEM = pl.BlockSpec(memory_space=pltpu.SMEM)
VMEM = pl.BlockSpec(memory_space=pltpu.VMEM)
ANY = pl.BlockSpec(memory_space=pl.ANY)


def shape(*dims):
    return jax.ShapeDtypeStruct(dims, F32)


def call(kernel, out_shape, in_specs, scratch=(), flops=0, moved=0, name=None):
    return pl.pallas_call(
        kernel,
        out_shape=out_shape,
        in_specs=in_specs,
        out_specs=jax.tree.map(lambda _: VMEM, out_shape),
        scratch_shapes=list(scratch),
        compiler_params=pltpu.CompilerParams(vmem_limit_bytes=48 << 20),
        cost_estimate=pl.CostEstimate(flops=flops, bytes_accessed=moved, transcendentals=0),
        name=name,
    )


def fire_tables():
    cell = np.arange(FC)
    coarse = (cell // 80 // 5) * 16 + cell % 80 // 5
    spread = (coarse[None, :] == np.arange(128)[:, None]).astype(np.float32)
    column = np.broadcast_to((cell % 80).astype(np.int32)[None, :], (8, FC))
    return jnp.asarray(spread, BF16), jnp.asarray(spread.T, BF16), jnp.asarray(column)


def both_ways(to_next, to_previous, axis):
    size = lax.axis_size(axis)
    ahead = [(i, (i + 1) % size) for i in range(size)]
    return (
        lax.ppermute(to_next, axis, ahead),
        lax.ppermute(to_previous, axis, [(j, i) for i, j in ahead]),
    )


def exchange(x):
    return lax.all_to_all(x.reshape(DEVICES, 8, 128), AXES, 0, 0, tiled=True).reshape(DEVICES * 8, 128)


def on_device(atmos, slot_tile, fuel_cat, front_burn, front_depth, fuel_rate, fuel_heat):
    ty, tx = lax.axis_index("ty"), lax.axis_index("tx")
    flags = jnp.stack([ty * NTX + tx, ty, tx]).astype(jnp.int32)
    tiles = jnp.pad(slot_tile.reshape(DEVICES, SLOTS).T, ((0, 8), (0, 0)), constant_values=-1)
    spread, gather, column = fire_tables()

    message = shape(2, AY, 128)
    east, west = call(pack_columns, (message, message), [VMEM], flops=4_000_000, moved=1_800_000)(atmos)
    from_west, from_east = both_ways(east, west, "tx")
    rate, heat, level = call(
        fuel_kernel, (shape(SLOTS, FC),) * 3, [SMEM, SMEM, VMEM, VMEM, VMEM], flops=4_000_000, moved=1_800_000
    )(fuel_rate, fuel_heat, fuel_cat, front_burn, front_depth)

    rows = shape(28, 8, 128)
    up, down = pl.pallas_call(
        pack_rows,
        grid=(1,),
        out_shape=(rows, rows),
        in_specs=[
            pl.BlockSpec((3, LEV, 8, 128), lambda i: (0, 0, 0, 0)),
            pl.BlockSpec((3, LEV, 8, 128), lambda i: (0, 0, 7, 0)),
        ]
        + [pl.BlockSpec((2, AY, 128), lambda i: (0, 0, 0))] * 4,
        out_specs=(pl.BlockSpec((28, 8, 128), lambda i: (0, 0, 0)),) * 2,
        compiler_params=pltpu.CompilerParams(vmem_limit_bytes=48 << 20),
        name="pack_rows",
    )(atmos, atmos, from_west, from_east, east, west)
    low, high = both_ways(up, down, "ty")

    halo = (from_west, from_east, east, west, low, high)

    def main_buffer(levels):
        return pltpu.VMEM((3, levels, ROWS, 128), F32)

    def rim_buffer(halves):
        return pltpu.VMEM((3, halves, ROWS, 128), F32)

    surface = pl.BlockSpec((3, 4, AY, 128), lambda i: (0, 0, 0, 0))
    whole2 = [pl.BlockSpec((2, AY, 128), lambda i: (0, 0, 0))] * 4
    whole3 = [pl.BlockSpec((28, 8, 128), lambda i: (0, 0, 0))] * 2
    winds = pl.pallas_call(
        wind_kernel,
        grid=(1,),
        out_shape=shape(DEVICES * 8, 128),
        in_specs=[SMEM, surface] + whole2 + whole3 + [pl.BlockSpec((32, 128), lambda i: (0, 0))],
        out_specs=pl.BlockSpec((DEVICES * 8, 128), lambda i: (0, 0)),
        scratch_shapes=[main_buffer(3), main_buffer(3), rim_buffer(1), rim_buffer(1), rim_buffer(1)],
        compiler_params=pltpu.CompilerParams(vmem_limit_bytes=48 << 20),
        name="wind",
    )(flags, atmos, *halo, tiles)
    got_winds = exchange(winds)

    main, rim = call(
        step_kernel,
        (shape(3, LEV, ROWS, 128), shape(3, 2, ROWS, 128)),
        [SMEM] + [VMEM] * 7,
        [main_buffer(LEV), rim_buffer(2), rim_buffer(2)],
        flops=40_000_000,
        moved=8_000_000,
    )(flags, atmos, *halo)

    heats, fire_level = call(
        fire_kernel,
        (shape(DEVICES * 8, 128), shape(SLOTS, FC)),
        [SMEM] + [VMEM] * 8,
        [pltpu.VMEM((128, FC), F32), pltpu.VMEM((64, FC), F32)],
        flops=40_000_000,
        moved=4_000_000,
    )(flags, got_winds, tiles, rate, heat, level, column, spread, gather)
    got_heats = exchange(heats)

    atmos_out = call(
        last_kernel,
        shape(3, LEV, AY, 128),
        [SMEM, VMEM, VMEM, ANY, ANY],
        [
            main_buffer(LEV),
            main_buffer(LEV),
            rim_buffer(2),
            rim_buffer(2),
            rim_buffer(2),
            pltpu.SemaphoreType.DMA((2,)),
        ],
        flops=40_000_000,
        moved=8_000_000,
    )(flags, got_heats, tiles, main, rim)
    return atmos_out, fire_level


def solution(mesh):
    in_specs = (
        P(None, None, "ty", "tx"),
        P(),
        P(("ty", "tx"), None),
        P(("ty", "tx"), None),
        P(("ty", "tx"), None),
        P(),
        P(),
    )
    out_specs = (P(None, None, "ty", "tx"), P(("ty", "tx"), None))
    return jax.shard_map(
        on_device, mesh=mesh, in_specs=in_specs, out_specs=out_specs, check_vma=False
    )
```

time: 663 us -> 82.4 us (0.12)
  waiting for transfers between devices: 389 us -> 18.3 us
  local copies, waits for them, and re-layouts: 147 us -> 14.4 us
  other arithmetic: 70.5 us -> 0.09 us
  Pallas kernels: 0 us -> 25.6 us
  starting transfers between devices: 38.8 us -> 22.7 us
  between operations: 14.7 us -> 0.77 us
    reduce_scatter x2 -> x0, waiting for transfers between devices: 314 us -> none  [on_device(): lax.psum_scatter(send_rows, ('ty', 'tx'), scatter_dimension=0, tiled=True)]
    all_gather x2 -> x0, waiting for transfers between devices: 71.5 us -> none  [on_device(): gathered = lax.all_gather(released, ('ty', 'tx'), axis=0, tiled=True)]
    slice x32 -> x0, local copies, waits for them, and re-layouts: 40.5 us -> none  [the longest x12 19.7 us: with_halo(): last = lax.slice_in_dim(x, length - width, length, axis=dim)]
    reshape x24 -> x2, local copies, waits for them, and re-layouts: 35.2 us -> 0.14 us  [on_device(): slot_tile.reshape(DEVICES, SLOTS)]
    ppermute x16 -> x4, starting transfers between devices: 38.7 us -> 9.14 us  [the longest x2 5.32 us: both_ways(): lax.ppermute(to_next, axis, ahead)]
    gather x4 -> x0, local copies, waits for them, and re-layouts: 26.4 us -> none  [the longest x2 22.1 us: on_device(): jnp.take(blocks, local_tile, axis=0)]
    pallas_call x0 -> x7, Pallas kernels: none -> 25.6 us  [the longest x1 9.11 us: on_device(): call(last_kernel, shape(3, LEV, AY, 128), [SMEM, VMEM, VMEM, ANY, ANY], [...]
    add x8 -> x0, other arithmetic: 23.4 us -> none  [the longest x4 20.6 us: tendency(): change = -advect + LATERAL_MIXING * lateral + VERTICAL_MIXING * vertical]
  transfers between devices with their start and end apart: 20 -> 6, of which waited for: 7 -> 5; matrix products, arithmetic and copies ran while one was open for 26% -> 0% of each run, Pallas kernels for 0% -> 11%
where the time goes in v1:
time: 82.4 us; the launch traced here: 81.9 us
  Pallas kernels  25.6 us (31%)
  starting transfers between devices  22.7 us (28%)
  waiting for transfers between devices  18.3 us (22%)
  local copies, waits for them, and re-layouts  14.4 us (17%)
    unnamed x40, local copies, waits for them, and re-layouts  14.2 us
    all_to_all x2, starting transfers between devices, exchange(): lax.all_to_all(x.reshape(DEVICES, 8, 128), AXES, 0, 0, tiled=True)  13.5 us
    all_to_all x2, waiting for transfers between devices, exchange(): lax.all_to_all(x.reshape(DEVICES, 8, 128), AXES, 0, 0, tiled=True)  12.8 us
    pallas_call x1, Pallas kernels, on_device(): call(last_kernel, shape(3, LEV, AY, 128), [SMEM, VMEM, VMEM, ANY, ANY], [...  9.11 us
    pallas_call x1, Pallas kernels, on_device(): call(step_kernel, (shape(3, LEV, ROWS, 128), shape(3, 2, ROWS, 128)), [SM...  7.64 us
    ppermute x2, starting transfers between devices, both_ways(): lax.ppermute(to_next, axis, ahead)  5.32 us
    pallas_call x1, Pallas kernels, on_device(): call(fire_kernel, (shape(DEVICES * 8, 128), shape(SLOTS, FC)), [SMEM] + [...  3.9 us
    ppermute x2, starting transfers between devices, both_ways(): lax.ppermute(to_previous, axis, [(j, i) for i, j in ahead])  3.82 us
  transfers between devices with their start and end apart: 6, of which 5 were waited for; matrix products, arithmetic and copies ran while one was open for 0% of the time, Pallas kernels for 11%

profile of v1, /device:TPU:1, one launch (start us, length us, event | category | flops | bytes accessed | tf_op | source)
XLA Modules:
  0.0 81.9 jit_solution(1203798156019665206)
XLA Ops:
  0.6 1.4 %copy-done = f32[3,16,64,128]{3,2,1,0:T(8,128)S(1)} copy-done((f32[3,16,64,128]{3,2,1,0:T(8,128)S(1)}, f32[3,16,64,128]{3,2,1,0:T(8,128)}, u32[]{:S(2)}) %copy-start) | copy-done | bytes 1572888
  2.0 0.9 %shard_map.113 = (f32[2,64,128]{2,1,0:T(8,128)S(1)}, f32[2,64,128]{2,1,0:T(8,128)S(1)}) custom-call(f32[3,16,64,128]{3,2,1,0:T(8,128)S(1)} %copy-done), custom_call_target="tpu_custom_call" | custom-call | flops 4000000 | bytes 1800000 | tf_op jit(solution)/shard_map/pallas_call | solution.py:567
  2.9 2.1 %collective-permute-start = (f32[2,64,128]{2,1,0:T(8,128)S(1)}, f32[2,64,128]{2,1,0:T(8,128)S(1)}, u32[]{:S(2)}, u32[]{:S(2)}) collective-permute-start(f32[2,64,128]{2,1,0:T(8,128)S(1)} %get-tuple-element.13.east), channel_id=1, source_target_pairs={{0,1},{1,2},{2,3},{3,4},{4,5},{5,6},{6,7},{7,8},{8,9},{9,10},{10,1... | collective-permute-start | bytes 196616 | tf_op jit(solution)/shard_map/ppermute | solution.py:551
  5.0 3.8 %collective-permute-start.1 = (f32[2,64,128]{2,1,0:T(8,128)S(1)}, f32[2,64,128]{2,1,0:T(8,128)S(1)}, u32[]{:S(2)}, u32[]{:S(2)}) collective-permute-start(f32[2,64,128]{2,1,0:T(8,128)S(1)} %get-tuple-element.14.west), channel_id=1, source_target_pairs={{1,0},{2,1},{3,2},{4,3},{5,4},{6,5},{7,6},{8,7},{9,8},{10,9},{11,1... | collective-permute-start | bytes 196616 | tf_op jit(solution)/shard_map/ppermute | solution.py:552
  8.9 1.5 %collective-permute-done.from_west = f32[2,64,128]{2,1,0:T(8,128)S(1)} collective-permute-done((f32[2,64,128]{2,1,0:T(8,128)S(1)}, f32[2,64,128]{2,1,0:T(8,128)S(1)}, u32[]{:S(2)}, u32[]{:S(2)}) %collective-permute-start) | collective-permute-done | bytes 65568 | tf_op jit(solution)/shard_map/ppermute | solution.py:551
  10.5 3.2 %collective-permute-start.2 = (f32[28,8,128]{2,1,0:T(8,128)S(1)}, f32[28,8,128]{2,1,0:T(8,128)S(1)}, u32[]{:S(2)}, u32[]{:S(2)}) collective-permute-start(f32[28,8,128]{2,1,0:T(8,128)S(1)} %get-tuple-element.15), channel_id=1, source_target_pairs={{0,16},{16,32},{32,48},{48,64},{64,80},{80,96},{96,112},{112,0},{1... | collective-permute-start | bytes 344072 | tf_op jit(solution)/shard_map/ppermute | solution.py:551
  13.7 0.1 reshape.19
  13.9 0.1 pad_add_fusion.flags
  14.0 1.5 %collective-permute-done.2.low = f32[28,8,128]{2,1,0:T(8,128)S(1)} collective-permute-done((f32[28,8,128]{2,1,0:T(8,128)S(1)}, f32[28,8,128]{2,1,0:T(8,128)S(1)}, u32[]{:S(2)}, u32[]{:S(2)}) %collective-permute-start.2) | collective-permute-done | bytes 114720 | tf_op jit(solution)/shard_map/ppermute | solution.py:551
  15.5 2.4 %collective-permute-done.3.high = f32[28,8,128]{2,1,0:T(8,128)S(1)} collective-permute-done((f32[28,8,128]{2,1,0:T(8,128)S(1)}, f32[28,8,128]{2,1,0:T(8,128)S(1)}, u32[]{:S(2)}, u32[]{:S(2)}) %collective-permute-start.3) | collective-permute-done | bytes 114720 | tf_op jit(solution)/shard_map/ppermute | solution.py:552
  17.9 3.0 %wind.1 = f32[1024,128]{1,0:T(8,128)} custom-call(s32[3]{0:T(128)S(1)} %pad_add_fusion.flags, f32[3,16,64,128]{3,2,1,0:T(8,128)S(1)} %copy-done.1, f32[2,64,128]{2,1,0:T(8,128)S(1)} %collective-permute-done.from_west, f32[2,64,128]{2,1,0:T(8,128)S(1)} %collective-permute-done.1.from_east, f32[2,64,128]{2,1,0:T(8,128)S(1)} %get-tuple-element.13.east, ...), custom_call_target="tpu_custom_call" | custom-call | tf_op jit(solution)/shard_map/wind/pallas_call | solution.py:600
  20.9 9.4 %all-to-all-start = ((f32[128,8,128]{2,1,0:T(8,128)}), f32[128,8,128]{2,1,0:T(8,128)S(1)}, u32[]{:S(2)}, u32[]{:S(2)}) async-start(f32[128,8,128]{2,1,0:T(8,128)} %bitcast.4), calls=%async_computation | async-start | bytes 1048576 | tf_op jit(solution)/shard_map/all_to_all | solution.py:557
  30.3 1.0 %copy-done.7 = s32[24,3200]{1,0:T(8,128)S(1)} copy-done((s32[24,3200]{1,0:T(8,128)S(1)}, s32[24,3200]{1,0:T(8,128)}, u32[]{:S(2)}) %copy-start.7) | copy-done | bytes 307224
  31.3 1.0 %copy-done.8 = s32[24,3200]{1,0:T(8,128)S(1)} copy-done((s32[24,3200]{1,0:T(8,128)S(1)}, s32[24,3200]{1,0:T(8,128)}, u32[]{:S(2)}) %copy-start.8) | copy-done | bytes 307224
  32.2 1.0 %copy-done.9 = f32[24,3200]{1,0:T(8,128)S(1)} copy-done((f32[24,3200]{1,0:T(8,128)S(1)}, f32[24,3200]{1,0:T(8,128)}, u32[]{:S(2)}) %copy-start.9) | copy-done | bytes 307224
  33.2 1.1 %shard_map.114 = (f32[24,3200]{1,0:T(8,128)S(1)}, f32[24,3200]{1,0:T(8,128)S(1)}, f32[24,3200]{1,0:T(8,128)S(1)}) custom-call(f32[13]{0:T(128)S(1)} %copy-done.16, f32[13]{0:T(128)S(1)} %copy-done.17, s32[24,3200]{1,0:T(8,128)S(1)} %copy-done.7, s32[24,3200]{1,0:T(8,128)S(1)} %copy-done.8, f32[24,3200]{1,0:T(8,128)S(1)} %copy-done.9), custom_call_target="tpu_custom_call" | custom-call | flops 4000000 | bytes 1800000 | tf_op jit(solution)/shard_map/pallas_call | solution.py:569
  34.3 0.7 copy-done.10
  35.0 0.7 copy-done.12
  35.7 0.7 copy-done.14
  36.4 7.8 %all-to-all-done = f32[128,8,128]{2,1,0:T(8,128)S(1)} async-done(((f32[128,8,128]{2,1,0:T(8,128)}), f32[128,8,128]{2,1,0:T(8,128)S(1)}, u32[]{:S(2)}, u32[]{:S(2)}) %all-to-all-start) | async-done | bytes 524320 | tf_op jit(solution)/shard_map/all_to_all | solution.py:557
  44.2 1.1 %copy-done.5 = bf16[128,3200]{1,0:T(8,128)(2,1)S(1)} copy-done((bf16[128,3200]{1,0:T(8,128)(2,1)S(1)}, bf16[128,3200]{1,0:T(8,128)(2,1)}, u32[]{:S(2)}) %copy-start.5) | copy-done | bytes 819224
  45.4 1.0 %copy-done.11 = f32[24,3200]{1,0:T(8,128)S(1)} copy-done((f32[24,3200]{1,0:T(8,128)S(1)}, f32[24,3200]{1,0:T(8,128)}, u32[]{:S(2)}) %copy-start.11) | copy-done | bytes 307224
  46.3 1.0 %copy-done.13 = f32[24,3200]{1,0:T(8,128)S(1)} copy-done((f32[24,3200]{1,0:T(8,128)S(1)}, f32[24,3200]{1,0:T(8,128)}, u32[]{:S(2)}) %copy-start.13) | copy-done | bytes 307224
  47.3 1.0 %copy-done.15 = f32[24,3200]{1,0:T(8,128)S(1)} copy-done((f32[24,3200]{1,0:T(8,128)S(1)}, f32[24,3200]{1,0:T(8,128)}, u32[]{:S(2)}) %copy-start.15) | copy-done | bytes 307224
  48.3 3.9 %shard_map.115 = (f32[1024,128]{1,0:T(8,128)S(1)}, f32[24,3200]{1,0:T(8,128)}) custom-call(s32[3]{0:T(128)S(1)} %pad_add_fusion.flags, f32[1024,128]{1,0:T(8,128)S(1)} %bitcast.9, s32[32,128]{1,0:T(8,128)S(1)} %pad.4.tiles, f32[24,3200]{1,0:T(8,128)S(1)} %copy-done.11, f32[24,3200]{1,0:T(8,128)S(1)} %copy-done.13, f32[24,3200]{1,0:T(8,128)S(1)} %copy-done.15, ...), custom_call_target="tpu_custom_call" | custom-call | flops 40000000 | bytes 4000000 | tf_op jit(solution)/shard_map/pallas_call | solution.py:621
  52.2 0.8 copy-done.6
  53.0 4.2 %all-to-all-start.1 = ((f32[128,8,128]{2,1,0:T(8,128)}), f32[128,8,128]{2,1,0:T(8,128)S(1)}, u32[]{:S(2)}, u32[]{:S(2)}) async-start(f32[128,8,128]{2,1,0:T(8,128)} %bitcast.10), calls=%async_computation.1 | async-start | bytes 1048576 | tf_op jit(solution)/shard_map/all_to_all | solution.py:557
  57.1 7.6 %shard_map.116 = (f32[3,16,88,128]{3,2,1,0:T(8,128)S(1)}, f32[3,2,88,128]{3,2,1,0:T(8,128)S(1)}) custom-call(s32[3]{0:T(128)S(1)} %pad_add_fusion.flags, f32[3,16,64,128]{3,2,1,0:T(8,128)S(1)} %copy-done.1, f32[2,64,128]{2,1,0:T(8,128)S(1)} %collective-permute-done.from_west, f32[2,64,128]{2,1,0:T(8,128)S(1)} %collective-permute-done.1.from_east, ...), custom_call_target="tpu_custom_call" | custom-call | flops 40000000 | bytes 8000000 | tf_op jit(solution)/shard_map/pallas_call | solution.py:612
  64.8 1.4 %copy-done.2 = f32[3,16,88,128]{3,2,1,0:T(8,128)} copy-done((f32[3,16,88,128]{3,2,1,0:T(8,128)}, f32[3,16,88,128]{3,2,1,0:T(8,128)S(1)}, u32[]{:S(2)}) %copy-start.2) | copy-done | bytes 2162712
  66.1 5.0 %all-to-all-done.1 = f32[128,8,128]{2,1,0:T(8,128)S(1)} async-done(((f32[128,8,128]{2,1,0:T(8,128)}), f32[128,8,128]{2,1,0:T(8,128)S(1)}, u32[]{:S(2)}, u32[]{:S(2)}) %all-to-all-start.1) | async-done | bytes 524320 | tf_op jit(solution)/shard_map/all_to_all | solution.py:557
  71.2 1.6 %copy-done.3 = f32[3,16,88,128]{3,2,1,0:T(8,128)S(1)} copy-done((f32[3,16,88,128]{3,2,1,0:T(8,128)S(1)}, f32[3,16,88,128]{3,2,1,0:T(8,128)}, u32[]{:S(2)}) %copy-start.3) | copy-done | bytes 2162712
  72.8 9.1 %shard_map.117 = f32[3,16,64,128]{3,2,1,0:T(8,128)} custom-call(s32[3]{0:T(128)S(1)} %pad_add_fusion.flags, f32[1024,128]{1,0:T(8,128)S(1)} %bitcast.8, s32[32,128]{1,0:T(8,128)S(1)} %pad.4.tiles, f32[3,16,88,128]{3,2,1,0:T(8,128)S(1)} %copy-done.3, f32[3,2,88,128]{3,2,1,0:T(8,128)S(1)} %get-tuple-element.22.rim_in), custom_call_target="tpu_custom_call" | custom-call | flops 40000000 | bytes 8000000 | tf_op jit(solution)/shard_map/pallas_call | solution.py:631
  (32 shorter events, 0.2 us)
Async XLA Ops:
  0.6 1.4 %copy-start = (f32[3,16,64,128]{3,2,1,0:T(8,128)S(1)}, f32[3,16,64,128]{3,2,1,0:T(8,128)}, u32[]{:S(2)}) copy-start(f32[3,16,64,128]{3,2,1,0:T(8,128)} %atmos.5) | copy-start | bytes 4718596
  2.9 7.5 %collective-permute-start = (f32[2,64,128]{2,1,0:T(8,128)S(1)}, f32[2,64,128]{2,1,0:T(8,128)S(1)}, u32[]{:S(2)}, u32[]{:S(2)}) collective-permute-start(f32[2,64,128]{2,1,0:T(8,128)S(1)} %get-tuple-element.13.east), channel_id=1, source_target_pairs={{0,1},{1,2},{2,3},{3,4},{4,5},{5,6},{6,7},{7,8},{8,9},{9,10},{10,1... | collective-permute-start | bytes 196616 | tf_op jit(solution)/shard_map/ppermute | solution.py:551
  5.0 8.7 %copy-start.19 = (s32[3072]{0:T(1024)S(1)}, s32[3072]{0:T(1024)}, u32[]{:S(2)}) copy-start(s32[3072]{0:T(1024)} %param.11) | copy-start | bytes 36868
  5.0 12.9 %copy-start.1 = (f32[3,16,64,128]{3,2,1,0:T(8,128)S(1)}, f32[3,16,64,128]{3,2,1,0:T(8,128)}, u32[]{:S(2)}) copy-start(f32[3,16,64,128]{3,2,1,0:T(8,128)} %atmos.5) | copy-start | bytes 4718596
  5.0 5.4 %collective-permute-start.1 = (f32[2,64,128]{2,1,0:T(8,128)S(1)}, f32[2,64,128]{2,1,0:T(8,128)S(1)}, u32[]{:S(2)}, u32[]{:S(2)}) collective-permute-start(f32[2,64,128]{2,1,0:T(8,128)S(1)} %get-tuple-element.14.west), channel_id=1, source_target_pairs={{1,0},{2,1},{3,2},{4,3},{5,4},{6,5},{7,6},{8,7},{9,8},{10,9},{11,1... | collective-permute-start | bytes 196616 | tf_op jit(solution)/shard_map/ppermute | solution.py:552
  10.5 5.0 %collective-permute-start.2 = (f32[28,8,128]{2,1,0:T(8,128)S(1)}, f32[28,8,128]{2,1,0:T(8,128)S(1)}, u32[]{:S(2)}, u32[]{:S(2)}) collective-permute-start(f32[28,8,128]{2,1,0:T(8,128)S(1)} %get-tuple-element.15), channel_id=1, source_target_pairs={{0,16},{16,32},{32,48},{48,64},{64,80},{80,96},{96,112},{112,0},{1... | collective-permute-start | bytes 344072 | tf_op jit(solution)/shard_map/ppermute | solution.py:551
  13.7 4.2 %collective-permute-start.3 = (f32[28,8,128]{2,1,0:T(8,128)S(1)}, f32[28,8,128]{2,1,0:T(8,128)S(1)}, u32[]{:S(2)}, u32[]{:S(2)}) collective-permute-start(f32[28,8,128]{2,1,0:T(8,128)S(1)} %get-tuple-element.16), channel_id=1, source_target_pairs={{16,0},{32,16},{48,32},{64,48},{80,64},{96,80},{112,96},{0,112},{1... | collective-permute-start | bytes 344072 | tf_op jit(solution)/shard_map/ppermute | solution.py:552
  14.0 16.3 %copy-start.16 = (f32[13]{0:T(128)S(1)}, f32[13]{0:T(128)}, u32[]{:S(2)}) copy-start(f32[13]{0:T(128)} %rates.1) | copy-start | bytes 160
  14.0 16.3 %copy-start.17 = (f32[13]{0:T(128)S(1)}, f32[13]{0:T(128)}, u32[]{:S(2)}) copy-start(f32[13]{0:T(128)} %heats.1) | copy-start | bytes 160
  20.9 23.3 %copy-start.18 = (s32[3200]{0:T(1024)S(1)}, s32[3200]{0:T(1024)}, u32[]{:S(2)}) copy-start(s32[3200]{0:T(1024)} %constant.21.clone) | copy-start | bytes 38404
  20.9 23.3 %copy-start.4 = (bf16[3200,128]{1,0:T(8,128)(2,1)S(1)}, bf16[3200,128]{1,0:T(8,128)(2,1)}, u32[]{:S(2)}) copy-start(bf16[3200,128]{1,0:T(8,128)(2,1)} %constant.20.clone.gather) | copy-start | bytes 2457604
  20.9 23.3 %all-to-all-start = ((f32[128,8,128]{2,1,0:T(8,128)}), f32[128,8,128]{2,1,0:T(8,128)S(1)}, u32[]{:S(2)}, u32[]{:S(2)}) async-start(f32[128,8,128]{2,1,0:T(8,128)} %bitcast.4), calls=%async_computation | async-start | bytes 1048576 | tf_op jit(solution)/shard_map/all_to_all | solution.py:557
  30.3 1.0 %copy-start.7 = (s32[24,3200]{1,0:T(8,128)S(1)}, s32[24,3200]{1,0:T(8,128)}, u32[]{:S(2)}) copy-start(s32[24,3200]{1,0:T(8,128)} %category.1) | copy-start | bytes 921604
  31.3 1.0 %copy-start.8 = (s32[24,3200]{1,0:T(8,128)S(1)}, s32[24,3200]{1,0:T(8,128)}, u32[]{:S(2)}) copy-start(s32[24,3200]{1,0:T(8,128)} %burn.1) | copy-start | bytes 921604
  32.2 1.0 %copy-start.9 = (f32[24,3200]{1,0:T(8,128)S(1)}, f32[24,3200]{1,0:T(8,128)}, u32[]{:S(2)}) copy-start(f32[24,3200]{1,0:T(8,128)} %depth.1) | copy-start | bytes 921604
  34.3 0.7 copy-start.10
  35.0 0.7 copy-start.12
  35.7 0.7 copy-start.14
  44.2 1.1 %copy-start.5 = (bf16[128,3200]{1,0:T(8,128)(2,1)S(1)}, bf16[128,3200]{1,0:T(8,128)(2,1)}, u32[]{:S(2)}) copy-start(bf16[128,3200]{1,0:T(8,128)(2,1)} %constant.19.clone.spread) | copy-start | bytes 2457604
  45.4 1.0 %copy-start.11 = (f32[24,3200]{1,0:T(8,128)S(1)}, f32[24,3200]{1,0:T(8,128)}, u32[]{:S(2)}) copy-start(f32[24,3200]{1,0:T(8,128)} %copy-done.10) | copy-start | bytes 921604
  46.3 1.0 %copy-start.13 = (f32[24,3200]{1,0:T(8,128)S(1)}, f32[24,3200]{1,0:T(8,128)}, u32[]{:S(2)}) copy-start(f32[24,3200]{1,0:T(8,128)} %copy-done.12) | copy-start | bytes 921604
  47.3 1.0 %copy-start.15 = (f32[24,3200]{1,0:T(8,128)S(1)}, f32[24,3200]{1,0:T(8,128)}, u32[]{:S(2)}) copy-start(f32[24,3200]{1,0:T(8,128)} %copy-done.14) | copy-start | bytes 921604
  52.2 0.8 copy-start.6
  53.0 18.2 %all-to-all-start.1 = ((f32[128,8,128]{2,1,0:T(8,128)}), f32[128,8,128]{2,1,0:T(8,128)S(1)}, u32[]{:S(2)}, u32[]{:S(2)}) async-start(f32[128,8,128]{2,1,0:T(8,128)} %bitcast.10), calls=%async_computation.1 | async-start | bytes 1048576 | tf_op jit(solution)/shard_map/all_to_all | solution.py:557
  64.8 1.4 %copy-start.2 = (f32[3,16,88,128]{3,2,1,0:T(8,128)}, f32[3,16,88,128]{3,2,1,0:T(8,128)S(1)}, u32[]{:S(2)}) copy-start(f32[3,16,88,128]{3,2,1,0:T(8,128)S(1)} %get-tuple-element.21.main_in) | copy-start | bytes 6488068
  71.2 1.6 %copy-start.3 = (f32[3,16,88,128]{3,2,1,0:T(8,128)S(1)}, f32[3,16,88,128]{3,2,1,0:T(8,128)}, u32[]{:S(2)}) copy-start(f32[3,16,88,128]{3,2,1,0:T(8,128)} %copy-done.2) | copy-start | bytes 6488068

commit v2 on v1

v2 whole, which is shorter than its diff:
```python
import jax
import jax.numpy as jnp
from jax import lax
from jax.experimental import pallas as pl
from jax.experimental.pallas import tpu as pltpu
from jax.sharding import PartitionSpec as P

AXES = ("ty", "tx")
NTY, NTX, DEVICES = 8, 16, 128
LEV, AY, AX = 16, 64, 128
SLOTS, FC = 24, 3200
ROWS = 88
TOP = 12
F32, BF16 = jnp.float32, jnp.bfloat16


def roll(x, shift, axis):
    size = x.shape[axis]
    return pltpu.roll(x, shift % size, axis) if shift % size else x


def iota(shape, dim):
    return lax.broadcasted_iota(jnp.int32, shape, dim)


def parts(x):
    high = x.astype(BF16)
    rest = x - high.astype(F32)
    middle = rest.astype(BF16)
    low = (rest - middle.astype(F32)).astype(BF16)
    return high, middle, low


def dot(a, b):
    return jnp.dot(a, b, preferred_element_type=F32)


def dot_rows(a, b):
    return lax.dot_general(a, b, (((1,), (1,)), ((), ())), preferred_element_type=F32)


def pick(onehot, x):
    high, middle, _ = parts(x)
    return dot(onehot, high) + dot(onehot, middle)


def swap_blocks(x):
    x = x.reshape(x.shape[0] // 8, 8, 128)
    sub, group = iota(x.shape, 1), iota(x.shape, 2) // 16
    for step in (1, 2, 4):
        sub_bit, group_bit = (sub & step) != 0, (group & step) != 0
        below = roll(roll(x, -step, 1), 16 * step, 2)
        above = roll(roll(x, step, 1), -16 * step, 2)
        x = jnp.where(sub_bit == group_bit, x, jnp.where(group_bit, below, above))
    return x.reshape(x.shape[0] * 8, 128)


def pick_right(x, onehot, product):
    high, middle, _ = parts(x)
    return product(high, onehot) + product(middle, onehot)


def slot_facts(tile):
    row, col = tile >> 7, tile & 127
    owner = (row >> 3) * NTX + (col >> 3)
    local = (row & 7) * 8 + (col & 7)
    live = tile >= 0
    return jnp.where(live, owner, -1), local + 1, live


def earlier(member):
    lower = (iota((32, 32), 0) > iota((32, 32), 1)).astype(F32).astype(BF16)
    return dot(lower, member.astype(BF16))


def slots_of(owner, local, home):
    member = (owner == home).astype(F32)
    before = earlier(member)
    numbers = member * local.astype(F32)
    return [
        jnp.sum(jnp.where(before == float(j), numbers, 0.0), axis=0, keepdims=True)
        for j in (0, 1)
    ]


def pack_rows(atmos, up, down, low_rows, high_rows, sems):
    copies = [
        pltpu.make_async_copy(atmos.at[:, :, pl.ds(0, 8), :], low_rows, sems.at[0]),
        pltpu.make_async_copy(atmos.at[:, :, pl.ds(AY - 8, 8), :], high_rows, sems.at[1]),
    ]
    for copy in copies:
        copy.start()
    for copy in copies:
        copy.wait()
    for c in range(3):
        for level in range(LEV):
            plane = c * LEV + level
            where = pl.ds(4 * (plane % 2), 4)
            up[plane // 2, where, :] = high_rows[c, level, 4:8, :]
            down[plane // 2, where, :] = low_rows[c, level, 0:4, :]


def packed_columns(plane, half, rows):
    lane = iota((rows, 128), 1)
    group, spot = lane // 16, lane % 16
    to_east = jnp.zeros((rows, 128), F32)
    to_west = jnp.zeros((rows, 128), F32)
    for c in range(3):
        both = jnp.zeros((rows, 128), F32)
        for k in range(8):
            moved = roll(plane(c, half * 8 + k), 16 * k + 4, 1)
            both = jnp.where(group == k, moved, both)
        inside = (spot >= 4 * c) & (spot < 4 * c + 4)
        to_east = jnp.where(inside, roll(both, 4 * c, 1), to_east)
        to_west = jnp.where(inside, roll(both, 4 * c - 4, 1), to_west)
    return to_east, to_west


def pack_columns(atmos, east, west, surface, blocks, planes, sems):
    copies = [
        pltpu.make_async_copy(atmos.at[:, pl.ds(8 * half, 8)], planes.at[:, pl.ds(8 * half, 8)], sems.at[half])
        for half in range(2)
    ]
    for copy in copies:
        copy.start()
    for half in range(2):
        copies[half].wait()
        if half == 0:
            surface[...] = planes[:, 0:3]
            blocks[...] = jnp.concatenate([swap_blocks(planes[c, 0]) for c in range(2)], axis=1)
        east[half], west[half] = packed_columns(lambda c, level: planes[c, level], half, AY)


def join_columns(east_rows, west_rows, low, high, east, west):
    def plane(c, level):
        piece = c * LEV + level
        where = slice(4 * (piece % 2), 4 * (piece % 2) + 4)
        return jnp.concatenate([low[piece // 2, where, :], high[piece // 2, where, :]], axis=0)

    for half in range(2):
        east[half, 0:AY, :] = east_rows[half]
        west[half, 0:AY, :] = west_rows[half]
        east[half, AY : AY + 8, :], west[half, AY : AY + 8, :] = packed_columns(plane, half, 8)


def rim_of(c, from_west, from_east, east, west):
    spot = iota(east.shape, 1) % 16
    out = jnp.where(spot < 3, roll(east, -(4 * c + 1), 1), 0.0)
    out = jnp.where((spot >= 3) & (spot < 7), roll(from_east, 3 - 4 * c, 1), out)
    out = jnp.where((spot >= 8) & (spot < 12), roll(from_west, 8 - 4 * c, 1), out)
    return jnp.where((spot >= 12) & (spot < 15), roll(west, 12 - 4 * c, 1), out)


def inside_window(first, rows, flags):
    y = iota((rows, 128), 0) + (first - TOP)
    return ((y >= 0) | (flags[1] > 0)) & ((y < AY) | (flags[1] < NTY - 1))


def rim_inside(first, rows, flags):
    spot = iota((rows, 128), 1) % 16
    east_out = (spot >= 3) & (spot < 7) & (flags[2] == NTX - 1)
    west_out = (spot >= 8) & (spot < 12) & (flags[2] == 0)
    return inside_window(first, rows, flags) & ~(east_out | west_out)


def fill_rim(rim, halves, flags, messages):
    for c in range(3):
        for half in range(halves):
            for source, first, rows in ((0, TOP, AY), (AY, 8, 4), (AY + 4, 76, 4)):
                value = rim_of(c, *(m[half, source : source + rows, :] for m in messages))
                rim[c, half, first : first + rows, :] = jnp.where(rim_inside(first, rows, flags), value, 0.0)


def fill_main(main, atmos, levels, flags, low, high):
    for c in range(3):
        for level in levels:
            piece = c * LEV + level
            where = slice(4 * (piece % 2), 4 * (piece % 2) + 4)
            main[c, level, TOP : TOP + AY, :] = atmos[c, level]
            main[c, level, 8:12, :] = jnp.where(flags[1] > 0, low[piece // 2, where, :], 0.0)
            main[c, level, 76:80, :] = jnp.where(flags[1] < NTY - 1, high[piece // 2, where, :], 0.0)


def tendency(centre, east, west, north, south, vertical):
    u, v, _ = centre
    up, vp = jnp.maximum(u, 0.0), jnp.maximum(v, 0.0)
    k_west, k_east = up + 0.25, up - u + 0.25
    k_south, k_north = vp + 0.25, vp - v + 0.25
    k_centre = k_west + k_east + k_south + k_north + 1.0
    out = []
    for c in range(3):
        out.append(
            k_west * west[c]
            + k_east * east[c]
            + k_south * south[c]
            + k_north * north[c]
            + 0.5 * vertical[c]
            - k_centre * centre[c]
        )
    out[0] = out[0] + 0.3 * v - 0.25 * (east[2] - west[2])
    out[1] = out[1] - 0.3 * u - 0.25 * (north[2] - south[2])
    return out


def edge_lanes(rim, edge, halves):
    spot = iota((72, 128), 1) % 16
    for c in range(3):
        for half in range(halves):
            x = rim[c, half, 8:80, :]
            edge[c, half, 8:80, :] = jnp.where(spot == 4, roll(x, -7, 1), x)


def main_tendency(source, edge, level, last, first, rows):
    lane = iota((rows, 128), 1)
    above, below = min(level + 1, last), max(level - 1, 0)
    here = pl.ds(first, rows)
    centre, east, west, north, south, vertical = [], [], [], [], [], []
    for c in range(3):
        x = source[c, level, here, :]
        side = roll(edge[c, level // 8, here, :], 124 - 16 * (level % 8), 1)
        centre.append(x)
        east.append(jnp.where(lane == 127, side, roll(x, -1, 1)))
        west.append(jnp.where(lane == 0, side, roll(x, 1, 1)))
        north.append(source[c, level, pl.ds(first + 1, rows), :])
        south.append(source[c, level, pl.ds(first - 1, rows), :])
        vertical.append(source[c, above, here, :] + source[c, below, here, :])
    return centre, tendency(centre, east, west, north, south, vertical)


def rim_tendency(source, halves, half, first, rows):
    lane = iota((rows, 128), 1)
    here = pl.ds(first, rows)
    centre, east, west, north, south, vertical = [], [], [], [], [], []
    for c in range(3):
        x = source[c, half, here, :]
        next_up = source[c, 1, here, :] if half == 0 and halves == 2 else x
        next_down = source[c, 0, here, :] if half == 1 else x
        above = jnp.where(lane < 112, roll(x, -16, 1), x if next_up is x else roll(next_up, -16, 1))
        below = jnp.where(lane >= 16, roll(x, 16, 1), x if next_down is x else roll(next_down, 16, 1))
        centre.append(x)
        east.append(roll(x, -1, 1))
        west.append(roll(x, 1, 1))
        north.append(source[c, half, pl.ds(first + 1, rows), :])
        south.append(source[c, half, pl.ds(first - 1, rows), :])
        vertical.append(above + below)
    return centre, tendency(centre, east, west, north, south, vertical)


CHUNKS = ((8, 24), (32, 24), (56, 24))
ALL_ROWS = tuple(range(8, 80, 8))
BODY = tuple(range(TOP, TOP + AY, 8))


def window_masks(flags):
    return {first: inside_window(first, 8, flags) for first in (8, 72)}


def first_stage(source, target, edge, levels, last, masks):
    for level in levels:
        for first in ALL_ROWS:
            centre, change = main_tendency(source, edge, level, last, first, 8)
            for c in range(3):
                value = centre[c] + 0.2 * change[c]
                if first in masks:
                    value = jnp.where(masks[first], value, 0.0)
                target[c, level, first : first + 8, :] = value


def second_stage(source, state, edge, levels, last, rows, write):
    for level in levels:
        for first in rows:
            centre, change = main_tendency(source, edge, level, last, first, 8)
            for c in range(3):
                old = state[c, level, first : first + 8, :]
                write(c, level, first, 0.5 * (old + centre[c]) + 0.1 * change[c])


def first_rim_stage(source, target, halves, flags):
    for half in range(halves):
        for first, rows in CHUNKS:
            centre, change = rim_tendency(source, halves, half, first, rows)
            for c in range(3):
                value = centre[c] + 0.2 * change[c]
                target[c, half, pl.ds(first, rows), :] = jnp.where(rim_inside(first, rows, flags), value, 0.0)


def second_rim_stage(source, state, halves, flags):
    for half in range(halves):
        for first, rows in CHUNKS:
            centre, change = rim_tendency(source, halves, half, first, rows)
            for c in range(3):
                here = pl.ds(first, rows)
                value = 0.5 * (state[c, half, here, :] + centre[c]) + 0.1 * change[c]
                state[c, half, here, :] = jnp.where(rim_inside(first, rows, flags), value, 0.0)


def plan_kernel(flags, tiles, wind_plan, fire_plan, fire_sends, alive, home_plan, strip_plan):
    me, ty, tx = flags[0], flags[1], flags[2]
    listed = tiles[...]
    owner, local, _ = slot_facts(listed)

    def numbers(dy, dx):
        ok = (ty + dy >= 0) & (ty + dy < NTY) & (tx + dx >= 0) & (tx + dx < NTX)
        return slots_of(owner, local, jnp.where(ok, me + dy * NTX + dx, -7))

    here = numbers(0, 0)
    north, south, west, east = numbers(1, 0), numbers(-1, 0), numbers(0, -1), numbers(0, 1)
    south_west, south_east = numbers(-1, -1), numbers(-1, 1)
    north_west, north_east = numbers(1, -1), numbers(1, 1)
    tile = iota((64, 128), 0).astype(F32) + 1.0
    edge_tile = iota((8, 128), 0).astype(F32) + 1.0
    row = iota((80, 128), 0)
    first_tile = ((row // 8 - 1) * 8 + 1).astype(F32)
    body = (row >= 8) & (row < 72)

    for j in range(2):
        chosen = (here[j] == tile).astype(F32)
        chosen = jnp.concatenate([chosen, chosen], axis=0).T.astype(BF16)
        wind_plan[j * 128 : (j + 1) * 128, 0:128] = chosen
        wind_plan[j * 128 : (j + 1) * 128, 128:256] = chosen
    mine = jnp.sum(
        jnp.where(iota((32, 128), 1) == me, listed.astype(F32), 0.0), axis=1, keepdims=True
    ).astype(jnp.int32)
    holder, _, live = slot_facts(mine)
    member = (holder == iota((32, 128), 1)).astype(F32)
    before = earlier(member)
    places = [jnp.where(before == float(j), member, 0.0) for j in (0, 1)]
    fire_plan[...] = jnp.concatenate(places, axis=1).astype(BF16)
    alive[...] = jnp.where(live, jnp.ones((32, 128), F32), 0.0)

    chosen = jnp.concatenate(places + [jnp.zeros((64, 128), F32)], axis=0).T
    part = iota((128, 128), 1) // 32
    for j in range(2):
        fire_sends[j * 128 : (j + 1) * 128, :] = jnp.where(part == j, chosen, 0.0).astype(BF16)
        from_south = (south[j] == edge_tile + 56.0).astype(F32)
        from_north = (north[j] == edge_tile).astype(F32)
        from_west = body & (west[j] == first_tile + 7.0)
        from_west = from_west | ((row == 7) & (south_west[j] == 64.0)) | ((row == 72) & (north_west[j] == 8.0))
        from_east = body & (east[j] == first_tile)
        from_east = from_east | ((row == 7) & (south_east[j] == 57.0)) | ((row == 72) & (north_east[j] == 1.0))
        lanes = slice(j * 128, (j + 1) * 128)
        home_plan[:, lanes] = (here[j] == tile).astype(F32).astype(BF16)
        strips = [from_south, from_north, from_west.astype(F32), from_east.astype(F32)]
        strip_plan[:, lanes] = jnp.concatenate(strips, axis=0).astype(BF16)


def wind_kernel(
    flags, planes, blocks, from_west, from_east, east, west, low, high, plan, fuel, out, main, middle, rim, rim_middle,
    edge,
):
    fill_rim(rim, 1, flags, (from_west, from_east, east, west))
    fill_main(main, planes, range(3), flags, low, high)
    edge_lanes(rim, edge, 1)
    first_stage(main, middle, edge, range(2), 2, window_masks(flags))
    first_rim_stage(rim, rim_middle, 1, flags)
    edge_lanes(rim_middle, edge, 1)
    later = [[], []]
    for first in BODY:
        centre, change = main_tendency(middle, edge, 0, 2, first, 8)
        for c in range(2):
            later[c].append(0.5 * (main[c, 0, first : first + 8, :] + centre[c]) + 0.1 * change[c])
    fields = [blocks[...]] + [swap_blocks(jnp.concatenate(x, axis=0)) for x in later]
    pieces = parts(jnp.concatenate(fields, axis=1))
    pieces = jnp.concatenate(pieces + (jnp.zeros((64, 512), BF16),), axis=0)
    picked = dot(plan[...], pieces)
    for j in range(2):
        for q in range(4):
            out[pl.ds(j * 4 + q, 128, stride=8), :] = picked[j * 128 : (j + 1) * 128, q * 128 : (q + 1) * 128]


def step_kernel(
    flags, atmos, from_west, from_east, east, west, low, high, out, rim, main, middle, rim_middle, edge, planes, sems
):
    groups = [pl.ds(4 * g, 4) for g in range(4)]
    loads = [pltpu.make_async_copy(atmos.at[:, x], planes.at[:, x], sems.at[g]) for g, x in enumerate(groups)]
    stores = [pltpu.make_async_copy(main.at[:, x], out.at[:, x], sems.at[4 + g]) for g, x in enumerate(groups)]
    for load in loads:
        load.start()
    fill_rim(rim, 2, flags, (from_west, from_east, east, west))
    edge_lanes(rim, edge, 2)
    masks = window_masks(flags)
    for g in range(4):
        loads[g].wait()
        fill_main(main, planes, range(4 * g, 4 * g + 4), flags, low, high)
        first_stage(main, middle, edge, range(max(4 * g - 1, 0), 4 * g + 3 if g < 3 else LEV), LEV - 1, masks)
    first_rim_stage(rim, rim_middle, 2, flags)
    edge_lanes(rim_middle, edge, 2)

    def write(c, level, first, value):
        if first in masks:
            value = jnp.where(masks[first], value, 0.0)
        main[c, level, first : first + 8, :] = value

    for g in range(4):
        second_stage(middle, main, edge, range(4 * g, 4 * g + 4), LEV - 1, ALL_ROWS, write)
        stores[g].start()
    second_rim_stage(rim_middle, rim, 2, flags)
    for store in stores:
        store.wait()


def slopes(p):
    cell = iota((8, FC), 1)
    col = cell - 80 * ((cell * 52429) >> 22)
    east = jnp.where(col == 79, p, roll(p, -1, 1))
    west = jnp.where(col == 0, p, roll(p, 1, 1))
    north = jnp.where(cell >= FC - 80, p, roll(p, -80, 1))
    south = jnp.where(cell < 80, p, roll(p, 80, 1))
    gx, gy = 0.5 * (east - west), 0.5 * (north - south)
    square = 1.0 + gx * gx + gy * gy
    inverse = lax.rsqrt(square)
    return gx * inverse, gy * inverse, square * inverse


def fuel_kernel(
    rates, heats, category, burn, depth, east, rate, heat, level, slope_x, slope_y, reach, kinds, burns, depths, sems
):
    copies = [
        pltpu.make_async_copy(source, target, sems.at[i])
        for i, (source, target) in enumerate(((category, kinds), (burn, burns), (depth, depths)))
    ]
    for copy in copies:
        copy.start()
    for copy in copies:
        copy.wait()
    for g in range(3):
        here = slice(8 * g, 8 * g + 8)
        kind = kinds[here, :]
        rate_cell = jnp.zeros(kind.shape, F32)
        heat_cell = jnp.zeros(kind.shape, F32)
        for k in range(13):
            match = kind == k
            rate_cell = jnp.where(match, rates[k], rate_cell)
            heat_cell = jnp.where(match, heats[k], heat_cell)
        p = jnp.where(burns[here, :] == 1, -depths[here, :], depths[here, :])
        along_x, along_y, stretch = slopes(p)
        rate[here, :] = rate_cell
        heat[here, :] = heat_cell
        level[here, :] = p
        slope_x[here, :] = along_x
        slope_y[here, :] = along_y
        reach[here, :] = rate_cell * stretch


def fire_kernel(
    received, plan, sends, live, rate, heat, level, slope_x, slope_y, reach, rim,
    out, out_level, wind, released, spread, sent, new_level, sems,
):
    cell = iota((1, FC), 1)
    fire_row = (cell * 52429) >> 22
    fire_col = cell - 80 * fire_row
    coarse = ((fire_row * 13108) >> 16) * 16 + ((fire_col * 13108) >> 16)
    spread[...] = (iota((128, FC), 0) == coarse).astype(F32).astype(BF16)
    rows = [[received[pl.ds(j * 4 + q, 128, stride=8), :] for q in range(4)] for j in range(2)]
    table = jnp.concatenate([jnp.concatenate(r, axis=1) for r in rows], axis=0)
    winds = pick(plan[...], table)
    winds = [winds[0:SLOTS, q * 128 : (q + 1) * 128] for q in range(4)]
    wind[...] = pick_right(jnp.concatenate(winds, axis=0), spread[...], dot)

    for g in range(3):
        here = slice(8 * g, 8 * g + 8)
        alive = live[here, 0:1] > 0.0
        p = level[here, :]
        tanh_p = jnp.tanh(p)
        along_x, along_y, far = slope_x[here, :], slope_y[here, :], reach[here, :]
        for t in range(2):
            if t:
                along_x, along_y, stretch = slopes(p)
                far = rate[here, :] * stretch
            u = wind[t * 48 + 8 * g : t * 48 + 8 * g + 8, :]
            v = wind[t * 48 + 24 + 8 * g : t * 48 + 32 + 8 * g, :]
            along = u * along_x + v * along_y
            softplus = jnp.maximum(along, 0.0) + jnp.log(1.0 + jnp.exp(-jnp.abs(along)))
            p = jnp.where(alive, p - far * (1.0 + softplus), p)
            tanh_new = jnp.tanh(p)
            released[t * 24 + 8 * g : t * 24 + 8 * g + 8, :] = heat[here, :] * (tanh_p - tanh_new)
            tanh_p = tanh_new
        new_level[here, :] = p
    level_copy = pltpu.make_async_copy(new_level, out_level, sems.at[0])
    level_copy.start()
    sums = 0.02 * pick_right(released[...], spread[...], dot_rows)

    heats = jnp.concatenate([sums[0:SLOTS], sums[SLOTS:]], axis=1)
    gap = jnp.zeros((8, 256), F32)
    heats = jnp.concatenate([heats, gap, heats, gap, jnp.zeros((64, 256), F32)], axis=0)
    blocks = pick(sends[...], heats)
    lane = iota((128, 128), 1)
    group, spot = lane // 16, lane % 16
    for j in range(2):
        first = blocks[j * 128 : (j + 1) * 128, 0:128]
        sent[pl.ds(j, 128, stride=6), :] = first
        sent[pl.ds(2 + j, 128, stride=6), :] = blocks[j * 128 : (j + 1) * 128, 128:256]
        north, south = roll(first, -16, 0), roll(first, 16, 0)
        west, east = roll(first, 1, 0), roll(first, -1, 0)
        west_corner, east_corner = roll(west, 41, 1), roll(east, 57, 1)
        strip = jnp.where(group < 2, north, jnp.where(group >= 6, south, 0.0))
        middle_rows = (group >= 2) & (group < 6)
        strip = jnp.where(middle_rows & (spot >= 14), west, strip)
        strip = jnp.where(middle_rows & ((spot == 12) | (spot == 13)), roll(west, 62, 1), strip)
        strip = jnp.where(middle_rows & (spot < 2), east, strip)
        strip = jnp.where(middle_rows & ((spot == 2) | (spot == 3)), roll(east, 66, 1), strip)
        strip = jnp.where(lane == 40, roll(west_corner, 16, 0), strip)
        strip = jnp.where(lane == 41, roll(east_corner, 16, 0), strip)
        strip = jnp.where(lane == 56, roll(west_corner, -16, 0), strip)
        strip = jnp.where(lane == 57, roll(east_corner, -16, 0), strip)
        sent[pl.ds(4 + j, 128, stride=6), :] = strip
    copy = pltpu.make_async_copy(sent, out, sems.at[1])
    copy.start()
    copy.wait()
    level_copy.wait()


def heat_fields(received, home_plan, strip_plan):
    rows = [received[pl.ds(q, 128, stride=6), :] for q in range(6)]
    table = jnp.concatenate(
        [jnp.concatenate([rows[0], rows[2]], axis=1), jnp.concatenate([rows[1], rows[3]], axis=1)], axis=0
    )
    home = pick(home_plan[...], table)
    strips = pick(strip_plan[...], jnp.concatenate(rows[4:6], axis=0))
    lane8 = iota((8, 128), 1)
    blocks = jnp.concatenate(
        [
            jnp.where(lane8 >= 96, strips[0:8], 0.0),
            home[:, 0:128],
            jnp.where(lane8 < 32, strips[8:16], 0.0),
        ],
        axis=0,
    )
    first, second = swap_blocks(blocks), swap_blocks(home[:, 128:256])

    lane, row = iota((80, 128), 1), iota((80, 128), 0)
    group, spot, y = lane // 16, lane % 16, row % 8
    straight = (y >= 2) & (y < 6)
    corner = (row == 7) | (row == 72)
    wanted_group = jnp.where(y < 2, y + 4, jnp.where(y > 5, y - 4, y))
    wanted_group = jnp.where(row == 7, 2, jnp.where(row == 72, 3, wanted_group))
    fits = group == wanted_group
    west_spot = spot - jnp.where(corner, 8, jnp.where(straight, 14, 12))
    east_spot = spot - jnp.where(corner, 9, jnp.where(straight, 0, 2))
    width = jnp.where(corner, 1, 2)
    west_fits = fits & (west_spot >= 0) & (west_spot < width)
    east_fits = fits & (east_spot >= 0) & (east_spot < width)
    value = jnp.where(west_fits, strips[16:96], 0.0) + jnp.where(east_fits, strips[96:176], 0.0)
    for shift in (64, 32, 16):
        value = value + roll(value, shift, 1)
    to_west = jnp.where(corner, roll(value, 3, 1), jnp.where(straight, roll(value, -4, 1), roll(value, -2, 1)))
    to_east = jnp.where(corner, roll(value, -6, 1), jnp.where(straight, roll(value, 3, 1), roll(value, 1, 1)))
    rim = jnp.where((lane == 11) | ((lane == 10) & ~corner), to_west, 0.0)
    rim = jnp.where((lane == 3) | ((lane == 4) & ~corner), to_east, rim)
    rim = jnp.where((lane == 12) | (lane == 13), roll(first, 12, 1), rim)
    rim = jnp.where((lane == 1) | (lane == 2), roll(first, 3, 1), rim)
    return first, second, rim


def upper_kernel(flags, main_in, rim, fire_level, out, kept, main, middle, rim_middle, edge, result, sems):
    groups = [(1, 4), (5, 4), (9, 4), (13, 3)]
    loads = [
        pltpu.make_async_copy(main_in.at[:, pl.ds(*x)], main.at[:, pl.ds(*x)], sems.at[g])
        for g, x in enumerate(groups)
    ]
    for load in loads:
        load.start()
    edge_lanes(rim, edge, 2)
    masks = window_masks(flags)
    for g, (first, count) in enumerate(groups):
        loads[g].wait()
        end = first + count - 1 if g < 3 else LEV
        first_stage(main, middle, edge, range(max(first - 1, 2), end), LEV - 1, masks)
    first_rim_stage(rim, rim_middle, 2, flags)
    edge_lanes(rim_middle, edge, 2)
    kept[...] = middle[:, 2:4]

    def write(c, level, first, value):
        result[c, level - 3, first - TOP : first - TOP + 8, :] = value

    stores = []
    for g, (first, count) in enumerate(((3, 4), (7, 4), (11, 5))):
        second_stage(middle, main, edge, range(first, first + count), LEV - 1, BODY, write)
        part = result.at[:, pl.ds(first - 3, count)]
        stores.append(pltpu.make_async_copy(part, out.at[:, pl.ds(first, count)], sems.at[4 + g]))
        stores[g].start()
    for store in stores:
        store.wait()


def lower_kernel(
    flags, received, home_plan, strip_plan, main_in, rim_in, kept, upper, out, main, middle, rim, rim_middle, edge,
    result, sems,
):
    copy = pltpu.make_async_copy(main_in.at[:, pl.ds(0, 3)], main, sems.at[0])
    copy.start()
    rim[:, 0] = rim_in[:, 0]
    middle[:, 2:4] = kept[...]
    first, second, rim_heat = heat_fields(received, home_plan, strip_plan)
    copy.wait()
    main[2, 0, 4:84, :] = main[2, 0, 4:84, :] + first
    rim[2, 0, 4:84, :] = rim[2, 0, 4:84, :] + rim_heat
    edge_lanes(rim, edge, 1)
    first_stage(main, middle, edge, range(2), 2, window_masks(flags))
    first_rim_stage(rim, rim_middle, 1, flags)
    edge_lanes(rim_middle, edge, 1)

    def write(c, level, row, value):
        if c == 2 and level == 0:
            value = value + second[row - TOP : row - TOP + 8]
        result[c, level, row - TOP : row - TOP + 8, :] = value

    stores = []
    for level in (2, 1, 0):
        second_stage(middle, main, edge, (level,), 3, BODY, write)
        stores.append(pltpu.make_async_copy(result.at[:, level], out.at[:, level], sems.at[1 + level]))
        stores[-1].start()
    for store in stores:
        store.wait()


SMEM = pl.BlockSpec(memory_space=pltpu.SMEM)
VMEM = pl.BlockSpec(memory_space=pltpu.VMEM)
HBM = pl.BlockSpec(memory_space=pltpu.HBM)
ANY = pl.BlockSpec(memory_space=pl.ANY)


def shape(*dims, dtype=F32):
    return jax.ShapeDtypeStruct(dims, dtype)


def hbm(*dims):
    return pltpu.HBM(dims, F32)


def in_hbm(x):
    return pltpu.with_memory_space_constraint(x, pltpu.HBM)


def call(kernel, name, out_shape, in_specs, scratch=(), out_specs=None, flops=0, moved=0, mib=16, aliases=None):
    return pl.pallas_call(
        kernel,
        out_shape=out_shape,
        in_specs=in_specs,
        out_specs=jax.tree.map(lambda _: VMEM, out_shape) if out_specs is None else out_specs,
        scratch_shapes=list(scratch),
        input_output_aliases=aliases or {},
        compiler_params=pltpu.CompilerParams(vmem_limit_bytes=mib << 20),
        cost_estimate=pl.CostEstimate(flops=flops, bytes_accessed=moved, transcendentals=0),
        name=name,
    )


def both_ways(to_next, to_previous, axis):
    size = lax.axis_size(axis)
    ahead = [(i, (i + 1) % size) for i in range(size)]
    return (
        lax.ppermute(to_next, axis, ahead),
        lax.ppermute(to_previous, axis, [(j, i) for i, j in ahead]),
    )


def exchange(x):
    return lax.all_to_all(x.reshape(-1), AXES, 0, 0, tiled=True).reshape(x.shape)


def main_buffer(levels):
    return pltpu.VMEM((3, levels, ROWS, 128), F32)


def rim_buffer(halves):
    return pltpu.VMEM((3, halves, ROWS, 128), F32)


def copy_sems(n):
    return pltpu.SemaphoreType.DMA((n,))


def on_device(atmos, slot_tile, fuel_cat, front_burn, front_depth, fuel_rate, fuel_heat):
    ty, tx = lax.axis_index("ty"), lax.axis_index("tx")
    flags = jnp.stack([ty * NTX + tx, ty, tx]).astype(jnp.int32)
    tiles = jnp.pad(slot_tile.reshape(DEVICES, SLOTS).T, ((0, 8), (0, 0)), constant_values=-1)
    atmos = in_hbm(atmos)

    rows = shape(24, 8, 128)
    eight = pltpu.VMEM((3, LEV, 8, 128), F32)
    up, down = call(pack_rows, "pack_rows", (rows, rows), [HBM], [eight, eight, copy_sems(2)], mib=8)(atmos)
    low, high = both_ways(up, down, "ty")
    body = shape(2, AY, 128)
    east_rows, west_rows, surface, blocks = call(
        pack_columns, "pack_columns", (body, body, shape(3, 3, AY, 128), shape(64, 256)), [HBM], [pltpu.VMEM((3, LEV, AY, 128), F32), copy_sems(2)],
        flops=4_000_000, moved=1_800_000, mib=8,
    )(atmos)
    columns = shape(2, AY + 8, 128)
    east, west = call(join_columns, "join_columns", (columns, columns), [VMEM] * 4, mib=8)(
        east_rows, west_rows, low, high
    )
    from_west, from_east = both_ways(east, west, "tx")
    halo = (from_west, from_east, east, west, low, high)

    cells = shape(SLOTS, FC)
    fuel = call(
        fuel_kernel,
        "fuel",
        (cells,) * 6,
        [SMEM, SMEM, HBM, HBM, HBM, ANY],
        [pltpu.VMEM((SLOTS, FC), jnp.int32)] * 2 + [pltpu.VMEM((SLOTS, FC), F32), copy_sems(3)],
        flops=8_000_000,
        moved=2_800_000,
    )(fuel_rate, fuel_heat, in_hbm(fuel_cat), in_hbm(front_burn), in_hbm(front_depth), east)
    wind_plan, fire_plan, fire_sends, alive, home_plan, strip_plan = call(
        plan_kernel,
        "plan",
        (
            shape(256, 256, dtype=BF16),
            shape(32, 256, dtype=BF16),
            shape(256, 128, dtype=BF16),
            shape(32, 128),
            shape(64, 256, dtype=BF16),
            shape(176, 256, dtype=BF16),
        ),
        [SMEM, VMEM],
        flops=4_000_000,
        moved=400_000,
        mib=8,
    )(flags, tiles)
    winds = call(
        wind_kernel,
        "wind",
        shape(DEVICES * 8, 128),
        [SMEM] + [VMEM] * 9 + [ANY],
        [main_buffer(3), main_buffer(3), rim_buffer(1), rim_buffer(1), rim_buffer(1)],
        flops=10_000_000,
        moved=2_000_000,
        mib=8,
    )(flags, surface, blocks, *halo, wind_plan, fuel[0])
    got_winds = exchange(winds)

    main, rim = call(
        step_kernel,
        "step",
        (hbm(3, LEV, ROWS, 128), shape(3, 2, ROWS, 128)),
        [SMEM, HBM] + [VMEM] * 6,
        [main_buffer(LEV), main_buffer(LEV), rim_buffer(2), rim_buffer(2)]
        + [pltpu.VMEM((3, LEV, AY, 128), F32), copy_sems(8)],
        (HBM, VMEM),
        flops=40_000_000,
        moved=8_000_000,
        mib=12,
    )(flags, atmos, *halo)

    heats, fire_level = call(
        fire_kernel,
        "fire",
        (hbm(DEVICES * 6, 128), hbm(SLOTS, FC)),
        [VMEM] * 10 + [ANY],
        [
            pltpu.VMEM((4 * SLOTS, FC), F32),
            pltpu.VMEM((2 * SLOTS, FC), F32),
            pltpu.VMEM((128, FC), BF16),
            pltpu.VMEM((DEVICES * 6, 128), F32),
            pltpu.VMEM((SLOTS, FC), F32),
            copy_sems(2),
        ],
        (HBM, HBM),
        flops=40_000_000,
        moved=4_000_000,
    )(got_winds, fire_plan, fire_sends, alive, *fuel, rim)
    got_heats = exchange(heats)

    upper, kept = call(
        upper_kernel,
        "upper",
        (hbm(3, LEV, AY, 128), shape(3, 2, ROWS, 128)),
        [SMEM, HBM, VMEM, HBM],
        [main_buffer(LEV), main_buffer(LEV), rim_buffer(2), rim_buffer(2)]
        + [pltpu.VMEM((3, LEV - 3, AY, 128), F32), copy_sems(7)],
        (HBM, VMEM),
        flops=40_000_000,
        moved=8_000_000,
        mib=12,
    )(flags, in_hbm(main), rim, in_hbm(fire_level))
    atmos_out = call(
        lower_kernel,
        "lower",
        hbm(3, LEV, AY, 128),
        [SMEM] + [VMEM] * 3 + [HBM] + [VMEM] * 2 + [HBM],
        [
            main_buffer(3),
            main_buffer(4),
            rim_buffer(1),
            rim_buffer(1),
            rim_buffer(1),
            pltpu.VMEM((3, 3, AY, 128), F32),
            copy_sems(4),
        ],
        HBM,
        flops=10_000_000,
        moved=2_000_000,
        mib=12,
        aliases={7: 0},
    )(flags, got_heats, home_plan, strip_plan, in_hbm(main), rim, kept, in_hbm(upper))
    return atmos_out, fire_level


def solution(mesh):
    in_specs = (
        P(None, None, "ty", "tx"),
        P(),
        P(("ty", "tx"), None),
        P(("ty", "tx"), None),
        P(("ty", "tx"), None),
        P(),
        P(),
    )
    out_specs = (P(None, None, "ty", "tx"), P(("ty", "tx"), None))
    return jax.shard_map(
        on_device, mesh=mesh, in_specs=in_specs, out_specs=out_specs, check_vma=False
    )
```

time: 82.4 us -> 66.5 us (0.81)
  local copies, waits for them, and re-layouts: 14.4 us -> 0.15 us
  starting transfers between devices: 22.7 us -> 18.2 us
  Pallas kernels: 25.6 us -> 27.9 us
    unnamed x40 -> x6, local copies, waits for them, and re-layouts: 14.2 us -> 0.01 us
    all_to_all x2, starting transfers between devices: 13.5 us -> 10.2 us  [exchange(): lax.all_to_all(x.reshape(-1), AXES, 0, 0, tiled=True).reshape(x.shape)]
    ppermute x2, starting transfers between devices: 5.32 us -> 3.04 us  [both_ways(): lax.ppermute(to_next, axis, ahead)]
    pallas_call x7 -> x10, Pallas kernels: 25.6 us -> 27.9 us  [the longest x1 6.7 us: on_device(): call(step_kernel, 'step', (hbm(3, LEV, ROWS, 128), shape(3, 2, ROWS, 128)...]
    all_to_all x2, waiting for transfers between devices: 12.8 us -> 14.2 us  [exchange(): lax.all_to_all(x.reshape(-1), AXES, 0, 0, tiled=True).reshape(x.shape)]
    ppermute x2, starting transfers between devices: 3.82 us -> 4.97 us  [both_ways(): lax.ppermute(to_previous, axis, [(j, i) for i, j in ahead])]
  transfers between devices with their start and end apart: 6 -> 6, of which waited for: 5 -> 4; matrix products, arithmetic and copies ran while one was open for 0% -> 0% of each run, Pallas kernels for 11% -> 27%
where the time goes in v2:
time: 66.5 us; the launch traced here: 66.1 us
  Pallas kernels  27.9 us (42%)
  waiting for transfers between devices  18.9 us (28%)
  starting transfers between devices  18.2 us (27%)
  between operations  0.93 us (1%)
    all_to_all x2, waiting for transfers between devices, exchange(): lax.all_to_all(x.reshape(-1), AXES, 0, 0, tiled=True).reshape(x.shape)  14.2 us
    all_to_all x2, starting transfers between devices, exchange(): lax.all_to_all(x.reshape(-1), AXES, 0, 0, tiled=True).reshape(x.shape)  10.2 us
    pallas_call x1, Pallas kernels, on_device(): call(step_kernel, 'step', (hbm(3, LEV, ROWS, 128), shape(3, 2, ROWS, 128)...  6.7 us
    pallas_call x1, Pallas kernels, on_device(): call(upper_kernel, 'upper', (hbm(3, LEV, AY, 128), shape(3, 2, ROWS, 128)...  5.69 us
    ppermute x2, starting transfers between devices, both_ways(): lax.ppermute(to_previous, axis, [(j, i) for i, j in ahead])  4.97 us
    pallas_call x1, Pallas kernels, on_device(): call(lower_kernel, 'lower', hbm(3, LEV, AY, 128), [SMEM] + [VMEM] * 3 + [...  3.11 us
    ppermute x2, waiting for transfers between devices, both_ways(): lax.ppermute(to_next, axis, ahead)  3.1 us
    ppermute x2, starting transfers between devices, both_ways(): lax.ppermute(to_next, axis, ahead)  3.04 us
  transfers between devices with their start and end apart: 6, of which 4 were waited for; matrix products, arithmetic and copies ran while one was open for 0% of the time, Pallas kernels for 27%

profile of v2, /device:TPU:1, one launch (start us, length us, event | category | flops | bytes accessed | tf_op | source)
XLA Modules:
  0.0 66.1 jit_solution(9067332772154533126)
XLA Ops:
  0.6 0.0 copy-start.2
  0.6 0.0 copy-start.1
  0.7 0.0 copy-start
  0.7 1.1 %pack_rows.1 = (f32[24,8,128]{2,1,0:T(8,128)S(1)}, f32[24,8,128]{2,1,0:T(8,128)S(1)}) custom-call(f32[3,16,64,128]{3,2,1,0:T(8,128)} %atmos.5), custom_call_target="tpu_custom_call" | custom-call | tf_op jit(solution)/shard_map/pack_rows/pallas_call | solution.py:682
  1.8 3.0 %collective-permute-start = (f32[24,8,128]{2,1,0:T(8,128)S(1)}, f32[24,8,128]{2,1,0:T(8,128)S(1)}, u32[]{:S(2)}, u32[]{:S(2)}) collective-permute-start(f32[24,8,128]{2,1,0:T(8,128)S(1)} %get-tuple-element.32), channel_id=1, source_target_pairs={{0,16},{16,32},{32,48},{48,64},{64,80},{80,96},{96,112},{112,0},{1... | collective-permute-start | bytes 294920 | tf_op jit(solution)/shard_map/ppermute | solution.py:653
  4.8 0.0 collective-permute-start.1
  4.8 0.0 copy-done.2
  4.8 0.1 reshape.23
  4.9 0.1 copy.11
  5.0 2.3 %pack_columns.1 = (f32[2,64,128]{2,1,0:T(8,128)S(1)}, f32[2,64,128]{2,1,0:T(8,128)S(1)}, f32[3,3,64,128]{3,2,1,0:T(8,128)S(1)}, f32[64,256]{1,0:T(8,128)S(1)}) custom-call(f32[3,16,64,128]{3,2,1,0:T(8,128)} %atmos.5), custom_call_target="tpu_custom_call" | custom-call | flops 4000000 | bytes 1800000 | tf_op jit(solution)/shard_map/pack_columns/pallas_call | solution.py:685
  7.2 0.0 collective-permute-done.low
  7.2 1.6 %collective-permute-done.1.high = f32[24,8,128]{2,1,0:T(8,128)S(1)} collective-permute-done((f32[24,8,128]{2,1,0:T(8,128)S(1)}, f32[24,8,128]{2,1,0:T(8,128)S(1)}, u32[]{:S(2)}, u32[]{:S(2)}) %collective-permute-start.1) | collective-permute-done | bytes 98336 | tf_op jit(solution)/shard_map/ppermute | solution.py:654
  8.8 0.2 join_columns.1
  9.0 5.0 %collective-permute-start.3 = (f32[2,72,128]{2,1,0:T(8,128)S(1)}, f32[2,72,128]{2,1,0:T(8,128)S(1)}, u32[]{:S(2)}, u32[]{:S(2)}) collective-permute-start(f32[2,72,128]{2,1,0:T(8,128)S(1)} %get-tuple-element.35.west), channel_id=1, source_target_pairs={{1,0},{2,1},{3,2},{4,3},{5,4},{6,5},{7,6},{8,7},{9,8},{10,9},{11,1... | collective-permute-start | bytes 221192 | tf_op jit(solution)/shard_map/ppermute | solution.py:654
  14.0 0.0 collective-permute-start.2
  14.0 0.1 pad_add_fusion.flags
  14.1 0.8 %plan.1 = (bf16[256,256]{1,0:T(8,128)(2,1)S(1)}, bf16[32,256]{1,0:T(8,128)(2,1)S(1)}, bf16[256,128]{1,0:T(8,128)(2,1)S(1)}, f32[32,128]{1,0:T(8,128)S(1)}, bf16[...) custom-call(s32[3]{0:T(128)S(1)} %pad_add_fusion.flags, s32[32,128]{1,0:T(8,128)S(1)} %pad.4.tiles), custom_call_target="tpu_custom_call" | custom-call | flops 4000000 | bytes 400000 | tf_op jit(solution)/shard_map/plan/pallas_call | solution.py:706
  14.9 0.0 copy-done.1
  14.9 0.0 copy-done
  14.9 2.5 %fuel.1 = (f32[24,3200]{1,0:T(8,128)S(1)}, f32[24,3200]{1,0:T(8,128)S(1)}, f32[24,3200]{1,0:T(8,128)S(1)}, f32[24,3200]{1,0:T(8,128)S(1)}, f32[24,3200]{1,0:T(8,128)S(1)}, /*index=5*/f32[24,3200]{1,0:T(8,128)S(1)}) custom-call(f32[13]{0:T(128)S(1)} %copy-done, f32[13]{0:T(128)S(1)} %copy-done.1, s32[24,3200]{1,0:T(8,128)} %category.1, s32[24,3200]{1,0:T(8,128)} %burn.1, ...), custom_call_target="tpu_custom_call" | custom-call | flops 8000000 | bytes 2800000 | tf_op jit(solution)/shard_map/fuel/pallas_call | solution.py:697
  17.4 0.0 collective-permute-done.3.from_east
  17.4 3.1 %collective-permute-done.2.from_west = f32[2,72,128]{2,1,0:T(8,128)S(1)} collective-permute-done((f32[2,72,128]{2,1,0:T(8,128)S(1)}, f32[2,72,128]{2,1,0:T(8,128)S(1)}, u32[]{:S(2)}, u32[]{:S(2)}) %collective-permute-start.2) | collective-permute-done | bytes 73760 | tf_op jit(solution)/shard_map/ppermute | solution.py:653
  20.5 2.5 %wind.1 = f32[1024,128]{1,0:T(8,128)} custom-call(s32[3]{0:T(128)S(1)} %pad_add_fusion.flags, f32[3,3,64,128]{3,2,1,0:T(8,128)S(1)} %get-tuple-element.28.planes, f32[64,256]{1,0:T(8,128)S(1)} %get-tuple-element.29.blocks, f32[2,72,128]{2,1,0:T(8,128)S(1)} %collective-permute-done.2.from_west, f32[2,72,128]{2,1,0:T(8,128)S(1)} %collective-permute-done.3.from_east, ...), custom_call_target="tpu_custom_call" | custom-call | flops 10000000 | bytes 2000000 | tf_op jit(solution)/shard_map/wind/pallas_call | solution.py:722
  23.0 6.0 %all-to-all-start = ((f32[128,1024,1]{1,2,0:T(1,128)}), f32[128,1024,1]{1,2,0:T(1,128)S(1)}, u32[]{:S(2)}, u32[]{:S(2)}) async-start(f32[128,1024,1]{1,2,0:T(1,128)} %bitcast.4), calls=%async_computation | async-start | bytes 1048576 | tf_op jit(solution)/shard_map/all_to_all | solution.py:659
  29.0 6.7 %step.1 = (f32[3,16,88,128]{3,2,1,0:T(8,128)}, f32[3,2,88,128]{3,2,1,0:T(8,128)S(1)}) custom-call(s32[3]{0:T(128)S(1)} %pad_add_fusion.flags, f32[3,16,64,128]{3,2,1,0:T(8,128)} %atmos.5, f32[2,72,128]{2,1,0:T(8,128)S(1)} %collective-permute-done.2.from_west, f32[2,72,128]{2,1,0:T(8,128)S(1)} %collective-permute-done.3.from_east, ...), custom_call_target="tpu_custom_call" | custom-call | flops 40000000 | bytes 8000000 | tf_op jit(solution)/shard_map/step/pallas_call | solution.py:734
  35.7 7.2 %all-to-all-done = f32[128,1024,1]{1,2,0:T(1,128)S(1)} async-done(((f32[128,1024,1]{1,2,0:T(1,128)}), f32[128,1024,1]{1,2,0:T(1,128)S(1)}, u32[]{:S(2)}, u32[]{:S(2)}) %all-to-all-start) | async-done | bytes 524320 | tf_op jit(solution)/shard_map/all_to_all | solution.py:659
  42.9 3.0 %fire.1 = (f32[768,128]{1,0:T(8,128)}, f32[24,3200]{1,0:T(8,128)}) custom-call(f32[1024,128]{1,0:T(8,128)S(1)} %bitcast.8, bf16[32,256]{1,0:T(8,128)(2,1)S(1)} %get-tuple-element.38.plan, bf16[256,128]{1,0:T(8,128)(2,1)S(1)} %get-tuple-element.39.sends, f32[32,128]{1,0:T(8,128)S(1)} %get-tuple-element.40.live, f32[24,3200]{1,0:T(8,128)S(1)} %get-tuple-element.37.fuel.rate, ...), custom_call_target="tpu_custom_call" | custom-call | flops 40000000 | bytes 4000000 | tf_op jit(solution)/shard_map/fire/pallas_call | solution.py:747
  45.9 4.2 %all-to-all-start.1 = ((f32[128,768,1]{1,2,0:T(1,128)}), f32[128,768,1]{1,2,0:T(1,128)S(1)}, u32[]{:S(2)}, u32[]{:S(2)}) async-start(f32[128,768,1]{1,2,0:T(1,128)} %bitcast.10), calls=%async_computation.1 | async-start | bytes 786432 | tf_op jit(solution)/shard_map/all_to_all | solution.py:659
  50.1 5.7 %upper.1 = (f32[3,16,64,128]{3,2,1,0:T(8,128)}, f32[3,2,88,128]{3,2,1,0:T(8,128)S(1)}) custom-call(s32[3]{0:T(128)S(1)} %pad_add_fusion.flags, f32[3,16,88,128]{3,2,1,0:T(8,128)} %get-tuple-element.50.main_in, f32[3,2,88,128]{3,2,1,0:T(8,128)S(1)} %get-tuple-element.46.rim.rim_in, f32[24,3200]{1,0:T(8,128)} %get-tuple-element.27.fire_level), custom_call_target="tpu_custom_call" | custom-call | flops 40000000 | bytes 8000000 | tf_op jit(solution)/shard_map/upper/pallas_call | solution.py:766
  55.8 7.0 %all-to-all-done.1 = f32[128,768,1]{1,2,0:T(1,128)S(1)} async-done(((f32[128,768,1]{1,2,0:T(1,128)}), f32[128,768,1]{1,2,0:T(1,128)S(1)}, u32[]{:S(2)}, u32[]{:S(2)}) %all-to-all-start.1) | async-done | bytes 393248 | tf_op jit(solution)/shard_map/all_to_all | solution.py:659
  62.8 3.1 %lower.1 = f32[3,16,64,128]{3,2,1,0:T(8,128)} custom-call(s32[3]{0:T(128)S(1)} %pad_add_fusion.flags, f32[768,128]{1,0:T(8,128)S(1)} %bitcast.9, bf16[64,256]{1,0:T(8,128)(2,1)S(1)} %get-tuple-element.48.home_plan, bf16[176,256]{1,0:T(8,128)(2,1)S(1)} %get-tuple-element.49.strip_plan, ...), custom_call_target="tpu_custom_call", output_to_operand_aliasing={{}: (7, {})} | custom-call | flops 10000000 | bytes 2000000 | tf_op jit(solution)/shard_map/lower/pallas_call | solution.py:778
  (1 shorter events, 0.0 us)
Async XLA Ops:
  0.6 4.2 %copy-start.2 = (s32[3072]{0:T(1024)S(1)}, s32[3072]{0:T(1024)}, u32[]{:S(2)}) copy-start(s32[3072]{0:T(1024)} %param.8) | copy-start | bytes 36868
  0.6 14.3 %copy-start.1 = (f32[13]{0:T(128)S(1)}, f32[13]{0:T(128)}, u32[]{:S(2)}) copy-start(f32[13]{0:T(128)} %heats.1) | copy-start | bytes 160
  0.7 14.3 %copy-start = (f32[13]{0:T(128)S(1)}, f32[13]{0:T(128)}, u32[]{:S(2)}) copy-start(f32[13]{0:T(128)} %rates.1) | copy-start | bytes 160
  1.8 5.5 %collective-permute-start = (f32[24,8,128]{2,1,0:T(8,128)S(1)}, f32[24,8,128]{2,1,0:T(8,128)S(1)}, u32[]{:S(2)}, u32[]{:S(2)}) collective-permute-start(f32[24,8,128]{2,1,0:T(8,128)S(1)} %get-tuple-element.32), channel_id=1, source_target_pairs={{0,16},{16,32},{32,48},{48,64},{64,80},{80,96},{96,112},{112,0},{1... | collective-permute-start | bytes 294920 | tf_op jit(solution)/shard_map/ppermute | solution.py:653
  4.8 4.0 %collective-permute-start.1 = (f32[24,8,128]{2,1,0:T(8,128)S(1)}, f32[24,8,128]{2,1,0:T(8,128)S(1)}, u32[]{:S(2)}, u32[]{:S(2)}) collective-permute-start(f32[24,8,128]{2,1,0:T(8,128)S(1)} %get-tuple-element.33), channel_id=1, source_target_pairs={{16,0},{32,16},{48,32},{64,48},{80,64},{96,80},{112,96},{0,112},{1... | collective-permute-start | bytes 294920 | tf_op jit(solution)/shard_map/ppermute | solution.py:654
  9.0 8.4 %collective-permute-start.3 = (f32[2,72,128]{2,1,0:T(8,128)S(1)}, f32[2,72,128]{2,1,0:T(8,128)S(1)}, u32[]{:S(2)}, u32[]{:S(2)}) collective-permute-start(f32[2,72,128]{2,1,0:T(8,128)S(1)} %get-tuple-element.35.west), channel_id=1, source_target_pairs={{1,0},{2,1},{3,2},{4,3},{5,4},{6,5},{7,6},{8,7},{9,8},{10,9},{11,1... | collective-permute-start | bytes 221192 | tf_op jit(solution)/shard_map/ppermute | solution.py:654
  14.0 6.5 %collective-permute-start.2 = (f32[2,72,128]{2,1,0:T(8,128)S(1)}, f32[2,72,128]{2,1,0:T(8,128)S(1)}, u32[]{:S(2)}, u32[]{:S(2)}) collective-permute-start(f32[2,72,128]{2,1,0:T(8,128)S(1)} %get-tuple-element.34.east), channel_id=1, source_target_pairs={{0,1},{1,2},{2,3},{3,4},{4,5},{5,6},{6,7},{7,8},{8,9},{9,10},{10,1... | collective-permute-start | bytes 221192 | tf_op jit(solution)/shard_map/ppermute | solution.py:653
  23.0 19.9 %all-to-all-start = ((f32[128,1024,1]{1,2,0:T(1,128)}), f32[128,1024,1]{1,2,0:T(1,128)S(1)}, u32[]{:S(2)}, u32[]{:S(2)}) async-start(f32[128,1024,1]{1,2,0:T(1,128)} %bitcast.4), calls=%async_computation | async-start | bytes 1048576 | tf_op jit(solution)/shard_map/all_to_all | solution.py:659
  45.9 16.9 %all-to-all-start.1 = ((f32[128,768,1]{1,2,0:T(1,128)}), f32[128,768,1]{1,2,0:T(1,128)S(1)}, u32[]{:S(2)}, u32[]{:S(2)}) async-start(f32[128,768,1]{1,2,0:T(1,128)} %bitcast.10), calls=%async_computation.1 | async-start | bytes 786432 | tf_op jit(solution)/shard_map/all_to_all | solution.py:659

commit v3 on v2

--- a/solution.py
+++ b/solution.py
@@ -17,6 +17,11 @@
 def roll(x, shift, axis):
     size = x.shape[axis]
     return pltpu.roll(x, shift % size, axis) if shift % size else x
+
+
+def place():
+    ty, tx = lax.axis_index("ty"), lax.axis_index("tx")
+    return ty * NTX + tx, ty, tx
 
 
 def iota(shape, dim):
@@ -57,7 +62,8 @@
 
 def pick_right(x, onehot, product):
     high, middle, _ = parts(x)
-    return product(high, onehot) + product(middle, onehot)
+    both = product(jnp.concatenate([high, middle], axis=0), onehot)
+    return both[0 : x.shape[0]] + both[x.shape[0] :]
 
 
 def slot_facts(tile):
@@ -100,35 +106,36 @@
             down[plane // 2, where, :] = low_rows[c, level, 0:4, :]
 
 
-def packed_columns(plane, half, rows):
+def packed_columns(plane, half, rows, quarters=None):
     lane = iota((rows, 128), 1)
     group, spot = lane // 16, lane % 16
+    both = [jnp.zeros((rows, 128), F32)] * 3
+    for k in range(8):
+        if quarters is not None and k % 4 == 0:
+            quarters[2 * half + k // 4].wait()
+        for c in range(3):
+            both[c] = jnp.where(group == k, roll(plane(c, half * 8 + k), 16 * k + 4, 1), both[c])
     to_east = jnp.zeros((rows, 128), F32)
     to_west = jnp.zeros((rows, 128), F32)
     for c in range(3):
-        both = jnp.zeros((rows, 128), F32)
-        for k in range(8):
-            moved = roll(plane(c, half * 8 + k), 16 * k + 4, 1)
-            both = jnp.where(group == k, moved, both)
         inside = (spot >= 4 * c) & (spot < 4 * c + 4)
-        to_east = jnp.where(inside, roll(both, 4 * c, 1), to_east)
-        to_west = jnp.where(inside, roll(both, 4 * c - 4, 1), to_west)
+        to_east = jnp.where(inside, roll(both[c], 4 * c, 1), to_east)
+        to_west = jnp.where(inside, roll(both[c], 4 * c - 4, 1), to_west)
     return to_east, to_west
 
 
 def pack_columns(atmos, east, west, surface, blocks, planes, sems):
-    copies = [
-        pltpu.make_async_copy(atmos.at[:, pl.ds(8 * half, 8)], planes.at[:, pl.ds(8 * half, 8)], sems.at[half])
-        for half in range(2)
+    quarters = [
+        pltpu.make_async_copy(atmos.at[:, pl.ds(4 * i, 4)], planes.at[:, pl.ds(4 * i, 4)], sems.at[i])
+        for i in range(4)
     ]
-    for copy in copies:
+    for copy in quarters:
         copy.start()
     for half in range(2):
-        copies[half].wait()
+        east[half], west[half] = packed_columns(lambda c, level: planes[c, level], half, AY, quarters)
         if half == 0:
             surface[...] = planes[:, 0:3]
             blocks[...] = jnp.concatenate([swap_blocks(planes[c, 0]) for c in range(2)], axis=1)
-        east[half], west[half] = packed_columns(lambda c, level: planes[c, level], half, AY)
 
 
 def join_columns(east_rows, west_rows, low, high, east, west):
@@ -294,7 +301,8 @@
                 state[c, half, here, :] = jnp.where(rim_inside(first, rows, flags), value, 0.0)
 
 
-def plan_kernel(flags, tiles, wind_plan, fire_plan, fire_sends, alive, home_plan, strip_plan):
+def plan_kernel(tiles, wind_plan, fire_plan, fire_sends, alive, home_plan, strip_plan):
+    flags = place()
     me, ty, tx = flags[0], flags[1], flags[2]
     listed = tiles[...]
     owner, local, _ = slot_facts(listed)
@@ -345,9 +353,10 @@
 
 
 def wind_kernel(
-    flags, planes, blocks, from_west, from_east, east, west, low, high, plan, fuel, out, main, middle, rim, rim_middle,
+    planes, blocks, from_west, from_east, east, west, low, high, plan, fuel, out, main, middle, rim, rim_middle,
     edge,
 ):
+    flags = place()
     fill_rim(rim, 1, flags, (from_west, from_east, east, west))
     fill_main(main, planes, range(3), flags, low, high)
     edge_lanes(rim, edge, 1)
@@ -369,8 +378,9 @@
 
 
 def step_kernel(
-    flags, atmos, from_west, from_east, east, west, low, high, out, rim, main, middle, rim_middle, edge, planes, sems
+    atmos, from_west, from_east, east, west, low, high, out, rim, main, middle, rim_middle, edge, planes, sems
 ):
+    flags = place()
     groups = [pl.ds(4 * g, 4) for g in range(4)]
     loads = [pltpu.make_async_copy(atmos.at[:, x], planes.at[:, x], sems.at[g]) for g, x in enumerate(groups)]
     stores = [pltpu.make_async_copy(main.at[:, x], out.at[:, x], sems.at[4 + g]) for g, x in enumerate(groups)]
@@ -552,8 +562,9 @@
     return first, second, rim
 
 
-def upper_kernel(flags, main_in, rim, fire_level, out, kept, main, middle, rim_middle, edge, result, sems):
-    groups = [(1, 4), (5, 4), (9, 4), (13, 3)]
+def upper_kernel(main_in, rim, fire_level, out, kept, bottom, main, middle, rim_middle, edge, result, sems):
+    flags = place()
+    groups = [(0, 5), (5, 4), (9, 4), (13, 3)]
     loads = [
         pltpu.make_async_copy(main_in.at[:, pl.ds(*x)], main.at[:, pl.ds(*x)], sems.at[g])
         for g, x in enumerate(groups)
@@ -568,6 +579,7 @@
         first_stage(main, middle, edge, range(max(first - 1, 2), end), LEV - 1, masks)
     first_rim_stage(rim, rim_middle, 2, flags)
     edge_lanes(rim_middle, edge, 2)
+    bottom[...] = main[:, 0:3]
     kept[...] = middle[:, 2:4]
 
     def write(c, level, first, value):
@@ -584,15 +596,14 @@
 
 
 def lower_kernel(
-    flags, received, home_plan, strip_plan, main_in, rim_in, kept, upper, out, main, middle, rim, rim_middle, edge,
+    received, home_plan, strip_plan, main_in, rim_in, kept, upper, out, main, middle, rim, rim_middle, edge,
     result, sems,
 ):
-    copy = pltpu.make_async_copy(main_in.at[:, pl.ds(0, 3)], main, sems.at[0])
-    copy.start()
+    flags = place()
+    main[...] = main_in[...]
     rim[:, 0] = rim_in[:, 0]
     middle[:, 2:4] = kept[...]
     first, second, rim_heat = heat_fields(received, home_plan, strip_plan)
-    copy.wait()
     main[2, 0, 4:84, :] = main[2, 0, 4:84, :] + first
     rim[2, 0, 4:84, :] = rim[2, 0, 4:84, :] + rim_heat
     edge_lanes(rim, edge, 1)
@@ -608,7 +619,7 @@
     stores = []
     for level in (2, 1, 0):
         second_stage(middle, main, edge, (level,), 3, BODY, write)
-        stores.append(pltpu.make_async_copy(result.at[:, level], out.at[:, level], sems.at[1 + level]))
+        stores.append(pltpu.make_async_copy(result.at[:, level], out.at[:, level], sems.at[level]))
         stores[-1].start()
     for store in stores:
         store.wait()
@@ -672,8 +683,6 @@
 
 
 def on_device(atmos, slot_tile, fuel_cat, front_burn, front_depth, fuel_rate, fuel_heat):
-    ty, tx = lax.axis_index("ty"), lax.axis_index("tx")
-    flags = jnp.stack([ty * NTX + tx, ty, tx]).astype(jnp.int32)
     tiles = jnp.pad(slot_tile.reshape(DEVICES, SLOTS).T, ((0, 8), (0, 0)), constant_values=-1)
     atmos = in_hbm(atmos)
 
@@ -683,7 +692,7 @@
     low, high = both_ways(up, down, "ty")
     body = shape(2, AY, 128)
     east_rows, west_rows, surface, blocks = call(
-        pack_columns, "pack_columns", (body, body, shape(3, 3, AY, 128), shape(64, 256)), [HBM], [pltpu.VMEM((3, LEV, AY, 128), F32), copy_sems(2)],
+        pack_columns, "pack_columns", (body, body, shape(3, 3, AY, 128), shape(64, 256)), [HBM], [pltpu.VMEM((3, LEV, AY, 128), F32), copy_sems(4)],
         flops=4_000_000, moved=1_800_000, mib=8,
     )(atmos)
     columns = shape(2, AY + 8, 128)
@@ -714,35 +723,35 @@
             shape(64, 256, dtype=BF16),
             shape(176, 256, dtype=BF16),
         ),
-        [SMEM, VMEM],
+        [VMEM],
         flops=4_000_000,
         moved=400_000,
         mib=8,
-    )(flags, tiles)
+    )(tiles)
     winds = call(
         wind_kernel,
         "wind",
         shape(DEVICES * 8, 128),
-        [SMEM] + [VMEM] * 9 + [ANY],
+        [VMEM] * 9 + [ANY],
         [main_buffer(3), main_buffer(3), rim_buffer(1), rim_buffer(1), rim_buffer(1)],
         flops=10_000_000,
         moved=2_000_000,
         mib=8,
-    )(flags, surface, blocks, *halo, wind_plan, fuel[0])
+    )(surface, blocks, *halo, wind_plan, fuel[0])
     got_winds = exchange(winds)
 
     main, rim = call(
         step_kernel,
         "step",
         (hbm(3, LEV, ROWS, 128), shape(3, 2, ROWS, 128)),
-        [SMEM, HBM] + [VMEM] * 6,
+        [HBM] + [VMEM] * 6,
         [main_buffer(LEV), main_buffer(LEV), rim_buffer(2), rim_buffer(2)]
         + [pltpu.VMEM((3, LEV, AY, 128), F32), copy_sems(8)],
         (HBM, VMEM),
         flops=40_000_000,
         moved=8_000_000,
         mib=12,
-    )(flags, atmos, *halo)
+    )(atmos, *halo)
 
     heats, fire_level = call(
         fire_kernel,
@@ -763,23 +772,23 @@
     )(got_winds, fire_plan, fire_sends, alive, *fuel, rim)
     got_heats = exchange(heats)
 
-    upper, kept = call(
+    upper, kept, bottom = call(
         upper_kernel,
         "upper",
-        (hbm(3, LEV, AY, 128), shape(3, 2, ROWS, 128)),
-        [SMEM, HBM, VMEM, HBM],
+        (hbm(3, LEV, AY, 128), shape(3, 2, ROWS, 128), shape(3, 3, ROWS, 128)),
+        [HBM, VMEM, HBM],
         [main_buffer(LEV), main_buffer(LEV), rim_buffer(2), rim_buffer(2)]
         + [pltpu.VMEM((3, LEV - 3, AY, 128), F32), copy_sems(7)],
-        (HBM, VMEM),
+        (HBM, VMEM, VMEM),
         flops=40_000_000,
         moved=8_000_000,
         mib=12,
-    )(flags, in_hbm(main), rim, in_hbm(fire_level))
+    )(in_hbm(main), rim, in_hbm(fire_level))
     atmos_out = call(
         lower_kernel,
         "lower",
         hbm(3, LEV, AY, 128),
-        [SMEM] + [VMEM] * 3 + [HBM] + [VMEM] * 2 + [HBM],
+        [VMEM] * 6 + [HBM],
         [
             main_buffer(3),
             main_buffer(4),
@@ -787,14 +796,14 @@
             rim_buffer(1),
             rim_buffer(1),
             pltpu.VMEM((3, 3, AY, 128), F32),
-            copy_sems(4),
+            copy_sems(3),
         ],
         HBM,
         flops=10_000_000,
         moved=2_000_000,
         mib=12,
-        aliases={7: 0},
-    )(flags, got_heats, home_plan, strip_plan, in_hbm(main), rim, kept, in_hbm(upper))
+        aliases={6: 0},
+    )(got_heats, home_plan, strip_plan, bottom, rim, kept, in_hbm(upper))
     return atmos_out, fire_level
 
 

time: 66.5 us -> 64 us (0.962)
  Pallas kernels: 27.9 us -> 23.8 us
  waiting for transfers between devices: 18.9 us -> 21 us
    pallas_call x2, Pallas kernels: 5.62 us -> 3.8 us  [the longest x1 1.97 us: on_device(): call(wind_kernel, 'wind', shape(DEVICES * 8, 128), [VMEM] * 9 + [ANY], [m...]
    all_to_all x2, waiting for transfers between devices: 14.2 us -> 15.5 us  [exchange(): lax.all_to_all(x.reshape(-1), AXES, 0, 0, tiled=True).reshape(x.shape)]
    pallas_call x1, Pallas kernels: 6.7 us -> 5.93 us  [on_device(): call(step_kernel, 'step', (hbm(3, LEV, ROWS, 128), shape(3, 2, ROWS, 128)...]
  transfers between devices with their start and end apart: 6 -> 6, of which waited for: 4 -> 4; matrix products, arithmetic and copies ran while one was open for 0% -> 0% of each run, Pallas kernels for 27% -> 25%
where the time goes in v3:
time: 64 us; the launch traced here: 63.6 us
  Pallas kernels  23.8 us (37%)
  waiting for transfers between devices  21 us (33%)
  starting transfers between devices  17.7 us (28%)
  between operations  0.93 us (1%)
    all_to_all x2, waiting for transfers between devices, exchange(): lax.all_to_all(x.reshape(-1), AXES, 0, 0, tiled=True).reshape(x.shape)  15.5 us
    all_to_all x2, starting transfers between devices, exchange(): lax.all_to_all(x.reshape(-1), AXES, 0, 0, tiled=True).reshape(x.shape)  9.72 us
    pallas_call x1, Pallas kernels, on_device(): call(step_kernel, 'step', (hbm(3, LEV, ROWS, 128), shape(3, 2, ROWS, 128)...  5.93 us
    pallas_call x1, Pallas kernels, on_device(): call(upper_kernel, 'upper', (hbm(3, LEV, AY, 128), shape(3, 2, ROWS, 128)...  5.2 us
    ppermute x2, starting transfers between devices, both_ways(): lax.ppermute(to_previous, axis, [(j, i) for i, j in ahead])  4.96 us
    ppermute x2, waiting for transfers between devices, both_ways(): lax.ppermute(to_next, axis, ahead)  3.54 us
    ppermute x2, starting transfers between devices, both_ways(): lax.ppermute(to_next, axis, ahead)  3.04 us
    pallas_call x1, Pallas kernels, on_device(): call(fire_kernel, 'fire', (hbm(DEVICES * 6, 128), hbm(SLOTS, FC)), [VMEM]...  2.8 us
  transfers between devices with their start and end apart: 6, of which 4 were waited for; matrix products, arithmetic and copies ran while one was open for 0% of the time, Pallas kernels for 25%

profile of v3, /device:TPU:1, one launch (start us, length us, event | category | flops | bytes accessed | tf_op | source)
XLA Modules:
  0.0 63.6 jit_solution(11545721359275842138)
XLA Ops:
  0.6 0.0 copy-start.2
  0.6 0.0 copy-start.1
  0.7 0.0 copy-start
  0.7 1.1 %pack_rows.1 = (f32[24,8,128]{2,1,0:T(8,128)S(1)}, f32[24,8,128]{2,1,0:T(8,128)S(1)}) custom-call(f32[3,16,64,128]{3,2,1,0:T(8,128)} %atmos.5), custom_call_target="tpu_custom_call" | custom-call | tf_op jit(solution)/shard_map/pack_rows/pallas_call | solution.py:691
  1.8 3.0 %collective-permute-start = (f32[24,8,128]{2,1,0:T(8,128)S(1)}, f32[24,8,128]{2,1,0:T(8,128)S(1)}, u32[]{:S(2)}, u32[]{:S(2)}) collective-permute-start(f32[24,8,128]{2,1,0:T(8,128)S(1)} %get-tuple-element.33), channel_id=1, source_target_pairs={{0,16},{16,32},{32,48},{48,64},{64,80},{80,96},{96,112},{112,0},{1... | collective-permute-start | bytes 294920 | tf_op jit(solution)/shard_map/ppermute | solution.py:664
  4.8 0.0 collective-permute-start.1
  4.8 2.0 %pack_columns.1 = (f32[2,64,128]{2,1,0:T(8,128)S(1)}, f32[2,64,128]{2,1,0:T(8,128)S(1)}, f32[3,3,64,128]{3,2,1,0:T(8,128)S(1)}, f32[64,256]{1,0:T(8,128)S(1)}) custom-call(f32[3,16,64,128]{3,2,1,0:T(8,128)} %atmos.5), custom_call_target="tpu_custom_call" | custom-call | flops 4000000 | bytes 1800000 | tf_op jit(solution)/shard_map/pack_columns/pallas_call | solution.py:694
  6.8 0.0 collective-permute-done.low
  6.9 2.0 %collective-permute-done.1.high = f32[24,8,128]{2,1,0:T(8,128)S(1)} collective-permute-done((f32[24,8,128]{2,1,0:T(8,128)S(1)}, f32[24,8,128]{2,1,0:T(8,128)S(1)}, u32[]{:S(2)}, u32[]{:S(2)}) %collective-permute-start.1) | collective-permute-done | bytes 98336 | tf_op jit(solution)/shard_map/ppermute | solution.py:665
  8.8 0.2 join_columns.1
  9.0 5.0 %collective-permute-start.3 = (f32[2,72,128]{2,1,0:T(8,128)S(1)}, f32[2,72,128]{2,1,0:T(8,128)S(1)}, u32[]{:S(2)}, u32[]{:S(2)}) collective-permute-start(f32[2,72,128]{2,1,0:T(8,128)S(1)} %get-tuple-element.36.west), channel_id=1, source_target_pairs={{1,0},{2,1},{3,2},{4,3},{5,4},{6,5},{7,6},{8,7},{9,8},{10,9},{11,1... | collective-permute-start | bytes 221192 | tf_op jit(solution)/shard_map/ppermute | solution.py:665
  14.0 0.0 collective-permute-start.2
  14.0 0.0 copy-done.2
  14.0 0.1 reshape.23
  14.1 0.1 copy.11
  14.1 0.3 plan.1
  14.5 0.0 copy-done.1
  14.5 0.0 copy-done
  14.5 2.5 %fuel.1 = (f32[24,3200]{1,0:T(8,128)S(1)}, f32[24,3200]{1,0:T(8,128)S(1)}, f32[24,3200]{1,0:T(8,128)S(1)}, f32[24,3200]{1,0:T(8,128)S(1)}, f32[24,3200]{1,0:T(8,128)S(1)}, /*index=5*/f32[24,3200]{1,0:T(8,128)S(1)}) custom-call(f32[13]{0:T(128)S(1)} %copy-done, f32[13]{0:T(128)S(1)} %copy-done.1, s32[24,3200]{1,0:T(8,128)} %category.1, s32[24,3200]{1,0:T(8,128)} %burn.1, ...), custom_call_target="tpu_custom_call" | custom-call | flops 8000000 | bytes 2800000 | tf_op jit(solution)/shard_map/fuel/pallas_call | solution.py:706
  17.0 0.0 collective-permute-done.3.from_east
  17.0 3.5 %collective-permute-done.2.from_west = f32[2,72,128]{2,1,0:T(8,128)S(1)} collective-permute-done((f32[2,72,128]{2,1,0:T(8,128)S(1)}, f32[2,72,128]{2,1,0:T(8,128)S(1)}, u32[]{:S(2)}, u32[]{:S(2)}) %collective-permute-start.2) | collective-permute-done | bytes 73760 | tf_op jit(solution)/shard_map/ppermute | solution.py:664
  20.5 2.0 %wind.1 = f32[1024,128]{1,0:T(8,128)} custom-call(f32[3,3,64,128]{3,2,1,0:T(8,128)S(1)} %get-tuple-element.29.planes, f32[64,256]{1,0:T(8,128)S(1)} %get-tuple-element.30.blocks, f32[2,72,128]{2,1,0:T(8,128)S(1)} %collective-permute-done.2.from_west, f32[2,72,128]{2,1,0:T(8,128)S(1)} %collective-permute-done.3.from_east, ...), custom_call_target="tpu_custom_call" | custom-call | flops 10000000 | bytes 2000000 | tf_op jit(solution)/shard_map/wind/pallas_call | solution.py:731
  22.5 5.5 %all-to-all-start = ((f32[128,1024,1]{1,2,0:T(1,128)}), f32[128,1024,1]{1,2,0:T(1,128)S(1)}, u32[]{:S(2)}, u32[]{:S(2)}) async-start(f32[128,1024,1]{1,2,0:T(1,128)} %bitcast.1), calls=%async_computation | async-start | bytes 1048576 | tf_op jit(solution)/shard_map/all_to_all | solution.py:670
  28.0 5.9 %step.1 = (f32[3,16,88,128]{3,2,1,0:T(8,128)}, f32[3,2,88,128]{3,2,1,0:T(8,128)S(1)}) custom-call(f32[3,16,64,128]{3,2,1,0:T(8,128)} %atmos.5, f32[2,72,128]{2,1,0:T(8,128)S(1)} %collective-permute-done.2.from_west, f32[2,72,128]{2,1,0:T(8,128)S(1)} %collective-permute-done.3.from_east, f32[2,72,128]{2,1,0:T(8,128)S(1)} %get-tuple-element.35.east, ...), custom_call_target="tpu_custom_call" | custom-call | flops 40000000 | bytes 8000000 | tf_op jit(solution)/shard_map/step/pallas_call | solution.py:743
  34.0 8.0 %all-to-all-done = f32[128,1024,1]{1,2,0:T(1,128)S(1)} async-done(((f32[128,1024,1]{1,2,0:T(1,128)}), f32[128,1024,1]{1,2,0:T(1,128)S(1)}, u32[]{:S(2)}, u32[]{:S(2)}) %all-to-all-start) | async-done | bytes 524320 | tf_op jit(solution)/shard_map/all_to_all | solution.py:670
  41.9 2.8 %fire.1 = (f32[768,128]{1,0:T(8,128)}, f32[24,3200]{1,0:T(8,128)}) custom-call(f32[1024,128]{1,0:T(8,128)S(1)} %bitcast.5, bf16[32,256]{1,0:T(8,128)(2,1)S(1)} %get-tuple-element.39.plan, bf16[256,128]{1,0:T(8,128)(2,1)S(1)} %get-tuple-element.40.sends, f32[32,128]{1,0:T(8,128)S(1)} %get-tuple-element.41.live, f32[24,3200]{1,0:T(8,128)S(1)} %get-tuple-element.38.fuel.rate, ...), custom_call_target="tpu_custom_call" | custom-call | flops 40000000 | bytes 4000000 | tf_op jit(solution)/shard_map/fire/pallas_call | solution.py:756
  44.8 4.2 %all-to-all-start.1 = ((f32[128,768,1]{1,2,0:T(1,128)}), f32[128,768,1]{1,2,0:T(1,128)S(1)}, u32[]{:S(2)}, u32[]{:S(2)}) async-start(f32[128,768,1]{1,2,0:T(1,128)} %bitcast.7), calls=%async_computation.1 | async-start | bytes 786432 | tf_op jit(solution)/shard_map/all_to_all | solution.py:670
  49.0 5.2 %upper.1 = (f32[3,16,64,128]{3,2,1,0:T(8,128)}, f32[3,2,88,128]{3,2,1,0:T(8,128)S(1)}, f32[3,3,88,128]{3,2,1,0:T(8,128)S(1)}) custom-call(f32[3,16,88,128]{3,2,1,0:T(8,128)} %get-tuple-element.51.main_in, f32[3,2,88,128]{3,2,1,0:T(8,128)S(1)} %get-tuple-element.47.rim.rim_in, f32[24,3200]{1,0:T(8,128)} %get-tuple-element.28.fire_level), custom_call_target="tpu_custom_call" | custom-call | flops 40000000 | bytes 8000000 | tf_op jit(solution)/shard_map/upper/pallas_call | solution.py:775
  54.2 7.5 %all-to-all-done.1 = f32[128,768,1]{1,2,0:T(1,128)S(1)} async-done(((f32[128,768,1]{1,2,0:T(1,128)}), f32[128,768,1]{1,2,0:T(1,128)S(1)}, u32[]{:S(2)}, u32[]{:S(2)}) %all-to-all-start.1) | async-done | bytes 393248 | tf_op jit(solution)/shard_map/all_to_all | solution.py:670
  61.6 1.8 %lower.1 = f32[3,16,64,128]{3,2,1,0:T(8,128)} custom-call(f32[768,128]{1,0:T(8,128)S(1)} %bitcast.6, bf16[64,256]{1,0:T(8,128)(2,1)S(1)} %get-tuple-element.49.home_plan, bf16[176,256]{1,0:T(8,128)(2,1)S(1)} %get-tuple-element.50.strip_plan, f32[3,3,88,128]{3,2,1,0:T(8,128)S(1)} %get-tuple-element.53.main_in, ...), custom_call_target="tpu_custom_call", output_to_operand_aliasing={{}: (6, {})} | custom-call | flops 10000000 | bytes 2000000 | tf_op jit(solution)/shard_map/lower/pallas_call | solution.py:787
  (1 shorter events, 0.0 us)
Async XLA Ops:
  0.6 13.4 %copy-start.2 = (s32[3072]{0:T(1024)S(1)}, s32[3072]{0:T(1024)}, u32[]{:S(2)}) copy-start(s32[3072]{0:T(1024)} %param.8) | copy-start | bytes 36868
  0.6 13.8 %copy-start.1 = (f32[13]{0:T(128)S(1)}, f32[13]{0:T(128)}, u32[]{:S(2)}) copy-start(f32[13]{0:T(128)} %heats.1) | copy-start | bytes 160
  0.7 13.8 %copy-start = (f32[13]{0:T(128)S(1)}, f32[13]{0:T(128)}, u32[]{:S(2)}) copy-start(f32[13]{0:T(128)} %rates.1) | copy-start | bytes 160
  1.8 5.1 %collective-permute-start = (f32[24,8,128]{2,1,0:T(8,128)S(1)}, f32[24,8,128]{2,1,0:T(8,128)S(1)}, u32[]{:S(2)}, u32[]{:S(2)}) collective-permute-start(f32[24,8,128]{2,1,0:T(8,128)S(1)} %get-tuple-element.33), channel_id=1, source_target_pairs={{0,16},{16,32},{32,48},{48,64},{64,80},{80,96},{96,112},{112,0},{1... | collective-permute-start | bytes 294920 | tf_op jit(solution)/shard_map/ppermute | solution.py:664
  4.8 4.0 %collective-permute-start.1 = (f32[24,8,128]{2,1,0:T(8,128)S(1)}, f32[24,8,128]{2,1,0:T(8,128)S(1)}, u32[]{:S(2)}, u32[]{:S(2)}) collective-permute-start(f32[24,8,128]{2,1,0:T(8,128)S(1)} %get-tuple-element.34), channel_id=1, source_target_pairs={{16,0},{32,16},{48,32},{64,48},{80,64},{96,80},{112,96},{0,112},{1... | collective-permute-start | bytes 294920 | tf_op jit(solution)/shard_map/ppermute | solution.py:665
  9.0 7.9 %collective-permute-start.3 = (f32[2,72,128]{2,1,0:T(8,128)S(1)}, f32[2,72,128]{2,1,0:T(8,128)S(1)}, u32[]{:S(2)}, u32[]{:S(2)}) collective-permute-start(f32[2,72,128]{2,1,0:T(8,128)S(1)} %get-tuple-element.36.west), channel_id=1, source_target_pairs={{1,0},{2,1},{3,2},{4,3},{5,4},{6,5},{7,6},{8,7},{9,8},{10,9},{11,1... | collective-permute-start | bytes 221192 | tf_op jit(solution)/shard_map/ppermute | solution.py:665
  14.0 6.5 %collective-permute-start.2 = (f32[2,72,128]{2,1,0:T(8,128)S(1)}, f32[2,72,128]{2,1,0:T(8,128)S(1)}, u32[]{:S(2)}, u32[]{:S(2)}) collective-permute-start(f32[2,72,128]{2,1,0:T(8,128)S(1)} %get-tuple-element.35.east), channel_id=1, source_target_pairs={{0,1},{1,2},{2,3},{3,4},{4,5},{5,6},{6,7},{7,8},{8,9},{9,10},{10,1... | collective-permute-start | bytes 221192 | tf_op jit(solution)/shard_map/ppermute | solution.py:664
  22.5 19.5 %all-to-all-start = ((f32[128,1024,1]{1,2,0:T(1,128)}), f32[128,1024,1]{1,2,0:T(1,128)S(1)}, u32[]{:S(2)}, u32[]{:S(2)}) async-start(f32[128,1024,1]{1,2,0:T(1,128)} %bitcast.1), calls=%async_computation | async-start | bytes 1048576 | tf_op jit(solution)/shard_map/all_to_all | solution.py:670
  44.8 16.9 %all-to-all-start.1 = ((f32[128,768,1]{1,2,0:T(1,128)}), f32[128,768,1]{1,2,0:T(1,128)S(1)}, u32[]{:S(2)}, u32[]{:S(2)}) async-start(f32[128,768,1]{1,2,0:T(1,128)} %bitcast.7), calls=%async_computation.1 | async-start | bytes 786432 | tf_op jit(solution)/shard_map/all_to_all | solution.py:670

commit v4 on v3

--- a/solution.py
+++ b/solution.py
@@ -1,5 +1,6 @@
 import jax
 import jax.numpy as jnp
+import numpy as np
 from jax import lax
 from jax.experimental import pallas as pl
 from jax.experimental.pallas import tpu as pltpu
@@ -38,10 +39,6 @@
 
 def dot(a, b):
     return jnp.dot(a, b, preferred_element_type=F32)
-
-
-def dot_rows(a, b):
-    return lax.dot_general(a, b, (((1,), (1,)), ((), ())), preferred_element_type=F32)
 
 
 def pick(onehot, x):
@@ -152,10 +149,9 @@
 
 def rim_of(c, from_west, from_east, east, west):
     spot = iota(east.shape, 1) % 16
-    out = jnp.where(spot < 3, roll(east, -(4 * c + 1), 1), 0.0)
-    out = jnp.where((spot >= 3) & (spot < 7), roll(from_east, 3 - 4 * c, 1), out)
-    out = jnp.where((spot >= 8) & (spot < 12), roll(from_west, 8 - 4 * c, 1), out)
-    return jnp.where((spot >= 12) & (spot < 15), roll(west, 12 - 4 * c, 1), out)
+    out = jnp.where(spot < 4, roll(east, -4 * c, 1), roll(from_east, 4 - 4 * c, 1))
+    out = jnp.where(spot < 8, out, roll(from_west, 8 - 4 * c, 1))
+    return jnp.where(spot < 12, out, roll(west, 12 - 4 * c, 1))
 
 
 def inside_window(first, rows, flags):
@@ -165,7 +161,7 @@
 
 def rim_inside(first, rows, flags):
     spot = iota((rows, 128), 1) % 16
-    east_out = (spot >= 3) & (spot < 7) & (flags[2] == NTX - 1)
+    east_out = (spot >= 4) & (spot < 8) & (flags[2] == NTX - 1)
     west_out = (spot >= 8) & (spot < 12) & (flags[2] == 0)
     return inside_window(first, rows, flags) & ~(east_out | west_out)
 
@@ -214,7 +210,7 @@
     for c in range(3):
         for half in range(halves):
             x = rim[c, half, 8:80, :]
-            edge[c, half, 8:80, :] = jnp.where(spot == 4, roll(x, -7, 1), x)
+            edge[c, half, 8:80, :] = jnp.where(spot == 5, roll(x, -6, 1), x)
 
 
 def main_tendency(source, edge, level, last, first, rows):
@@ -224,10 +220,13 @@
     centre, east, west, north, south, vertical = [], [], [], [], [], []
     for c in range(3):
         x = source[c, level, here, :]
-        side = roll(edge[c, level // 8, here, :], 124 - 16 * (level % 8), 1)
         centre.append(x)
-        east.append(jnp.where(lane == 127, side, roll(x, -1, 1)))
-        west.append(jnp.where(lane == 0, side, roll(x, 1, 1)))
+        east.append(roll(x, -1, 1))
+        west.append(roll(x, 1, 1))
+        if edge is not None:
+            side = roll(edge[c, level // 8, here, :], 123 - 16 * (level % 8), 1)
+            east[c] = jnp.where(lane == 127, side, east[c])
+            west[c] = jnp.where(lane == 0, side, west[c])
         north.append(source[c, level, pl.ds(first + 1, rows), :])
         south.append(source[c, level, pl.ds(first - 1, rows), :])
         vertical.append(source[c, above, here, :] + source[c, below, here, :])
@@ -352,61 +351,34 @@
         strip_plan[:, lanes] = jnp.concatenate(strips, axis=0).astype(BF16)
 
 
-def wind_kernel(
-    planes, blocks, from_west, from_east, east, west, low, high, plan, fuel, out, main, middle, rim, rim_middle,
-    edge,
-):
+def surface_kernel(planes, low, high, after, out, main, middle):
+    flags = place()
+    fill_main(main, planes, range(3), flags, low, high)
+    first_stage(main, middle, None, range(2), 2, window_masks(flags))
+    for first in BODY:
+        centre, change = main_tendency(middle, None, 0, 2, first, 8)
+        for c in range(2):
+            value = 0.5 * (main[c, 0, first : first + 8, :] + centre[c]) + 0.1 * change[c]
+            out[first - TOP : first - TOP + 8, 128 * c : 128 * c + 128] = value
+
+
+def wind_kernel(inner, blocks, from_west, from_east, east, west, plan, out, rim, rim_middle):
     flags = place()
     fill_rim(rim, 1, flags, (from_west, from_east, east, west))
-    fill_main(main, planes, range(3), flags, low, high)
-    edge_lanes(rim, edge, 1)
-    first_stage(main, middle, edge, range(2), 2, window_masks(flags))
     first_rim_stage(rim, rim_middle, 1, flags)
-    edge_lanes(rim_middle, edge, 1)
-    later = [[], []]
-    for first in BODY:
-        centre, change = main_tendency(middle, edge, 0, 2, first, 8)
-        for c in range(2):
-            later[c].append(0.5 * (main[c, 0, first : first + 8, :] + centre[c]) + 0.1 * change[c])
-    fields = [blocks[...]] + [swap_blocks(jnp.concatenate(x, axis=0)) for x in later]
-    pieces = parts(jnp.concatenate(fields, axis=1))
+    centre, change = rim_tendency(rim_middle, 1, 0, TOP, AY)
+    lane = iota((AY, 128), 1)
+    later = []
+    for c in range(2):
+        sides = 0.5 * (rim[c, 0, TOP : TOP + AY, :] + centre[c]) + 0.1 * change[c]
+        field = jnp.where(lane < 2, roll(sides, -12, 1), inner[:, 128 * c : 128 * c + 128])
+        later.append(jnp.where(lane >= 126, roll(sides, 124, 1), field))
+    pieces = parts(jnp.concatenate([blocks[...]] + [swap_blocks(x) for x in later], axis=1))
     pieces = jnp.concatenate(pieces + (jnp.zeros((64, 512), BF16),), axis=0)
     picked = dot(plan[...], pieces)
     for j in range(2):
         for q in range(4):
             out[pl.ds(j * 4 + q, 128, stride=8), :] = picked[j * 128 : (j + 1) * 128, q * 128 : (q + 1) * 128]
-
-
-def step_kernel(
-    atmos, from_west, from_east, east, west, low, high, out, rim, main, middle, rim_middle, edge, planes, sems
-):
-    flags = place()
-    groups = [pl.ds(4 * g, 4) for g in range(4)]
-    loads = [pltpu.make_async_copy(atmos.at[:, x], planes.at[:, x], sems.at[g]) for g, x in enumerate(groups)]
-    stores = [pltpu.make_async_copy(main.at[:, x], out.at[:, x], sems.at[4 + g]) for g, x in enumerate(groups)]
-    for load in loads:
-        load.start()
-    fill_rim(rim, 2, flags, (from_west, from_east, east, west))
-    edge_lanes(rim, edge, 2)
-    masks = window_masks(flags)
-    for g in range(4):
-        loads[g].wait()
-        fill_main(main, planes, range(4 * g, 4 * g + 4), flags, low, high)
-        first_stage(main, middle, edge, range(max(4 * g - 1, 0), 4 * g + 3 if g < 3 else LEV), LEV - 1, masks)
-    first_rim_stage(rim, rim_middle, 2, flags)
-    edge_lanes(rim_middle, edge, 2)
-
-    def write(c, level, first, value):
-        if first in masks:
-            value = jnp.where(masks[first], value, 0.0)
-        main[c, level, first : first + 8, :] = value
-
-    for g in range(4):
-        second_stage(middle, main, edge, range(4 * g, 4 * g + 4), LEV - 1, ALL_ROWS, write)
-        stores[g].start()
-    second_rim_stage(rim_middle, rim, 2, flags)
-    for store in stores:
-        store.wait()
 
 
 def slopes(p):
@@ -422,17 +394,7 @@
     return gx * inverse, gy * inverse, square * inverse
 
 
-def fuel_kernel(
-    rates, heats, category, burn, depth, east, rate, heat, level, slope_x, slope_y, reach, kinds, burns, depths, sems
-):
-    copies = [
-        pltpu.make_async_copy(source, target, sems.at[i])
-        for i, (source, target) in enumerate(((category, kinds), (burn, burns), (depth, depths)))
-    ]
-    for copy in copies:
-        copy.start()
-    for copy in copies:
-        copy.wait()
+def fuel_fields(rates, heats, kinds, burns, depths, rate, heat, level, slope_x, slope_y, reach):
     for g in range(3):
         here = slice(8 * g, 8 * g + 8)
         kind = kinds[here, :]
@@ -440,8 +402,8 @@
         heat_cell = jnp.zeros(kind.shape, F32)
         for k in range(13):
             match = kind == k
-            rate_cell = jnp.where(match, rates[k], rate_cell)
-            heat_cell = jnp.where(match, heats[k], heat_cell)
+            rate_cell = jnp.where(match, rates[0:1, k : k + 1], rate_cell)
+            heat_cell = jnp.where(match, heats[0:1, k : k + 1], heat_cell)
         p = jnp.where(burns[here, :] == 1, -depths[here, :], depths[here, :])
         along_x, along_y, stretch = slopes(p)
         rate[here, :] = rate_cell
@@ -452,10 +414,53 @@
         reach[here, :] = rate_cell * stretch
 
 
+def step_kernel(
+    atmos, from_west, from_east, east, west, low, high, rates, heats, category, burn, depth,
+    out, rim, rate, heat, level, slope_x, slope_y, reach,
+    main, middle, rim_middle, edge, planes, kinds, burns, depths, sems,
+):
+    flags = place()
+    groups = [pl.ds(4 * g, 4) for g in range(4)]
+    loads = [pltpu.make_async_copy(atmos.at[:, x], planes.at[:, x], sems.at[g]) for g, x in enumerate(groups)]
+    stores = [pltpu.make_async_copy(main.at[:, x], out.at[:, x], sems.at[4 + g]) for g, x in enumerate(groups)]
+    fuel = [
+        pltpu.make_async_copy(source, target, sems.at[8 + i])
+        for i, (source, target) in enumerate(((category, kinds), (burn, burns), (depth, depths)))
+    ]
+    for load in loads + fuel:
+        load.start()
+    fill_rim(rim, 2, flags, (from_west, from_east, east, west))
+    edge_lanes(rim, edge, 2)
+    masks = window_masks(flags)
+    for g in range(4):
+        loads[g].wait()
+        fill_main(main, planes, range(4 * g, 4 * g + 4), flags, low, high)
+        first_stage(main, middle, edge, range(max(4 * g - 1, 0), 4 * g + 3 if g < 3 else LEV), LEV - 1, masks)
+    first_rim_stage(rim, rim_middle, 2, flags)
+    edge_lanes(rim_middle, edge, 2)
+
+    def write(c, level, first, value):
+        if first in masks:
+            value = jnp.where(masks[first], value, 0.0)
+        main[c, level, first : first + 8, :] = value
+
+    for g in range(4):
+        second_stage(middle, main, edge, range(4 * g, 4 * g + 4), LEV - 1, ALL_ROWS, write)
+        stores[g].start()
+    second_rim_stage(rim_middle, rim, 2, flags)
+    for load in fuel:
+        load.wait()
+    fuel_fields(rates, heats, kinds, burns, depths, rate, heat, level, slope_x, slope_y, reach)
+    for store in stores:
+        store.wait()
+
+
 def fire_kernel(
-    received, plan, sends, live, rate, heat, level, slope_x, slope_y, reach, rim,
-    out, out_level, wind, released, spread, sent, new_level, sems,
+    received, plan, sends, live, rate, heat, level, slope_x, slope_y, reach, table_in, rim,
+    out, out_level, wind, released, spread, gather, sent, new_level, sems,
 ):
+    gather_copy = pltpu.make_async_copy(table_in, gather, sems.at[2])
+    gather_copy.start()
     cell = iota((1, FC), 1)
     fire_row = (cell * 52429) >> 22
     fire_col = cell - 80 * fire_row
@@ -488,7 +493,8 @@
         new_level[here, :] = p
     level_copy = pltpu.make_async_copy(new_level, out_level, sems.at[0])
     level_copy.start()
-    sums = 0.02 * pick_right(released[...], spread[...], dot_rows)
+    gather_copy.wait()
+    sums = 0.02 * pick_right(released[...], gather[...], dot)
 
     heats = jnp.concatenate([sums[0:SLOTS], sums[SLOTS:]], axis=1)
     gap = jnp.zeros((8, 256), F32)
@@ -554,11 +560,11 @@
     for shift in (64, 32, 16):
         value = value + roll(value, shift, 1)
     to_west = jnp.where(corner, roll(value, 3, 1), jnp.where(straight, roll(value, -4, 1), roll(value, -2, 1)))
-    to_east = jnp.where(corner, roll(value, -6, 1), jnp.where(straight, roll(value, 3, 1), roll(value, 1, 1)))
+    to_east = jnp.where(corner, roll(value, -5, 1), jnp.where(straight, roll(value, 4, 1), roll(value, 2, 1)))
     rim = jnp.where((lane == 11) | ((lane == 10) & ~corner), to_west, 0.0)
-    rim = jnp.where((lane == 3) | ((lane == 4) & ~corner), to_east, rim)
+    rim = jnp.where((lane == 4) | ((lane == 5) & ~corner), to_east, rim)
     rim = jnp.where((lane == 12) | (lane == 13), roll(first, 12, 1), rim)
-    rim = jnp.where((lane == 1) | (lane == 2), roll(first, 3, 1), rim)
+    rim = jnp.where((lane == 2) | (lane == 3), roll(first, 4, 1), rim)
     return first, second, rim
 
 
@@ -657,6 +663,12 @@
     )
 
 
+def gather_table():
+    cell = np.arange(FC)
+    coarse = cell // 80 // 5 * 16 + cell % 80 // 5
+    return jnp.asarray((coarse[:, None] == np.arange(128)[None, :]).astype(np.float32), BF16)
+
+
 def both_ways(to_next, to_previous, axis):
     size = lax.axis_size(axis)
     ahead = [(i, (i + 1) % size) for i in range(size)]
@@ -703,15 +715,6 @@
     halo = (from_west, from_east, east, west, low, high)
 
     cells = shape(SLOTS, FC)
-    fuel = call(
-        fuel_kernel,
-        "fuel",
-        (cells,) * 6,
-        [SMEM, SMEM, HBM, HBM, HBM, ANY],
-        [pltpu.VMEM((SLOTS, FC), jnp.int32)] * 2 + [pltpu.VMEM((SLOTS, FC), F32), copy_sems(3)],
-        flops=8_000_000,
-        moved=2_800_000,
-    )(fuel_rate, fuel_heat, in_hbm(fuel_cat), in_hbm(front_burn), in_hbm(front_depth), east)
     wind_plan, fire_plan, fire_sends, alive, home_plan, strip_plan = call(
         plan_kernel,
         "plan",
@@ -728,48 +731,69 @@
         moved=400_000,
         mib=8,
     )(tiles)
+    inner = call(
+        surface_kernel,
+        "surface",
+        shape(AY, 256),
+        [VMEM] * 3 + [ANY],
+        [main_buffer(3), main_buffer(3)],
+        flops=10_000_000,
+        moved=2_000_000,
+        mib=8,
+    )(surface, low, high, east)
     winds = call(
         wind_kernel,
         "wind",
         shape(DEVICES * 8, 128),
-        [VMEM] * 9 + [ANY],
-        [main_buffer(3), main_buffer(3), rim_buffer(1), rim_buffer(1), rim_buffer(1)],
+        [VMEM] * 7,
+        [rim_buffer(1), rim_buffer(1)],
         flops=10_000_000,
         moved=2_000_000,
         mib=8,
-    )(surface, blocks, *halo, wind_plan, fuel[0])
+    )(inner, blocks, from_west, from_east, east, west, wind_plan)
     got_winds = exchange(winds)
 
-    main, rim = call(
+    main, rim, *fuel = call(
         step_kernel,
         "step",
-        (hbm(3, LEV, ROWS, 128), shape(3, 2, ROWS, 128)),
-        [HBM] + [VMEM] * 6,
+        (hbm(3, LEV, ROWS, 128), shape(3, 2, ROWS, 128)) + (cells,) * 6,
+        [HBM] + [VMEM] * 8 + [HBM] * 3,
         [main_buffer(LEV), main_buffer(LEV), rim_buffer(2), rim_buffer(2)]
-        + [pltpu.VMEM((3, LEV, AY, 128), F32), copy_sems(8)],
-        (HBM, VMEM),
+        + [pltpu.VMEM((3, LEV, AY, 128), F32)]
+        + [pltpu.VMEM((SLOTS, FC), jnp.int32)] * 2
+        + [pltpu.VMEM((SLOTS, FC), F32), copy_sems(11)],
+        (HBM,) + (VMEM,) * 7,
         flops=40_000_000,
         moved=8_000_000,
         mib=12,
-    )(atmos, *halo)
+    )(
+        atmos,
+        *halo,
+        fuel_rate.reshape(1, -1),
+        fuel_heat.reshape(1, -1),
+        in_hbm(fuel_cat),
+        in_hbm(front_burn),
+        in_hbm(front_depth),
+    )
 
     heats, fire_level = call(
         fire_kernel,
         "fire",
         (hbm(DEVICES * 6, 128), hbm(SLOTS, FC)),
-        [VMEM] * 10 + [ANY],
+        [VMEM] * 10 + [HBM, ANY],
         [
             pltpu.VMEM((4 * SLOTS, FC), F32),
             pltpu.VMEM((2 * SLOTS, FC), F32),
             pltpu.VMEM((128, FC), BF16),
+            pltpu.VMEM((FC, 128), BF16),
             pltpu.VMEM((DEVICES * 6, 128), F32),
             pltpu.VMEM((SLOTS, FC), F32),
-            copy_sems(2),
+            copy_sems(3),
         ],
         (HBM, HBM),
         flops=40_000_000,
         moved=4_000_000,
-    )(got_winds, fire_plan, fire_sends, alive, *fuel, rim)
+    )(got_winds, fire_plan, fire_sends, alive, *fuel, in_hbm(gather_table()), rim)
     got_heats = exchange(heats)
 
     upper, kept, bottom = call(

time: 64 us -> 63.4 us (level)
  Pallas kernels: 23.8 us -> 21.9 us
  waiting for transfers between devices: 21 us -> 22.5 us
    pallas_call x2, Pallas kernels: 4.42 us -> 1.97 us  [the longest x1 1.7 us: on_device(): call(wind_kernel, 'wind', shape(DEVICES * 8, 128), [VMEM] * 7, [rim_buffe...]
    ppermute x2, waiting for transfers between devices: 3.54 us -> 5.12 us  [both_ways(): lax.ppermute(to_next, axis, ahead)]
    all_to_all x2, waiting for transfers between devices: 15.5 us -> 14.8 us  [exchange(): lax.all_to_all(x.reshape(-1), AXES, 0, 0, tiled=True).reshape(x.shape)]
    pallas_call x1, Pallas kernels: 5.93 us -> 6.57 us  [on_device(): call(step_kernel, 'step', (hbm(3, LEV, ROWS, 128), shape(3, 2, ROWS, 128)...]
  transfers between devices with their start and end apart: 6 -> 6, of which waited for: 4 -> 5; matrix products, arithmetic and copies ran while one was open for 0% -> 0% of each run, Pallas kernels for 25% -> 23%
where the time goes in v4:
time: 63.4 us; the launch traced here: 63.1 us
  waiting for transfers between devices  22.5 us (35%)
  Pallas kernels  21.9 us (35%)
  starting transfers between devices  17.6 us (28%)
  between operations  0.9 us (1%)
    all_to_all x2, waiting for transfers between devices, exchange(): lax.all_to_all(x.reshape(-1), AXES, 0, 0, tiled=True).reshape(x.shape)  14.8 us
    all_to_all x2, starting transfers between devices, exchange(): lax.all_to_all(x.reshape(-1), AXES, 0, 0, tiled=True).reshape(x.shape)  9.61 us
    pallas_call x1, Pallas kernels, on_device(): call(step_kernel, 'step', (hbm(3, LEV, ROWS, 128), shape(3, 2, ROWS, 128)...  6.57 us
    pallas_call x1, Pallas kernels, on_device(): call(upper_kernel, 'upper', (hbm(3, LEV, AY, 128), shape(3, 2, ROWS, 128)...  5.25 us
    ppermute x2, waiting for transfers between devices, both_ways(): lax.ppermute(to_next, axis, ahead)  5.12 us
    ppermute x2, starting transfers between devices, both_ways(): lax.ppermute(to_previous, axis, [(j, i) for i, j in ahead])  4.96 us
    ppermute x2, starting transfers between devices, both_ways(): lax.ppermute(to_next, axis, ahead)  3.04 us
    pallas_call x1, Pallas kernels, on_device(): call(fire_kernel, 'fire', (hbm(DEVICES * 6, 128), hbm(SLOTS, FC)), [VMEM]...  2.63 us
  transfers between devices with their start and end apart: 6, of which 5 were waited for; matrix products, arithmetic and copies ran while one was open for 0% of the time, Pallas kernels for 23%

profile of v4, /device:TPU:1, one launch (start us, length us, event | category | flops | bytes accessed | tf_op | source)
XLA Modules:
  0.0 63.1 jit_solution(3457126276190551299)
XLA Ops:
  0.6 0.0 copy-start.2
  0.6 1.1 %pack_rows.1 = (f32[24,8,128]{2,1,0:T(8,128)S(1)}, f32[24,8,128]{2,1,0:T(8,128)S(1)}) custom-call(f32[3,16,64,128]{3,2,1,0:T(8,128)} %atmos.5), custom_call_target="tpu_custom_call" | custom-call | tf_op jit(solution)/shard_map/pack_rows/pallas_call | solution.py:703
  1.7 3.0 %collective-permute-start = (f32[24,8,128]{2,1,0:T(8,128)S(1)}, f32[24,8,128]{2,1,0:T(8,128)S(1)}, u32[]{:S(2)}, u32[]{:S(2)}) collective-permute-start(f32[24,8,128]{2,1,0:T(8,128)S(1)} %get-tuple-element.30), channel_id=1, source_target_pairs={{0,16},{16,32},{32,48},{48,64},{64,80},{80,96},{96,112},{112,0},{1... | collective-permute-start | bytes 294920 | tf_op jit(solution)/shard_map/ppermute | solution.py:676
  4.8 0.0 collective-permute-start.1
  4.8 2.0 %pack_columns.1 = (f32[2,64,128]{2,1,0:T(8,128)S(1)}, f32[2,64,128]{2,1,0:T(8,128)S(1)}, f32[3,3,64,128]{3,2,1,0:T(8,128)S(1)}, f32[64,256]{1,0:T(8,128)S(1)}) custom-call(f32[3,16,64,128]{3,2,1,0:T(8,128)} %atmos.5), custom_call_target="tpu_custom_call" | custom-call | flops 4000000 | bytes 1800000 | tf_op jit(solution)/shard_map/pack_columns/pallas_call | solution.py:706
  6.8 0.0 collective-permute-done.low
  6.8 2.0 %collective-permute-done.1.high = f32[24,8,128]{2,1,0:T(8,128)S(1)} collective-permute-done((f32[24,8,128]{2,1,0:T(8,128)S(1)}, f32[24,8,128]{2,1,0:T(8,128)S(1)}, u32[]{:S(2)}, u32[]{:S(2)}) %collective-permute-start.1) | collective-permute-done | bytes 98336 | tf_op jit(solution)/shard_map/ppermute | solution.py:677
  8.8 0.0 copy-start
  8.8 0.0 copy-start.1
  8.8 0.2 join_columns.1
  9.0 5.0 %collective-permute-start.3 = (f32[2,72,128]{2,1,0:T(8,128)S(1)}, f32[2,72,128]{2,1,0:T(8,128)S(1)}, u32[]{:S(2)}, u32[]{:S(2)}) collective-permute-start(f32[2,72,128]{2,1,0:T(8,128)S(1)} %get-tuple-element.36.west), channel_id=1, source_target_pairs={{1,0},{2,1},{3,2},{4,3},{5,4},{6,5},{7,6},{8,7},{9,8},{10,9},{11,1... | collective-permute-start | bytes 221192 | tf_op jit(solution)/shard_map/ppermute | solution.py:677
  14.0 0.0 collective-permute-start.2
  14.0 0.0 copy-done.2
  14.0 0.1 reshape.29
  14.1 0.1 copy.12
  14.1 0.3 plan.1
  14.5 0.3 surface.1.inner
  14.7 0.6 %collective-permute-done.3.from_east = f32[2,72,128]{2,1,0:T(8,128)S(1)} collective-permute-done((f32[2,72,128]{2,1,0:T(8,128)S(1)}, f32[2,72,128]{2,1,0:T(8,128)S(1)}, u32[]{:S(2)}, u32[]{:S(2)}) %collective-permute-start.3) | collective-permute-done | bytes 73760 | tf_op jit(solution)/shard_map/ppermute | solution.py:677
  15.4 5.1 %collective-permute-done.2.from_west = f32[2,72,128]{2,1,0:T(8,128)S(1)} collective-permute-done((f32[2,72,128]{2,1,0:T(8,128)S(1)}, f32[2,72,128]{2,1,0:T(8,128)S(1)}, u32[]{:S(2)}, u32[]{:S(2)}) %collective-permute-start.2) | collective-permute-done | bytes 73760 | tf_op jit(solution)/shard_map/ppermute | solution.py:676
  20.5 1.7 %wind.1 = f32[1024,128]{1,0:T(8,128)} custom-call(f32[64,256]{1,0:T(8,128)S(1)} %surface.1.inner, f32[64,256]{1,0:T(8,128)S(1)} %get-tuple-element.35.blocks, f32[2,72,128]{2,1,0:T(8,128)S(1)} %collective-permute-done.2.from_west, f32[2,72,128]{2,1,0:T(8,128)S(1)} %collective-permute-done.3.from_east, f32[2,72,128]{2,1,0:T(8,128)S(1)} %get-tuple-element.34.after.east, ...), custom_call_target="tpu_custom_call" | custom-call | flops 10000000 | bytes 2000000 | tf_op jit(solution)/shard_map/wind/pallas_call | solution.py:744
  22.2 5.4 %all-to-all-start = ((f32[128,1024,1]{1,2,0:T(1,128)}), f32[128,1024,1]{1,2,0:T(1,128)S(1)}, u32[]{:S(2)}, u32[]{:S(2)}) async-start(f32[128,1024,1]{1,2,0:T(1,128)} %bitcast.1), calls=%async_computation | async-start | bytes 1048576 | tf_op jit(solution)/shard_map/all_to_all | solution.py:682
  27.6 0.0 copy-done
  27.6 0.0 copy-done.1
  27.6 6.6 %step.1 = (f32[3,16,88,128]{3,2,1,0:T(8,128)}, f32[3,2,88,128]{3,2,1,0:T(8,128)S(1)}, f32[24,3200]{1,0:T(8,128)S(1)}, f32[24,3200]{1,0:T(8,128)S(1)}, f32[24,320...) custom-call(f32[3,16,64,128]{3,2,1,0:T(8,128)} %atmos.5, ...), custom_call_target="tpu_custom_call" | custom-call | flops 40000000 | bytes 8000000 | tf_op jit(solution)/shard_map/step/pallas_call | solution.py:756
  34.2 7.3 %all-to-all-done = f32[128,1024,1]{1,2,0:T(1,128)S(1)} async-done(((f32[128,1024,1]{1,2,0:T(1,128)}), f32[128,1024,1]{1,2,0:T(1,128)S(1)}, u32[]{:S(2)}, u32[]{:S(2)}) %all-to-all-start) | async-done | bytes 524320 | tf_op jit(solution)/shard_map/all_to_all | solution.py:682
  41.5 2.6 %fire.1 = (f32[768,128]{1,0:T(8,128)}, f32[24,3200]{1,0:T(8,128)}) custom-call(f32[1024,128]{1,0:T(8,128)S(1)} %bitcast.7, bf16[32,256]{1,0:T(8,128)(2,1)S(1)} %get-tuple-element.38.plan, bf16[256,128]{1,0:T(8,128)(2,1)S(1)} %get-tuple-element.39.sends, f32[32,128]{1,0:T(8,128)S(1)} %get-tuple-element.40.live, f32[24,3200]{1,0:T(8,128)S(1)} %get-tuple-element.41.rate, ...), custom_call_target="tpu_custom_call" | custom-call | flops 40000000 | bytes 4000000 | tf_op jit(solution)/shard_map/fire/pallas_call | solution.py:779
  44.2 4.2 %all-to-all-start.1 = ((f32[128,768,1]{1,2,0:T(1,128)}), f32[128,768,1]{1,2,0:T(1,128)S(1)}, u32[]{:S(2)}, u32[]{:S(2)}) async-start(f32[128,768,1]{1,2,0:T(1,128)} %bitcast.11), calls=%async_computation.1 | async-start | bytes 786432 | tf_op jit(solution)/shard_map/all_to_all | solution.py:682
  48.4 5.2 %upper.1 = (f32[3,16,64,128]{3,2,1,0:T(8,128)}, f32[3,2,88,128]{3,2,1,0:T(8,128)S(1)}, f32[3,3,88,128]{3,2,1,0:T(8,128)S(1)}) custom-call(f32[3,16,88,128]{3,2,1,0:T(8,128)} %get-tuple-element.51.main_in, f32[3,2,88,128]{3,2,1,0:T(8,128)S(1)} %get-tuple-element.47.rim.rim_in, f32[24,3200]{1,0:T(8,128)} %get-tuple-element.28.fire_level), custom_call_target="tpu_custom_call" | custom-call | flops 40000000 | bytes 8000000 | tf_op jit(solution)/shard_map/upper/pallas_call | solution.py:799
  53.6 7.4 %all-to-all-done.1 = f32[128,768,1]{1,2,0:T(1,128)S(1)} async-done(((f32[128,768,1]{1,2,0:T(1,128)}), f32[128,768,1]{1,2,0:T(1,128)S(1)}, u32[]{:S(2)}, u32[]{:S(2)}) %all-to-all-start.1) | async-done | bytes 393248 | tf_op jit(solution)/shard_map/all_to_all | solution.py:682
  61.1 1.8 %lower.1 = f32[3,16,64,128]{3,2,1,0:T(8,128)} custom-call(f32[768,128]{1,0:T(8,128)S(1)} %bitcast.8, bf16[64,256]{1,0:T(8,128)(2,1)S(1)} %get-tuple-element.49.home_plan, bf16[176,256]{1,0:T(8,128)(2,1)S(1)} %get-tuple-element.50.strip_plan, f32[3,3,88,128]{3,2,1,0:T(8,128)S(1)} %get-tuple-element.53.main_in, ...), custom_call_target="tpu_custom_call", output_to_operand_aliasing={{}: (6, {})} | custom-call | flops 10000000 | bytes 2000000 | tf_op jit(solution)/shard_map/lower/pallas_call | solution.py:811
  (1 shorter events, 0.0 us)
Async XLA Ops:
  0.6 13.3 %copy-start.2 = (s32[3072]{0:T(1024)S(1)}, s32[3072]{0:T(1024)}, u32[]{:S(2)}) copy-start(s32[3072]{0:T(1024)} %param.9) | copy-start | bytes 36868
  1.7 5.1 %collective-permute-start = (f32[24,8,128]{2,1,0:T(8,128)S(1)}, f32[24,8,128]{2,1,0:T(8,128)S(1)}, u32[]{:S(2)}, u32[]{:S(2)}) collective-permute-start(f32[24,8,128]{2,1,0:T(8,128)S(1)} %get-tuple-element.30), channel_id=1, source_target_pairs={{0,16},{16,32},{32,48},{48,64},{64,80},{80,96},{96,112},{112,0},{1... | collective-permute-start | bytes 294920 | tf_op jit(solution)/shard_map/ppermute | solution.py:676
  4.8 4.0 %collective-permute-start.1 = (f32[24,8,128]{2,1,0:T(8,128)S(1)}, f32[24,8,128]{2,1,0:T(8,128)S(1)}, u32[]{:S(2)}, u32[]{:S(2)}) collective-permute-start(f32[24,8,128]{2,1,0:T(8,128)S(1)} %get-tuple-element.31), channel_id=1, source_target_pairs={{16,0},{32,16},{48,32},{64,48},{80,64},{96,80},{112,96},{0,112},{1... | collective-permute-start | bytes 294920 | tf_op jit(solution)/shard_map/ppermute | solution.py:677
  8.8 18.8 %copy-start = (f32[13]{0:T(128)S(1)}, f32[13]{0:T(128)}, u32[]{:S(2)}) copy-start(f32[13]{0:T(128)} %param.13) | copy-start | bytes 160
  8.8 18.8 %copy-start.1 = (f32[13]{0:T(128)S(1)}, f32[13]{0:T(128)}, u32[]{:S(2)}) copy-start(f32[13]{0:T(128)} %param.14) | copy-start | bytes 160
  9.0 6.4 %collective-permute-start.3 = (f32[2,72,128]{2,1,0:T(8,128)S(1)}, f32[2,72,128]{2,1,0:T(8,128)S(1)}, u32[]{:S(2)}, u32[]{:S(2)}) collective-permute-start(f32[2,72,128]{2,1,0:T(8,128)S(1)} %get-tuple-element.36.west), channel_id=1, source_target_pairs={{1,0},{2,1},{3,2},{4,3},{5,4},{6,5},{7,6},{8,7},{9,8},{10,9},{11,1... | collective-permute-start | bytes 221192 | tf_op jit(solution)/shard_map/ppermute | solution.py:677
  14.0 6.5 %collective-permute-start.2 = (f32[2,72,128]{2,1,0:T(8,128)S(1)}, f32[2,72,128]{2,1,0:T(8,128)S(1)}, u32[]{:S(2)}, u32[]{:S(2)}) collective-permute-start(f32[2,72,128]{2,1,0:T(8,128)S(1)} %get-tuple-element.34.after.east), channel_id=1, source_target_pairs={{0,1},{1,2},{2,3},{3,4},{4,5},{5,6},{6,7},{7,8},{8,9},{9,10},{10,1... | collective-permute-start | bytes 221192 | tf_op jit(solution)/shard_map/ppermute | solution.py:676
  22.2 19.3 %all-to-all-start = ((f32[128,1024,1]{1,2,0:T(1,128)}), f32[128,1024,1]{1,2,0:T(1,128)S(1)}, u32[]{:S(2)}, u32[]{:S(2)}) async-start(f32[128,1024,1]{1,2,0:T(1,128)} %bitcast.1), calls=%async_computation | async-start | bytes 1048576 | tf_op jit(solution)/shard_map/all_to_all | solution.py:682
  44.2 16.9 %all-to-all-start.1 = ((f32[128,768,1]{1,2,0:T(1,128)}), f32[128,768,1]{1,2,0:T(1,128)S(1)}, u32[]{:S(2)}, u32[]{:S(2)}) async-start(f32[128,768,1]{1,2,0:T(1,128)} %bitcast.11), calls=%async_computation.1 | async-start | bytes 786432 | tf_op jit(solution)/shard_map/all_to_all | solution.py:682

commit v5 on v4

--- a/solution.py
+++ b/solution.py
@@ -6,7 +6,7 @@
 from jax.experimental.pallas import tpu as pltpu
 from jax.sharding import PartitionSpec as P
 
-AXES = ("ty", "tx")
+AXES = ("tx", "ty")
 NTY, NTX, DEVICES = 8, 16, 128
 LEV, AY, AX = 16, 64, 128
 SLOTS, FC = 24, 3200
@@ -22,7 +22,7 @@
 
 def place():
     ty, tx = lax.axis_index("ty"), lax.axis_index("tx")
-    return ty * NTX + tx, ty, tx
+    return tx * NTY + ty, ty, tx
 
 
 def iota(shape, dim):
@@ -65,7 +65,7 @@
 
 def slot_facts(tile):
     row, col = tile >> 7, tile & 127
-    owner = (row >> 3) * NTX + (col >> 3)
+    owner = (col >> 3) * NTY + (row >> 3)
     local = (row & 7) * 8 + (col & 7)
     live = tile >= 0
     return jnp.where(live, owner, -1), local + 1, live
@@ -308,7 +308,7 @@
 
     def numbers(dy, dx):
         ok = (ty + dy >= 0) & (ty + dy < NTY) & (tx + dx >= 0) & (tx + dx < NTX)
-        return slots_of(owner, local, jnp.where(ok, me + dy * NTX + dx, -7))
+        return slots_of(owner, local, jnp.where(ok, me + dx * NTY + dy, -7))
 
     here = numbers(0, 0)
     north, south, west, east = numbers(1, 0), numbers(-1, 0), numbers(0, -1), numbers(0, 1)
@@ -506,19 +506,17 @@
         first = blocks[j * 128 : (j + 1) * 128, 0:128]
         sent[pl.ds(j, 128, stride=6), :] = first
         sent[pl.ds(2 + j, 128, stride=6), :] = blocks[j * 128 : (j + 1) * 128, 128:256]
-        north, south = roll(first, -16, 0), roll(first, 16, 0)
-        west, east = roll(first, 1, 0), roll(first, -1, 0)
-        west_corner, east_corner = roll(west, 41, 1), roll(east, 57, 1)
+        north, south = roll(first, -1, 0), roll(first, 1, 0)
+        west, east = roll(first, NTY, 0), roll(first, -NTY, 0)
+        corners = jnp.where((lane == 40) | (lane == 56), roll(west, 41, 1), roll(east, 57, 1))
         strip = jnp.where(group < 2, north, jnp.where(group >= 6, south, 0.0))
         middle_rows = (group >= 2) & (group < 6)
         strip = jnp.where(middle_rows & (spot >= 14), west, strip)
         strip = jnp.where(middle_rows & ((spot == 12) | (spot == 13)), roll(west, 62, 1), strip)
         strip = jnp.where(middle_rows & (spot < 2), east, strip)
         strip = jnp.where(middle_rows & ((spot == 2) | (spot == 3)), roll(east, 66, 1), strip)
-        strip = jnp.where(lane == 40, roll(west_corner, 16, 0), strip)
-        strip = jnp.where(lane == 41, roll(east_corner, 16, 0), strip)
-        strip = jnp.where(lane == 56, roll(west_corner, -16, 0), strip)
-        strip = jnp.where(lane == 57, roll(east_corner, -16, 0), strip)
+        strip = jnp.where((lane == 40) | (lane == 41), roll(corners, 1, 0), strip)
+        strip = jnp.where((lane == 56) | (lane == 57), roll(corners, -1, 0), strip)
         sent[pl.ds(4 + j, 128, stride=6), :] = strip
     copy = pltpu.make_async_copy(sent, out, sems.at[1])
     copy.start()
@@ -695,7 +693,8 @@
 
 
 def on_device(atmos, slot_tile, fuel_cat, front_burn, front_depth, fuel_rate, fuel_heat):
-    tiles = jnp.pad(slot_tile.reshape(DEVICES, SLOTS).T, ((0, 8), (0, 0)), constant_values=-1)
+    tiles = slot_tile.reshape(NTY, NTX, SLOTS).transpose(2, 1, 0).reshape(SLOTS, DEVICES)
+    tiles = jnp.pad(tiles, ((0, 8), (0, 0)), constant_values=-1)
     atmos = in_hbm(atmos)
 
     rows = shape(24, 8, 128)
@@ -740,7 +739,7 @@
         flops=10_000_000,
         moved=2_000_000,
         mib=8,
-    )(surface, low, high, east)
+    )(surface, low, high, west)
     winds = call(
         wind_kernel,
         "wind",

time: 63.4 us -> 62.9 us (level)
  waiting for transfers between devices: 22.5 us -> 17.5 us
  starting transfers between devices: 17.6 us -> 22 us
    all_to_all x2, starting transfers between devices: 9.61 us -> 13.9 us  [exchange(): lax.all_to_all(x.reshape(-1), AXES, 0, 0, tiled=True).reshape(x.shape)]
    ppermute x2, waiting for transfers between devices: 5.12 us -> 1.48 us  [both_ways(): lax.ppermute(to_next, axis, ahead)]
    ppermute x2, starting transfers between devices: 3.04 us -> 4.32 us  [both_ways(): lax.ppermute(to_next, axis, ahead)]
    ppermute x2, starting transfers between devices: 4.96 us -> 3.8 us  [both_ways(): lax.ppermute(to_previous, axis, [(j, i) for i, j in ahead])]
    all_to_all x2, waiting for transfers between devices: 14.8 us -> 14 us  [exchange(): lax.all_to_all(x.reshape(-1), AXES, 0, 0, tiled=True).reshape(x.shape)]
  transfers between devices with their start and end apart: 6 -> 6, of which waited for: 5 -> 4; matrix products, arithmetic and copies ran while one was open for 0% -> 0% of each run, Pallas kernels for 23% -> 23%
where the time goes in v5:
time: 62.9 us; the launch traced here: 62.5 us
  starting transfers between devices  22 us (35%)
  Pallas kernels  21.9 us (35%)
  waiting for transfers between devices  17.5 us (28%)
  between operations  0.92 us (1%)
    all_to_all x2, waiting for transfers between devices, exchange(): lax.all_to_all(x.reshape(-1), AXES, 0, 0, tiled=True).reshape(x.shape)  14 us
    all_to_all x2, starting transfers between devices, exchange(): lax.all_to_all(x.reshape(-1), AXES, 0, 0, tiled=True).reshape(x.shape)  13.9 us
    pallas_call x1, Pallas kernels, on_device(): call(step_kernel, 'step', (hbm(3, LEV, ROWS, 128), shape(3, 2, ROWS, 128)...  6.57 us
    pallas_call x1, Pallas kernels, on_device(): call(upper_kernel, 'upper', (hbm(3, LEV, AY, 128), shape(3, 2, ROWS, 128)...  5.25 us
    ppermute x2, starting transfers between devices, both_ways(): lax.ppermute(to_next, axis, ahead)  4.32 us
    ppermute x2, starting transfers between devices, both_ways(): lax.ppermute(to_previous, axis, [(j, i) for i, j in ahead])  3.8 us
    pallas_call x1, Pallas kernels, on_device(): call(fire_kernel, 'fire', (hbm(DEVICES * 6, 128), hbm(SLOTS, FC)), [VMEM]...  2.63 us
    pallas_call x1, Pallas kernels, on_device(): call(pack_columns, 'pack_columns', (body, body, shape(3, 3, AY, 128), sha...  2.04 us
  transfers between devices with their start and end apart: 6, of which 4 were waited for; matrix products, arithmetic and copies ran while one was open for 0% of the time, Pallas kernels for 23%

profile of v5, /device:TPU:1, one launch (start us, length us, event | category | flops | bytes accessed | tf_op | source)
XLA Modules:
  0.0 62.5 jit_solution(15645580605984810045)
XLA Ops:
  0.6 0.0 copy-start.2
  0.6 1.1 %pack_rows.1 = (f32[24,8,128]{2,1,0:T(8,128)S(1)}, f32[24,8,128]{2,1,0:T(8,128)S(1)}) custom-call(f32[3,16,64,128]{3,2,1,0:T(8,128)} %atmos.5), custom_call_target="tpu_custom_call" | custom-call | tf_op jit(solution)/shard_map/pack_rows/pallas_call | solution.py:702
  1.7 3.0 %collective-permute-start = (f32[24,8,128]{2,1,0:T(8,128)S(1)}, f32[24,8,128]{2,1,0:T(8,128)S(1)}, u32[]{:S(2)}, u32[]{:S(2)}) collective-permute-start(f32[24,8,128]{2,1,0:T(8,128)S(1)} %get-tuple-element.30), channel_id=1, source_target_pairs={{0,16},{16,32},{32,48},{48,64},{64,80},{80,96},{96,112},{112,0},{1... | collective-permute-start | bytes 294920 | tf_op jit(solution)/shard_map/ppermute | solution.py:674
  4.8 0.0 collective-permute-start.1
  4.8 2.0 %pack_columns.1 = (f32[2,64,128]{2,1,0:T(8,128)S(1)}, f32[2,64,128]{2,1,0:T(8,128)S(1)}, f32[3,3,64,128]{3,2,1,0:T(8,128)S(1)}, f32[64,256]{1,0:T(8,128)S(1)}) custom-call(f32[3,16,64,128]{3,2,1,0:T(8,128)} %atmos.5), custom_call_target="tpu_custom_call" | custom-call | flops 4000000 | bytes 1800000 | tf_op jit(solution)/shard_map/pack_columns/pallas_call | solution.py:705
  6.8 0.0 collective-permute-done.low
  6.8 2.0 %collective-permute-done.1.high = f32[24,8,128]{2,1,0:T(8,128)S(1)} collective-permute-done((f32[24,8,128]{2,1,0:T(8,128)S(1)}, f32[24,8,128]{2,1,0:T(8,128)S(1)}, u32[]{:S(2)}, u32[]{:S(2)}) %collective-permute-start.1) | collective-permute-done | bytes 98336 | tf_op jit(solution)/shard_map/ppermute | solution.py:675
  8.8 0.2 join_columns.1
  9.0 0.0 copy-start
  9.0 0.0 copy-start.1
  9.0 1.3 %collective-permute-start.2 = (f32[2,72,128]{2,1,0:T(8,128)S(1)}, f32[2,72,128]{2,1,0:T(8,128)S(1)}, u32[]{:S(2)}, u32[]{:S(2)}) collective-permute-start(f32[2,72,128]{2,1,0:T(8,128)S(1)} %get-tuple-element.36.east), channel_id=1, source_target_pairs={{0,1},{1,2},{2,3},{3,4},{4,5},{5,6},{6,7},{7,8},{8,9},{9,10},{10,1... | collective-permute-start | bytes 221192 | tf_op jit(solution)/shard_map/ppermute | solution.py:674
  10.3 3.8 %collective-permute-start.3 = (f32[2,72,128]{2,1,0:T(8,128)S(1)}, f32[2,72,128]{2,1,0:T(8,128)S(1)}, u32[]{:S(2)}, u32[]{:S(2)}) collective-permute-start(f32[2,72,128]{2,1,0:T(8,128)S(1)} %get-tuple-element.34.after.west), channel_id=1, source_target_pairs={{1,0},{2,1},{3,2},{4,3},{5,4},{6,5},{7,6},{8,7},{9,8},{10,9},{11,1... | collective-permute-start | bytes 221192 | tf_op jit(solution)/shard_map/ppermute | solution.py:675
  14.1 0.0 copy-done.2
  14.1 0.1 reshape.32
  14.2 0.1 copy.14
  14.3 0.3 plan.1
  14.6 0.3 surface.1.inner
  14.9 1.5 %collective-permute-done.2.from_west = f32[2,72,128]{2,1,0:T(8,128)S(1)} collective-permute-done((f32[2,72,128]{2,1,0:T(8,128)S(1)}, f32[2,72,128]{2,1,0:T(8,128)S(1)}, u32[]{:S(2)}, u32[]{:S(2)}) %collective-permute-start.2) | collective-permute-done | bytes 73760 | tf_op jit(solution)/shard_map/ppermute | solution.py:674
  16.4 0.0 collective-permute-done.3.from_east
  16.4 1.7 %wind.1 = f32[1024,128]{1,0:T(8,128)} custom-call(f32[64,256]{1,0:T(8,128)S(1)} %surface.1.inner, f32[64,256]{1,0:T(8,128)S(1)} %get-tuple-element.35.blocks, f32[2,72,128]{2,1,0:T(8,128)S(1)} %collective-permute-done.2.from_west, f32[2,72,128]{2,1,0:T(8,128)S(1)} %collective-permute-done.3.from_east, f32[2,72,128]{2,1,0:T(8,128)S(1)} %get-tuple-element.36.east, ...), custom_call_target="tpu_custom_call" | custom-call | flops 10000000 | bytes 2000000 | tf_op jit(solution)/shard_map/wind/pallas_call | solution.py:743
  18.1 9.3 %all-to-all-start = ((f32[128,1024,1]{1,2,0:T(1,128)}), f32[128,1024,1]{1,2,0:T(1,128)S(1)}, u32[]{:S(2)}, u32[]{:S(2)}) async-start(f32[128,1024,1]{1,2,0:T(1,128)} %bitcast.2), calls=%async_computation | async-start | bytes 1048576 | tf_op jit(solution)/shard_map/all_to_all | solution.py:680
  27.4 0.0 copy-done
  27.4 0.0 copy-done.1
  27.4 6.6 %step.1 = (f32[3,16,88,128]{3,2,1,0:T(8,128)}, f32[3,2,88,128]{3,2,1,0:T(8,128)S(1)}, f32[24,3200]{1,0:T(8,128)S(1)}, f32[24,3200]{1,0:T(8,128)S(1)}, f32[24,320...) custom-call(f32[3,16,64,128]{3,2,1,0:T(8,128)} %atmos.5, ...), custom_call_target="tpu_custom_call" | custom-call | flops 40000000 | bytes 8000000 | tf_op jit(solution)/shard_map/step/pallas_call | solution.py:755
  34.0 7.0 %all-to-all-done = f32[128,1024,1]{1,2,0:T(1,128)S(1)} async-done(((f32[128,1024,1]{1,2,0:T(1,128)}), f32[128,1024,1]{1,2,0:T(1,128)S(1)}, u32[]{:S(2)}, u32[]{:S(2)}) %all-to-all-start) | async-done | bytes 524320 | tf_op jit(solution)/shard_map/all_to_all | solution.py:680
  41.0 2.6 %fire.1 = (f32[768,128]{1,0:T(8,128)}, f32[24,3200]{1,0:T(8,128)}) custom-call(f32[1024,128]{1,0:T(8,128)S(1)} %bitcast.10, bf16[32,256]{1,0:T(8,128)(2,1)S(1)} %get-tuple-element.38.plan, bf16[256,128]{1,0:T(8,128)(2,1)S(1)} %get-tuple-element.39.sends, f32[32,128]{1,0:T(8,128)S(1)} %get-tuple-element.40.live, f32[24,3200]{1,0:T(8,128)S(1)} %get-tuple-element.41.rate, ...), custom_call_target="tpu_custom_call" | custom-call | flops 40000000 | bytes 4000000 | tf_op jit(solution)/shard_map/fire/pallas_call | solution.py:778
  43.6 4.6 %all-to-all-start.1 = ((f32[128,768,1]{1,2,0:T(1,128)}), f32[128,768,1]{1,2,0:T(1,128)S(1)}, u32[]{:S(2)}, u32[]{:S(2)}) async-start(f32[128,768,1]{1,2,0:T(1,128)} %bitcast.14), calls=%async_computation.1 | async-start | bytes 786432 | tf_op jit(solution)/shard_map/all_to_all | solution.py:680
  48.2 5.2 %upper.1 = (f32[3,16,64,128]{3,2,1,0:T(8,128)}, f32[3,2,88,128]{3,2,1,0:T(8,128)S(1)}, f32[3,3,88,128]{3,2,1,0:T(8,128)S(1)}) custom-call(f32[3,16,88,128]{3,2,1,0:T(8,128)} %get-tuple-element.51.main_in, f32[3,2,88,128]{3,2,1,0:T(8,128)S(1)} %get-tuple-element.47.rim.rim_in, f32[24,3200]{1,0:T(8,128)} %get-tuple-element.28.fire_level), custom_call_target="tpu_custom_call" | custom-call | flops 40000000 | bytes 8000000 | tf_op jit(solution)/shard_map/upper/pallas_call | solution.py:798
  53.5 7.1 %all-to-all-done.1 = f32[128,768,1]{1,2,0:T(1,128)S(1)} async-done(((f32[128,768,1]{1,2,0:T(1,128)}), f32[128,768,1]{1,2,0:T(1,128)S(1)}, u32[]{:S(2)}, u32[]{:S(2)}) %all-to-all-start.1) | async-done | bytes 393248 | tf_op jit(solution)/shard_map/all_to_all | solution.py:680
  60.5 1.8 %lower.1 = f32[3,16,64,128]{3,2,1,0:T(8,128)} custom-call(f32[768,128]{1,0:T(8,128)S(1)} %bitcast.11, bf16[64,256]{1,0:T(8,128)(2,1)S(1)} %get-tuple-element.49.home_plan, bf16[176,256]{1,0:T(8,128)(2,1)S(1)} %get-tuple-element.50.strip_plan, f32[3,3,88,128]{3,2,1,0:T(8,128)S(1)} %get-tuple-element.53.main_in, ...), custom_call_target="tpu_custom_call", output_to_operand_aliasing={{}: (6, {})} | custom-call | flops 10000000 | bytes 2000000 | tf_op jit(solution)/shard_map/lower/pallas_call | solution.py:810
  (2 shorter events, 0.0 us)
Async XLA Ops:
  0.6 13.5 %copy-start.2 = (s32[3072]{0:T(1024)S(1)}, s32[3072]{0:T(1024)}, u32[]{:S(2)}) copy-start(s32[3072]{0:T(1024)} %param.9) | copy-start | bytes 36868
  1.7 5.1 %collective-permute-start = (f32[24,8,128]{2,1,0:T(8,128)S(1)}, f32[24,8,128]{2,1,0:T(8,128)S(1)}, u32[]{:S(2)}, u32[]{:S(2)}) collective-permute-start(f32[24,8,128]{2,1,0:T(8,128)S(1)} %get-tuple-element.30), channel_id=1, source_target_pairs={{0,16},{16,32},{32,48},{48,64},{64,80},{80,96},{96,112},{112,0},{1... | collective-permute-start | bytes 294920 | tf_op jit(solution)/shard_map/ppermute | solution.py:674
  4.8 4.0 %collective-permute-start.1 = (f32[24,8,128]{2,1,0:T(8,128)S(1)}, f32[24,8,128]{2,1,0:T(8,128)S(1)}, u32[]{:S(2)}, u32[]{:S(2)}) collective-permute-start(f32[24,8,128]{2,1,0:T(8,128)S(1)} %get-tuple-element.31), channel_id=1, source_target_pairs={{16,0},{32,16},{48,32},{64,48},{80,64},{96,80},{112,96},{0,112},{1... | collective-permute-start | bytes 294920 | tf_op jit(solution)/shard_map/ppermute | solution.py:675
  9.0 18.4 %copy-start = (f32[13]{0:T(128)S(1)}, f32[13]{0:T(128)}, u32[]{:S(2)}) copy-start(f32[13]{0:T(128)} %param.13) | copy-start | bytes 160
  9.0 18.4 %copy-start.1 = (f32[13]{0:T(128)S(1)}, f32[13]{0:T(128)}, u32[]{:S(2)}) copy-start(f32[13]{0:T(128)} %param.14) | copy-start | bytes 160
  9.0 7.4 %collective-permute-start.2 = (f32[2,72,128]{2,1,0:T(8,128)S(1)}, f32[2,72,128]{2,1,0:T(8,128)S(1)}, u32[]{:S(2)}, u32[]{:S(2)}) collective-permute-start(f32[2,72,128]{2,1,0:T(8,128)S(1)} %get-tuple-element.36.east), channel_id=1, source_target_pairs={{0,1},{1,2},{2,3},{3,4},{4,5},{5,6},{6,7},{7,8},{8,9},{9,10},{10,1... | collective-permute-start | bytes 221192 | tf_op jit(solution)/shard_map/ppermute | solution.py:674
  10.3 6.1 %collective-permute-start.3 = (f32[2,72,128]{2,1,0:T(8,128)S(1)}, f32[2,72,128]{2,1,0:T(8,128)S(1)}, u32[]{:S(2)}, u32[]{:S(2)}) collective-permute-start(f32[2,72,128]{2,1,0:T(8,128)S(1)} %get-tuple-element.34.after.west), channel_id=1, source_target_pairs={{1,0},{2,1},{3,2},{4,3},{5,4},{6,5},{7,6},{8,7},{9,8},{10,9},{11,1... | collective-permute-start | bytes 221192 | tf_op jit(solution)/shard_map/ppermute | solution.py:675
  18.1 22.9 %all-to-all-start = ((f32[128,1024,1]{1,2,0:T(1,128)}), f32[128,1024,1]{1,2,0:T(1,128)S(1)}, u32[]{:S(2)}, u32[]{:S(2)}) async-start(f32[128,1024,1]{1,2,0:T(1,128)} %bitcast.2), calls=%async_computation | async-start | bytes 1048576 | tf_op jit(solution)/shard_map/all_to_all | solution.py:680
  43.6 17.0 %all-to-all-start.1 = ((f32[128,768,1]{1,2,0:T(1,128)}), f32[128,768,1]{1,2,0:T(1,128)S(1)}, u32[]{:S(2)}, u32[]{:S(2)}) async-start(f32[128,768,1]{1,2,0:T(1,128)} %bitcast.14), calls=%async_computation.1 | async-start | bytes 786432 | tf_op jit(solution)/shard_map/all_to_all | solution.py:680

commit v6 on v5

--- a/solution.py
+++ b/solution.py
@@ -121,7 +121,7 @@
     return to_east, to_west
 
 
-def pack_columns(atmos, east, west, surface, blocks, planes, sems):
+def pack_columns(atmos, after, east, west, surface, blocks, planes, sems):
     quarters = [
         pltpu.make_async_copy(atmos.at[:, pl.ds(4 * i, 4)], planes.at[:, pl.ds(4 * i, 4)], sems.at[i])
         for i in range(4)
@@ -703,9 +703,9 @@
     low, high = both_ways(up, down, "ty")
     body = shape(2, AY, 128)
     east_rows, west_rows, surface, blocks = call(
-        pack_columns, "pack_columns", (body, body, shape(3, 3, AY, 128), shape(64, 256)), [HBM], [pltpu.VMEM((3, LEV, AY, 128), F32), copy_sems(4)],
+        pack_columns, "pack_columns", (body, body, shape(3, 3, AY, 128), shape(64, 256)), [HBM, ANY], [pltpu.VMEM((3, LEV, AY, 128), F32), copy_sems(4)],
         flops=4_000_000, moved=1_800_000, mib=8,
-    )(atmos)
+    )(atmos, down)
     columns = shape(2, AY + 8, 128)
     east, west = call(join_columns, "join_columns", (columns, columns), [VMEM] * 4, mib=8)(
         east_rows, west_rows, low, high

time: 62.9 us -> 62.9 us (level)
  no operation moved by 1% of the time
where the time goes in v6:
time: 62.9 us; the launch traced here: 62.5 us
  starting transfers between devices  22 us (35%)
  Pallas kernels  21.9 us (35%)
  waiting for transfers between devices  17.5 us (28%)
  between operations  0.92 us (1%)
    all_to_all x2, waiting for transfers between devices, exchange(): lax.all_to_all(x.reshape(-1), AXES, 0, 0, tiled=True).reshape(x.shape)  14 us
    all_to_all x2, starting transfers between devices, exchange(): lax.all_to_all(x.reshape(-1), AXES, 0, 0, tiled=True).reshape(x.shape)  13.9 us
    pallas_call x1, Pallas kernels, on_device(): call(step_kernel, 'step', (hbm(3, LEV, ROWS, 128), shape(3, 2, ROWS, 128)...  6.57 us
    pallas_call x1, Pallas kernels, on_device(): call(upper_kernel, 'upper', (hbm(3, LEV, AY, 128), shape(3, 2, ROWS, 128)...  5.25 us
    ppermute x2, starting transfers between devices, both_ways(): lax.ppermute(to_next, axis, ahead)  4.32 us
    ppermute x2, starting transfers between devices, both_ways(): lax.ppermute(to_previous, axis, [(j, i) for i, j in ahead])  3.8 us
    pallas_call x1, Pallas kernels, on_device(): call(fire_kernel, 'fire', (hbm(DEVICES * 6, 128), hbm(SLOTS, FC)), [VMEM]...  2.63 us
    pallas_call x1, Pallas kernels, on_device(): call(pack_columns, 'pack_columns', (body, body, shape(3, 3, AY, 128), sha...  2.04 us
  transfers between devices with their start and end apart: 6, of which 4 were waited for; matrix products, arithmetic and copies ran while one was open for 0% of the time, Pallas kernels for 23%

profile of v6, /device:TPU:1, one launch (start us, length us, event | category | flops | bytes accessed | tf_op | source)
XLA Modules:
  0.0 62.5 jit_solution(12968716409953019563)
XLA Ops:
  0.6 0.0 copy-start.2
  0.6 1.1 %pack_rows.1 = (f32[24,8,128]{2,1,0:T(8,128)S(1)}, f32[24,8,128]{2,1,0:T(8,128)S(1)}) custom-call(f32[3,16,64,128]{3,2,1,0:T(8,128)} %atmos.5), custom_call_target="tpu_custom_call" | custom-call | tf_op jit(solution)/shard_map/pack_rows/pallas_call | solution.py:702
  1.7 3.0 %collective-permute-start = (f32[24,8,128]{2,1,0:T(8,128)S(1)}, f32[24,8,128]{2,1,0:T(8,128)S(1)}, u32[]{:S(2)}, u32[]{:S(2)}) collective-permute-start(f32[24,8,128]{2,1,0:T(8,128)S(1)} %get-tuple-element.31), channel_id=1, source_target_pairs={{0,16},{16,32},{32,48},{48,64},{64,80},{80,96},{96,112},{112,0},{1... | collective-permute-start | bytes 294920 | tf_op jit(solution)/shard_map/ppermute | solution.py:674
  4.8 0.0 collective-permute-start.1
  4.8 2.0 %pack_columns.1 = (f32[2,64,128]{2,1,0:T(8,128)S(1)}, f32[2,64,128]{2,1,0:T(8,128)S(1)}, f32[3,3,64,128]{3,2,1,0:T(8,128)S(1)}, f32[64,256]{1,0:T(8,128)S(1)}) custom-call(f32[3,16,64,128]{3,2,1,0:T(8,128)} %atmos.5, f32[24,8,128]{2,1,0:T(8,128)S(1)} %get-tuple-element.29.after), custom_call_target="tpu_custom_call" | custom-call | flops 4000000 | bytes 1800000 | tf_op jit(solution)/shard_map/pack_columns/pallas_call | solution.py:705
  6.8 0.0 collective-permute-done.low
  6.8 2.0 %collective-permute-done.1.high = f32[24,8,128]{2,1,0:T(8,128)S(1)} collective-permute-done((f32[24,8,128]{2,1,0:T(8,128)S(1)}, f32[24,8,128]{2,1,0:T(8,128)S(1)}, u32[]{:S(2)}, u32[]{:S(2)}) %collective-permute-start.1) | collective-permute-done | bytes 98336 | tf_op jit(solution)/shard_map/ppermute | solution.py:675
  8.8 0.2 join_columns.1
  9.0 0.0 copy-start
  9.0 0.0 copy-start.1
  9.0 1.3 %collective-permute-start.2 = (f32[2,72,128]{2,1,0:T(8,128)S(1)}, f32[2,72,128]{2,1,0:T(8,128)S(1)}, u32[]{:S(2)}, u32[]{:S(2)}) collective-permute-start(f32[2,72,128]{2,1,0:T(8,128)S(1)} %get-tuple-element.36.east), channel_id=1, source_target_pairs={{0,1},{1,2},{2,3},{3,4},{4,5},{5,6},{6,7},{7,8},{8,9},{9,10},{10,1... | collective-permute-start | bytes 221192 | tf_op jit(solution)/shard_map/ppermute | solution.py:674
  10.3 3.8 %collective-permute-start.3 = (f32[2,72,128]{2,1,0:T(8,128)S(1)}, f32[2,72,128]{2,1,0:T(8,128)S(1)}, u32[]{:S(2)}, u32[]{:S(2)}) collective-permute-start(f32[2,72,128]{2,1,0:T(8,128)S(1)} %get-tuple-element.34.after.west), channel_id=1, source_target_pairs={{1,0},{2,1},{3,2},{4,3},{5,4},{6,5},{7,6},{8,7},{9,8},{10,9},{11,1... | collective-permute-start | bytes 221192 | tf_op jit(solution)/shard_map/ppermute | solution.py:675
  14.1 0.0 copy-done.2
  14.1 0.1 reshape.32
  14.2 0.1 copy.14
  14.3 0.3 plan.1
  14.6 0.3 surface.1.inner
  14.9 1.5 %collective-permute-done.2.from_west = f32[2,72,128]{2,1,0:T(8,128)S(1)} collective-permute-done((f32[2,72,128]{2,1,0:T(8,128)S(1)}, f32[2,72,128]{2,1,0:T(8,128)S(1)}, u32[]{:S(2)}, u32[]{:S(2)}) %collective-permute-start.2) | collective-permute-done | bytes 73760 | tf_op jit(solution)/shard_map/ppermute | solution.py:674
  16.4 0.0 collective-permute-done.3.from_east
  16.4 1.7 %wind.1 = f32[1024,128]{1,0:T(8,128)} custom-call(f32[64,256]{1,0:T(8,128)S(1)} %surface.1.inner, f32[64,256]{1,0:T(8,128)S(1)} %get-tuple-element.35.blocks, f32[2,72,128]{2,1,0:T(8,128)S(1)} %collective-permute-done.2.from_west, f32[2,72,128]{2,1,0:T(8,128)S(1)} %collective-permute-done.3.from_east, f32[2,72,128]{2,1,0:T(8,128)S(1)} %get-tuple-element.36.east, ...), custom_call_target="tpu_custom_call" | custom-call | flops 10000000 | bytes 2000000 | tf_op jit(solution)/shard_map/wind/pallas_call | solution.py:743
  18.1 9.3 %all-to-all-start = ((f32[128,1024,1]{1,2,0:T(1,128)}), f32[128,1024,1]{1,2,0:T(1,128)S(1)}, u32[]{:S(2)}, u32[]{:S(2)}) async-start(f32[128,1024,1]{1,2,0:T(1,128)} %bitcast.2), calls=%async_computation | async-start | bytes 1048576 | tf_op jit(solution)/shard_map/all_to_all | solution.py:680
  27.4 0.0 copy-done
  27.4 0.0 copy-done.1
  27.4 6.6 %step.1 = (f32[3,16,88,128]{3,2,1,0:T(8,128)}, f32[3,2,88,128]{3,2,1,0:T(8,128)S(1)}, f32[24,3200]{1,0:T(8,128)S(1)}, f32[24,3200]{1,0:T(8,128)S(1)}, f32[24,320...) custom-call(f32[3,16,64,128]{3,2,1,0:T(8,128)} %atmos.5, ...), custom_call_target="tpu_custom_call" | custom-call | flops 40000000 | bytes 8000000 | tf_op jit(solution)/shard_map/step/pallas_call | solution.py:755
  34.0 7.0 %all-to-all-done = f32[128,1024,1]{1,2,0:T(1,128)S(1)} async-done(((f32[128,1024,1]{1,2,0:T(1,128)}), f32[128,1024,1]{1,2,0:T(1,128)S(1)}, u32[]{:S(2)}, u32[]{:S(2)}) %all-to-all-start) | async-done | bytes 524320 | tf_op jit(solution)/shard_map/all_to_all | solution.py:680
  41.0 2.6 %fire.1 = (f32[768,128]{1,0:T(8,128)}, f32[24,3200]{1,0:T(8,128)}) custom-call(f32[1024,128]{1,0:T(8,128)S(1)} %bitcast.10, bf16[32,256]{1,0:T(8,128)(2,1)S(1)} %get-tuple-element.38.plan, bf16[256,128]{1,0:T(8,128)(2,1)S(1)} %get-tuple-element.39.sends, f32[32,128]{1,0:T(8,128)S(1)} %get-tuple-element.40.live, f32[24,3200]{1,0:T(8,128)S(1)} %get-tuple-element.41.rate, ...), custom_call_target="tpu_custom_call" | custom-call | flops 40000000 | bytes 4000000 | tf_op jit(solution)/shard_map/fire/pallas_call | solution.py:778
  43.6 4.6 %all-to-all-start.1 = ((f32[128,768,1]{1,2,0:T(1,128)}), f32[128,768,1]{1,2,0:T(1,128)S(1)}, u32[]{:S(2)}, u32[]{:S(2)}) async-start(f32[128,768,1]{1,2,0:T(1,128)} %bitcast.14), calls=%async_computation.1 | async-start | bytes 786432 | tf_op jit(solution)/shard_map/all_to_all | solution.py:680
  48.2 5.2 %upper.1 = (f32[3,16,64,128]{3,2,1,0:T(8,128)}, f32[3,2,88,128]{3,2,1,0:T(8,128)S(1)}, f32[3,3,88,128]{3,2,1,0:T(8,128)S(1)}) custom-call(f32[3,16,88,128]{3,2,1,0:T(8,128)} %get-tuple-element.51.main_in, f32[3,2,88,128]{3,2,1,0:T(8,128)S(1)} %get-tuple-element.47.rim.rim_in, f32[24,3200]{1,0:T(8,128)} %get-tuple-element.28.fire_level), custom_call_target="tpu_custom_call" | custom-call | flops 40000000 | bytes 8000000 | tf_op jit(solution)/shard_map/upper/pallas_call | solution.py:798
  53.5 7.1 %all-to-all-done.1 = f32[128,768,1]{1,2,0:T(1,128)S(1)} async-done(((f32[128,768,1]{1,2,0:T(1,128)}), f32[128,768,1]{1,2,0:T(1,128)S(1)}, u32[]{:S(2)}, u32[]{:S(2)}) %all-to-all-start.1) | async-done | bytes 393248 | tf_op jit(solution)/shard_map/all_to_all | solution.py:680
  60.5 1.8 %lower.1 = f32[3,16,64,128]{3,2,1,0:T(8,128)} custom-call(f32[768,128]{1,0:T(8,128)S(1)} %bitcast.11, bf16[64,256]{1,0:T(8,128)(2,1)S(1)} %get-tuple-element.49.home_plan, bf16[176,256]{1,0:T(8,128)(2,1)S(1)} %get-tuple-element.50.strip_plan, f32[3,3,88,128]{3,2,1,0:T(8,128)S(1)} %get-tuple-element.53.main_in, ...), custom_call_target="tpu_custom_call", output_to_operand_aliasing={{}: (6, {})} | custom-call | flops 10000000 | bytes 2000000 | tf_op jit(solution)/shard_map/lower/pallas_call | solution.py:810
  (2 shorter events, 0.0 us)
Async XLA Ops:
  0.6 13.5 %copy-start.2 = (s32[3072]{0:T(1024)S(1)}, s32[3072]{0:T(1024)}, u32[]{:S(2)}) copy-start(s32[3072]{0:T(1024)} %param.9) | copy-start | bytes 36868
  1.7 5.1 %collective-permute-start = (f32[24,8,128]{2,1,0:T(8,128)S(1)}, f32[24,8,128]{2,1,0:T(8,128)S(1)}, u32[]{:S(2)}, u32[]{:S(2)}) collective-permute-start(f32[24,8,128]{2,1,0:T(8,128)S(1)} %get-tuple-element.31), channel_id=1, source_target_pairs={{0,16},{16,32},{32,48},{48,64},{64,80},{80,96},{96,112},{112,0},{1... | collective-permute-start | bytes 294920 | tf_op jit(solution)/shard_map/ppermute | solution.py:674
  4.8 4.0 %collective-permute-start.1 = (f32[24,8,128]{2,1,0:T(8,128)S(1)}, f32[24,8,128]{2,1,0:T(8,128)S(1)}, u32[]{:S(2)}, u32[]{:S(2)}) collective-permute-start(f32[24,8,128]{2,1,0:T(8,128)S(1)} %get-tuple-element.29.after), channel_id=1, source_target_pairs={{16,0},{32,16},{48,32},{64,48},{80,64},{96,80},{112,96},{0,112},{1... | collective-permute-start | bytes 294920 | tf_op jit(solution)/shard_map/ppermute | solution.py:675
  9.0 18.4 %copy-start = (f32[13]{0:T(128)S(1)}, f32[13]{0:T(128)}, u32[]{:S(2)}) copy-start(f32[13]{0:T(128)} %param.13) | copy-start | bytes 160
  9.0 18.4 %copy-start.1 = (f32[13]{0:T(128)S(1)}, f32[13]{0:T(128)}, u32[]{:S(2)}) copy-start(f32[13]{0:T(128)} %param.14) | copy-start | bytes 160
  9.0 7.4 %collective-permute-start.2 = (f32[2,72,128]{2,1,0:T(8,128)S(1)}, f32[2,72,128]{2,1,0:T(8,128)S(1)}, u32[]{:S(2)}, u32[]{:S(2)}) collective-permute-start(f32[2,72,128]{2,1,0:T(8,128)S(1)} %get-tuple-element.36.east), channel_id=1, source_target_pairs={{0,1},{1,2},{2,3},{3,4},{4,5},{5,6},{6,7},{7,8},{8,9},{9,10},{10,1... | collective-permute-start | bytes 221192 | tf_op jit(solution)/shard_map/ppermute | solution.py:674
  10.3 6.1 %collective-permute-start.3 = (f32[2,72,128]{2,1,0:T(8,128)S(1)}, f32[2,72,128]{2,1,0:T(8,128)S(1)}, u32[]{:S(2)}, u32[]{:S(2)}) collective-permute-start(f32[2,72,128]{2,1,0:T(8,128)S(1)} %get-tuple-element.34.after.west), channel_id=1, source_target_pairs={{1,0},{2,1},{3,2},{4,3},{5,4},{6,5},{7,6},{8,7},{9,8},{10,9},{11,1... | collective-permute-start | bytes 221192 | tf_op jit(solution)/shard_map/ppermute | solution.py:675
  18.1 22.9 %all-to-all-start = ((f32[128,1024,1]{1,2,0:T(1,128)}), f32[128,1024,1]{1,2,0:T(1,128)S(1)}, u32[]{:S(2)}, u32[]{:S(2)}) async-start(f32[128,1024,1]{1,2,0:T(1,128)} %bitcast.2), calls=%async_computation | async-start | bytes 1048576 | tf_op jit(solution)/shard_map/all_to_all | solution.py:680
  43.6 17.0 %all-to-all-start.1 = ((f32[128,768,1]{1,2,0:T(1,128)}), f32[128,768,1]{1,2,0:T(1,128)S(1)}, u32[]{:S(2)}, u32[]{:S(2)}) async-start(f32[128,768,1]{1,2,0:T(1,128)} %bitcast.14), calls=%async_computation.1 | async-start | bytes 786432 | tf_op jit(solution)/shard_map/all_to_all | solution.py:680
